TPU v7x, 512 devices: a whole 4x4x16 slice. The times are simulated.
512 devices in a mesh: tm: 32 (over x, y, core), space: 16 (over z).
Axes of the slice: x: 4, y: 4, z: 16, core: 2. Of those that a mesh axis runs over, the one named last changes fastest.
Arguments:
- initial_state: float32 [64, 2048], P(None, 'space'), may hold values from -6 to 6
- forcing: float32 [128, 64, 2048], P('tm', None, 'space'), may hold values from -4 to 4
- coarse_gain: float32 [32, 64, 2048], P('tm', None, 'space'), may hold values from 0.05 to 1, as said below
- block_inverse: float32 [64, 64, 2048], P(None, None, 'space'), may hold values from -0.25 to 1.1
- face_blocks: float32 [6, 64, 64], replicated, may hold values from -0.1875 to 0.1875
- neighbor: int32 [6, 2048], P(None, 'space'), may hold values from -1 to 255, as said below
- send_rows: int32 [2, 1024], P(None, 'space'), may hold values from 0 to 127, as said below
Outputs:
- coarse_end: float32 [32, 64, 2048], P('tm', None, 'space')
- residual: float32 [32, 64, 2048], P('tm', None, 'space')
Inputs may be any that keep to these rules, and one draw needn't show every extreme that they name: `neighbor`: for face f (-x, +x, -y, +y, -z, +z) of the element in local column e, the local column of its neighbour in the extended field of its partition; -1 where the face lies on the domain's side along x or y. `send_rows`: row 0 lists the local columns of a partition's lowest element layer, row 1 those of its highest, in the same order of x and y. `coarse_gain`: Positive, below one.
All inputs are finite; a program needn't handle non-finite values.
Results may differ from a plain program's by a relative error of at most 0.00014.
Values sent between devices are 32-bit elements; how exact they have to be, the bound alone decides.
No kernel may reach another device: no remote copies, remote signals or barrier semaphores. Data moves between devices by JAX's collectives and lax.ppermute only.
A program may use at most 64 MiB of HBM per device.

v0:
```python
import jax
import jax.numpy as jnp
from jax import lax
from jax.sharding import PartitionSpec as P

STEPS = 4
SWEEPS = 2
ITERS = 2


HIGHEST_PRECISION = lax.Precision.HIGHEST


def extended_2(cells, sides, width):
    for axis, dim in sides:
        count = lax.axis_size(axis)
        ends = count - 1
        head = lax.slice_in_dim(cells, 0, width, axis=dim)
        tail = lax.slice_in_dim(cells, cells.shape[dim] - width, cells.shape[dim], axis=dim)
        cells = jnp.concatenate(
            [
                lax.ppermute(tail, axis, [(i, (i + 1) % count) for i in range(ends)]),
                cells,
                lax.ppermute(head, axis, [((i + 1) % count, i) for i in range(ends)]),
            ],
            axis=dim,
        )
    return cells


def shifted(x, axis, by):
    size = lax.axis_size(axis)
    pairs = [(i, i + by) for i in range(size) if 0 <= i + by < size]
    return lax.ppermute(x, axis, pairs)


def carried_in(part, axis, combine, identity):
    place = lax.axis_index(axis)
    gathered = jax.tree.map(lambda a: lax.all_gather(a, axis), part)
    state = jax.tree.map(lambda a, e: jnp.zeros_like(a) + jnp.asarray(e, a.dtype), part, identity)

    def one(lap, state):
        return combine(
            state, jax.tree.map(lambda a: lax.dynamic_index_in_dim(a, lap, 0, False), gathered)
        )

    return lax.fori_loop(0, place, one, state)


def apply_inverse(block_inverse, vector):
    return jnp.einsum("ije,je->ie", block_inverse, vector, precision=HIGHEST_PRECISION)


def extend(field_now, send_rows):
    values = field_now.shape[0]
    layer_size = send_rows.shape[1]
    bottom = jnp.take(field_now, send_rows[0], axis=1)
    upper_rows = jnp.take(field_now, send_rows[1], axis=1)
    stacked = jnp.stack([bottom.reshape(-1), upper_rows.reshape(-1)], axis=0)
    padded = extended_2(stacked, (("space", 0),), 1)
    below_rows = padded[0].reshape(values, layer_size)
    above_rows = padded[3].reshape(values, layer_size)
    return jnp.concatenate([field_now, below_rows, above_rows], axis=1)


def coupling(field_now, face_blocks, neighbor, send_rows):
    extended = extend(field_now, send_rows)
    face_valid = (neighbor >= 0).astype(jnp.float32)
    picked = jnp.take(extended, jnp.maximum(neighbor, 0), axis=1) * face_valid[None]
    return jnp.einsum("fij,jfe->ie", face_blocks, picked, precision=HIGHEST_PRECISION)


def fine_step(field_now, source, block_inverse, face_blocks, neighbor, send_rows):
    right_side = field_now + source
    iterate = apply_inverse(block_inverse, right_side)
    for sweep_index in range(SWEEPS):
        iterate = apply_inverse(
            block_inverse, right_side - coupling(iterate, face_blocks, neighbor, send_rows)
        )
    return iterate


def compose(earlier, later):
    return (earlier[0] * later[0], later[0] * earlier[1] + later[1])


def body(initial_state, forcing, coarse_gain, block_inverse, face_blocks, neighbor, send_rows):
    gain_now = coarse_gain[0]
    slot_index = lax.axis_index("tm")
    first_slice = (slot_index == 0).astype(jnp.float32)
    coarse = jnp.zeros_like(initial_state)
    residual = coarse
    for iteration in range(ITERS):
        previous = shifted(coarse, "tm", 1)
        field_now = previous + first_slice * initial_state
        for step_index in range(STEPS):
            field_now = fine_step(
                field_now, forcing[step_index], block_inverse, face_blocks, neighbor, send_rows
            )
        residual = field_now - coarse
        prefix = carried_in(
            (gain_now, residual), "tm", compose, (jnp.ones_like(gain_now), jnp.zeros_like(residual))
        )
        correction = gain_now * prefix[1] + residual
        coarse = coarse + correction
    return (coarse[None], residual[None])


def solution(mesh):
    return jax.shard_map(
        body,
        mesh=mesh,
        in_specs=(
            P(None, "space"),
            P("tm", None, "space"),
            P("tm", None, "space"),
            P(None, None, "space"),
            P(),
            P(None, "space"),
            P(None, "space"),
        ),
        out_specs=(P("tm", None, "space"), P("tm", None, "space")),
        check_vma=False,
    )
```

profile of v0, /device:TPU:63, one launch (start us, length us, event | category | flops | bytes accessed | tf_op | source)
XLA Modules:
  0.0 450.0 jit_solution(2671542772720091949)
XLA Ops:
  14.5 3.5 collective-permute-start.1
  28.6 4.8 %collective-permute-start.3 = (f32[1,4096]{1,0:T(1,128)S(1)}, f32[1,4096]{1,0:T(1,128)S(1)}, u32[]{:S(2)}, u32[]{:S(2)}) collective-permute-start(f32[1,4096]{1,0:T(1,128)S(1)} %stack_reshape.98), channel_id=1, source_target_pairs={{0,1},{1,2},{2,3},{3,4},{4,5},{5,6},{6,7},{7,8},{8,9},{9,10},{10,1... | collective-permute-start | bytes 49160 | tf_op jit(solution)/shard_map/ppermute | solution.py:22
  36.3 3.0 collective-permute-done.4
  44.5 3.4 collective-permute-start.5
  57.8 4.0 collective-permute-start.7
  64.8 3.0 collective-permute-done.8
  72.9 3.4 collective-permute-start.9
  86.8 3.4 collective-permute-start.11
  100.1 3.4 collective-permute-start.13
  113.0 3.4 collective-permute-start.15
  125.3 29.7 %all-gather.6.cloned.1.call-done = f32[32,64,128]{2,1,0:T(8,128)} async-done(((f32[1,64,128]{2,1,0:T(8,128)}), f32[32,64,128]{2,1,0:T(8,128)}) %all-gather.6.cloned.1.call-update) | async-done | bytes 1048592 | tf_op jit(solution)/shard_map/all_gather | solution.py:39
  155.0 61.3 %all-gather.8.cloned.1.call-done = f32[2048,128]{1,0:T(8,128)} async-done(((f32[64,128]{1,0:T(8,128)}), f32[2048,128]{1,0:T(8,128)}) %all-gather.8.cloned.1.call-update) | async-done | bytes 1048592 | tf_op jit(solution)/shard_map/all_gather | solution.py:39
  216.3 25.3 %while.24 = (s32[]{:T(128)}, f32[64,128]{1,0:T(8,128)S(1)}, s32[]{:T(128)}, f32[32,64,128]{2,1,0:T(8,128)}, f32[32,64,128]{2,1,0:T(8,128)}, /*index=5*/s32[]{:T(128)}, s32[]{:T(128)}, s32[]{:T(128)}) while((s32[]{:T(128)}, f32[64,128]{1,0:T(8,128)S(1)}, s32[]{:T(128)}, f32[32,64,128]{2,1,0:T(8,128)}, f32[32,64,128]{2,1,0:T(8,128)}, ...), condition=%wide.region_1.4_spmd, body=%wide.region_0.3_spmd.sunk | while | flops 16389 | bytes 131195 | solution.py:47
  247.4 3.2 collective-permute-start.18
  260.1 4.2 collective-permute-start.20
  267.3 3.0 collective-permute-done.21
  275.4 3.4 collective-permute-start.22
  288.3 3.2 collective-permute-start.24
  302.4 3.4 collective-permute-start.26
  316.2 3.4 collective-permute-start.28
  329.5 3.4 collective-permute-start.30
  342.4 3.1 collective-permute-start.32
  354.1 62.7 %all-gather.10.cloned.1.call-done = f32[2048,128]{1,0:T(8,128)} async-done(((f32[64,128]{1,0:T(8,128)}), f32[2048,128]{1,0:T(8,128)}) %all-gather.10.cloned.1.call-update) | async-done | bytes 1048592 | tf_op jit(solution)/shard_map/all_gather | solution.py:39
  416.8 25.3 %while.25 = (s32[]{:T(128)}, f32[64,128]{1,0:T(8,128)S(1)}, s32[]{:T(128)}, f32[32,64,128]{2,1,0:T(8,128)}, f32[32,64,128]{2,1,0:T(8,128)}, /*index=5*/s32[]{:T(128)}, s32[]{:T(128)}, s32[]{:T(128)}) while((s32[]{:T(128)}, f32[64,128]{1,0:T(8,128)S(1)}, s32[]{:T(128)}, f32[32,64,128]{2,1,0:T(8,128)}, f32[32,64,128]{2,1,0:T(8,128)}, ...), condition=%wide.region_3.6_spmd, body=%wide.region_2.5_spmd.sunk | while | flops 16389 | bytes 131195 | solution.py:47
  (474 shorter events, 214.0 us)
Async XLA Ops:
  7.2 147.8 %all-gather.6.cloned.1.call-start = ((), (), s32[]{:S(2)}) async-start(), calls=%async_computation | async-start | bytes 1081344 | tf_op jit(solution)/shard_map/all_gather | solution.py:39
  14.5 6.5 %collective-permute-start.1 = (f32[1,4096]{1,0:T(1,128)S(1)}, f32[1,4096]{1,0:T(1,128)S(1)}, u32[]{:S(2)}, u32[]{:S(2)}) collective-permute-start(f32[1,4096]{1,0:T(1,128)S(1)} %stack_reshape.96), channel_id=1, source_target_pairs={{0,1},{1,2},{2,3},{3,4},{4,5},{5,6},{6,7},{7,8},{8,9},{9,10},{10,1... | collective-permute-start | bytes 49160 | tf_op jit(solution)/shard_map/ppermute | solution.py:22
  28.6 6.9 %collective-permute-start.3 = (f32[1,4096]{1,0:T(1,128)S(1)}, f32[1,4096]{1,0:T(1,128)S(1)}, u32[]{:S(2)}, u32[]{:S(2)}) collective-permute-start(f32[1,4096]{1,0:T(1,128)S(1)} %stack_reshape.98), channel_id=1, source_target_pairs={{0,1},{1,2},{2,3},{3,4},{4,5},{5,6},{6,7},{7,8},{8,9},{9,10},{10,1... | collective-permute-start | bytes 49160 | tf_op jit(solution)/shard_map/ppermute | solution.py:22
  33.6 5.7 %collective-permute-start.4 = (f32[1,4096]{1,0:T(1,128)S(1)}, f32[1,4096]{1,0:T(1,128)S(1)}, u32[]{:S(2)}, u32[]{:S(2)}) collective-permute-start(f32[1,4096]{1,0:T(1,128)S(1)} %stack_reshape.99), channel_id=1, source_target_pairs={{1,0},{2,1},{3,2},{4,3},{5,4},{6,5},{7,6},{8,7},{9,8},{10,9},{11,1... | collective-permute-start | bytes 49160 | tf_op jit(solution)/shard_map/ppermute | solution.py:24
  44.5 5.6 %collective-permute-start.5 = (f32[1,4096]{1,0:T(1,128)S(1)}, f32[1,4096]{1,0:T(1,128)S(1)}, u32[]{:S(2)}, u32[]{:S(2)}) collective-permute-start(f32[1,4096]{1,0:T(1,128)S(1)} %stack_reshape.100), channel_id=1, source_target_pairs={{0,1},{1,2},{2,3},{3,4},{4,5},{5,6},{6,7},{7,8},{8,9},{9,10},{10,1... | collective-permute-start | bytes 49160 | tf_op jit(solution)/shard_map/ppermute | solution.py:22
  57.8 6.2 %collective-permute-start.7 = (f32[1,4096]{1,0:T(1,128)S(1)}, f32[1,4096]{1,0:T(1,128)S(1)}, u32[]{:S(2)}, u32[]{:S(2)}) collective-permute-start(f32[1,4096]{1,0:T(1,128)S(1)} %stack_reshape.102), channel_id=1, source_target_pairs={{0,1},{1,2},{2,3},{3,4},{4,5},{5,6},{6,7},{7,8},{8,9},{9,10},{10,1... | collective-permute-start | bytes 49160 | tf_op jit(solution)/shard_map/ppermute | solution.py:22
  62.1 5.7 %collective-permute-start.8 = (f32[1,4096]{1,0:T(1,128)S(1)}, f32[1,4096]{1,0:T(1,128)S(1)}, u32[]{:S(2)}, u32[]{:S(2)}) collective-permute-start(f32[1,4096]{1,0:T(1,128)S(1)} %stack_reshape.103), channel_id=1, source_target_pairs={{1,0},{2,1},{3,2},{4,3},{5,4},{6,5},{7,6},{8,7},{9,8},{10,9},{11,1... | collective-permute-start | bytes 49160 | tf_op jit(solution)/shard_map/ppermute | solution.py:24
  72.9 5.6 %collective-permute-start.9 = (f32[1,4096]{1,0:T(1,128)S(1)}, f32[1,4096]{1,0:T(1,128)S(1)}, u32[]{:S(2)}, u32[]{:S(2)}) collective-permute-start(f32[1,4096]{1,0:T(1,128)S(1)} %stack_reshape.104), channel_id=1, source_target_pairs={{0,1},{1,2},{2,3},{3,4},{4,5},{5,6},{6,7},{7,8},{8,9},{9,10},{10,1... | collective-permute-start | bytes 49160 | tf_op jit(solution)/shard_map/ppermute | solution.py:22
  76.6 5.4 %collective-permute-start.10 = (f32[1,4096]{1,0:T(1,128)S(1)}, f32[1,4096]{1,0:T(1,128)S(1)}, u32[]{:S(2)}, u32[]{:S(2)}) collective-permute-start(f32[1,4096]{1,0:T(1,128)S(1)} %stack_reshape.105), channel_id=1, source_target_pairs={{1,0},{2,1},{3,2},{4,3},{5,4},{6,5},{7,6},{8,7},{9,8},{10,9},{11,1... | collective-permute-start | bytes 49160 | tf_op jit(solution)/shard_map/ppermute | solution.py:24
  86.8 5.6 %collective-permute-start.11 = (f32[1,4096]{1,0:T(1,128)S(1)}, f32[1,4096]{1,0:T(1,128)S(1)}, u32[]{:S(2)}, u32[]{:S(2)}) collective-permute-start(f32[1,4096]{1,0:T(1,128)S(1)} %stack_reshape.106), channel_id=1, source_target_pairs={{0,1},{1,2},{2,3},{3,4},{4,5},{5,6},{6,7},{7,8},{8,9},{9,10},{10,1... | collective-permute-start | bytes 49160 | tf_op jit(solution)/shard_map/ppermute | solution.py:22
  92.3 123.9 %all-gather.8.cloned.1.call-start = ((), (), s32[]{:S(2)}) async-start(), calls=%async_computation.1 | async-start | bytes 1081344 | tf_op jit(solution)/shard_map/all_gather | solution.py:39
  100.1 5.7 %collective-permute-start.13 = (f32[1,4096]{1,0:T(1,128)S(1)}, f32[1,4096]{1,0:T(1,128)S(1)}, u32[]{:S(2)}, u32[]{:S(2)}) collective-permute-start(f32[1,4096]{1,0:T(1,128)S(1)} %stack_reshape.108), channel_id=1, source_target_pairs={{0,1},{1,2},{2,3},{3,4},{4,5},{5,6},{6,7},{7,8},{8,9},{9,10},{10,1... | collective-permute-start | bytes 49160 | tf_op jit(solution)/shard_map/ppermute | solution.py:22
  113.0 5.6 %collective-permute-start.15 = (f32[1,4096]{1,0:T(1,128)S(1)}, f32[1,4096]{1,0:T(1,128)S(1)}, u32[]{:S(2)}, u32[]{:S(2)}) collective-permute-start(f32[1,4096]{1,0:T(1,128)S(1)} %stack_reshape.110), channel_id=1, source_target_pairs={{0,1},{1,2},{2,3},{3,4},{4,5},{5,6},{6,7},{7,8},{8,9},{9,10},{10,1... | collective-permute-start | bytes 49160 | tf_op jit(solution)/shard_map/ppermute | solution.py:22
  125.3 291.5 %all-gather.10.cloned.1.call-start = ((), (), s32[]{:S(2)}) async-start(), calls=%async_computation.2 | async-start | bytes 1081344 | tf_op jit(solution)/shard_map/all_gather | solution.py:39
  247.4 5.6 %collective-permute-start.18 = (f32[1,4096]{1,0:T(1,128)S(1)}, f32[1,4096]{1,0:T(1,128)S(1)}, u32[]{:S(2)}, u32[]{:S(2)}) collective-permute-start(f32[1,4096]{1,0:T(1,128)S(1)} %stack_reshape.112), channel_id=1, source_target_pairs={{0,1},{1,2},{2,3},{3,4},{4,5},{5,6},{6,7},{7,8},{8,9},{9,10},{10,1... | collective-permute-start | bytes 49160 | tf_op jit(solution)/shard_map/ppermute | solution.py:22
  260.1 6.4 %collective-permute-start.20 = (f32[1,4096]{1,0:T(1,128)S(1)}, f32[1,4096]{1,0:T(1,128)S(1)}, u32[]{:S(2)}, u32[]{:S(2)}) collective-permute-start(f32[1,4096]{1,0:T(1,128)S(1)} %stack_reshape.114), channel_id=1, source_target_pairs={{0,1},{1,2},{2,3},{3,4},{4,5},{5,6},{6,7},{7,8},{8,9},{9,10},{10,1... | collective-permute-start | bytes 49160 | tf_op jit(solution)/shard_map/ppermute | solution.py:22
  264.6 5.7 %collective-permute-start.21 = (f32[1,4096]{1,0:T(1,128)S(1)}, f32[1,4096]{1,0:T(1,128)S(1)}, u32[]{:S(2)}, u32[]{:S(2)}) collective-permute-start(f32[1,4096]{1,0:T(1,128)S(1)} %stack_reshape.115), channel_id=1, source_target_pairs={{1,0},{2,1},{3,2},{4,3},{5,4},{6,5},{7,6},{8,7},{9,8},{10,9},{11,1... | collective-permute-start | bytes 49160 | tf_op jit(solution)/shard_map/ppermute | solution.py:24
  275.4 5.6 %collective-permute-start.22 = (f32[1,4096]{1,0:T(1,128)S(1)}, f32[1,4096]{1,0:T(1,128)S(1)}, u32[]{:S(2)}, u32[]{:S(2)}) collective-permute-start(f32[1,4096]{1,0:T(1,128)S(1)} %stack_reshape.116), channel_id=1, source_target_pairs={{0,1},{1,2},{2,3},{3,4},{4,5},{5,6},{6,7},{7,8},{8,9},{9,10},{10,1... | collective-permute-start | bytes 49160 | tf_op jit(solution)/shard_map/ppermute | solution.py:22
  288.3 5.6 %collective-permute-start.24 = (f32[1,4096]{1,0:T(1,128)S(1)}, f32[1,4096]{1,0:T(1,128)S(1)}, u32[]{:S(2)}, u32[]{:S(2)}) collective-permute-start(f32[1,4096]{1,0:T(1,128)S(1)} %stack_reshape.118), channel_id=1, source_target_pairs={{0,1},{1,2},{2,3},{3,4},{4,5},{5,6},{6,7},{7,8},{8,9},{9,10},{10,1... | collective-permute-start | bytes 49160 | tf_op jit(solution)/shard_map/ppermute | solution.py:22
  302.4 5.8 %collective-permute-start.26 = (f32[1,4096]{1,0:T(1,128)S(1)}, f32[1,4096]{1,0:T(1,128)S(1)}, u32[]{:S(2)}, u32[]{:S(2)}) collective-permute-start(f32[1,4096]{1,0:T(1,128)S(1)} %stack_reshape.120), channel_id=1, source_target_pairs={{0,1},{1,2},{2,3},{3,4},{4,5},{5,6},{6,7},{7,8},{8,9},{9,10},{10,1... | collective-permute-start | bytes 49160 | tf_op jit(solution)/shard_map/ppermute | solution.py:22
  306.0 5.4 %collective-permute-start.27 = (f32[1,4096]{1,0:T(1,128)S(1)}, f32[1,4096]{1,0:T(1,128)S(1)}, u32[]{:S(2)}, u32[]{:S(2)}) collective-permute-start(f32[1,4096]{1,0:T(1,128)S(1)} %stack_reshape.121), channel_id=1, source_target_pairs={{1,0},{2,1},{3,2},{4,3},{5,4},{6,5},{7,6},{8,7},{9,8},{10,9},{11,1... | collective-permute-start | bytes 49160 | tf_op jit(solution)/shard_map/ppermute | solution.py:24
  316.2 5.6 %collective-permute-start.28 = (f32[1,4096]{1,0:T(1,128)S(1)}, f32[1,4096]{1,0:T(1,128)S(1)}, u32[]{:S(2)}, u32[]{:S(2)}) collective-permute-start(f32[1,4096]{1,0:T(1,128)S(1)} %stack_reshape.122), channel_id=1, source_target_pairs={{0,1},{1,2},{2,3},{3,4},{4,5},{5,6},{6,7},{7,8},{8,9},{9,10},{10,1... | collective-permute-start | bytes 49160 | tf_op jit(solution)/shard_map/ppermute | solution.py:22
  329.5 5.6 %collective-permute-start.30 = (f32[1,4096]{1,0:T(1,128)S(1)}, f32[1,4096]{1,0:T(1,128)S(1)}, u32[]{:S(2)}, u32[]{:S(2)}) collective-permute-start(f32[1,4096]{1,0:T(1,128)S(1)} %stack_reshape.124), channel_id=1, source_target_pairs={{0,1},{1,2},{2,3},{3,4},{4,5},{5,6},{6,7},{7,8},{8,9},{9,10},{10,1... | collective-permute-start | bytes 49160 | tf_op jit(solution)/shard_map/ppermute | solution.py:22
  342.4 5.5 %collective-permute-start.32 = (f32[1,4096]{1,0:T(1,128)S(1)}, f32[1,4096]{1,0:T(1,128)S(1)}, u32[]{:S(2)}, u32[]{:S(2)}) collective-permute-start(f32[1,4096]{1,0:T(1,128)S(1)} %stack_reshape.126), channel_id=1, source_target_pairs={{0,1},{1,2},{2,3},{3,4},{4,5},{5,6},{6,7},{7,8},{8,9},{9,10},{10,1... | collective-permute-start | bytes 49160 | tf_op jit(solution)/shard_map/ppermute | solution.py:22
  (18 other events, 325.4 us)
Sparse Core Ops, SparseCore 0:
  92.5 62.5 all-gather.5
  158.7 57.5 all-gather.7
  354.2 62.5 all-gather.9
where the time goes:
time: 456 us; the launch traced here: 450 us
  waiting for transfers between devices  189 us (41%)
  starting transfers between devices  90.9 us (20%)
  other arithmetic  88.3 us (19%)
  local copies, waits for them, and re-layouts  59.1 us (13%)
  between operations  15.6 us (3%)
  matrix products  5.43 us (1%)
    all_gather x3, waiting for transfers between devices, carried_in(): gathered = jax.tree.map(lambda a: lax.all_gather(a, axis), part)  154 us
    ppermute x16, starting transfers between devices, extended_2(): lax.ppermute(tail, axis, [(i, (i + 1) % count) for i in range(ends)])  56.3 us
    add x62, other arithmetic, compose(): return (earlier[0] * later[0], later[0] * earlier[1] + later[1])  49.1 us
    ppermute x16, waiting for transfers between devices, extended_2(): lax.ppermute(head, axis, [((i + 1) % count, i) for i in range(ends)])  33.6 us
    ppermute x16, starting transfers between devices, extended_2(): lax.ppermute(head, axis, [((i + 1) % count, i) for i in range(ends)])  31.8 us
    gather x32, local copies, waits for them, and re-layouts, coupling(): jnp.take(extended, jnp.maximum(neighbor, 0), axis=1) * face_valid[None]  27.5 us
    ppermute x16, other arithmetic, extended_2(): lax.ppermute(tail, axis, [(i, (i + 1) % count) for i in range(ends)])  10.3 us
    ppermute x16, other arithmetic, extended_2(): lax.ppermute(head, axis, [((i + 1) % count, i) for i in range(ends)])  10.3 us
  transfers between devices with their start and end apart: 37, of which 20 were waited for; matrix products, arithmetic and copies ran while one was open for 7% of the time, Pallas kernels for 0%

commit v1 on v0

v1 whole, which is shorter than its diff:
```python
import functools

import jax
import jax.numpy as jnp
from jax import lax
from jax.experimental import pallas as pl
from jax.experimental.pallas import tpu as pltpu
from jax.sharding import Mesh, PartitionSpec as P


VALUES = 64
LANES = 128
HALF = 64
STEPS = 4
STAGES = 2 * STEPS
HIGHEST = lax.Precision.HIGHEST
F32 = jnp.float32
FIELD = (VALUES, LANES)


def vmem(x):
    return pltpu.with_memory_space_constraint(x, pltpu.VMEM)


def call(kernel, name, outs, *args, keep=True, flops=1 << 22):
    whole = pl.BlockSpec(memory_space=pltpu.VMEM)
    shapes = tuple(
        pltpu.VMEM(shape, dtype) if keep else jax.ShapeDtypeStruct(shape, dtype)
        for shape, dtype in outs
    )
    return pl.pallas_call(
        kernel,
        out_shape=shapes,
        in_specs=[whole] * len(args),
        out_specs=(whole,) * len(shapes),
        scratch_shapes=[pltpu.VMEM(FIELD, F32)],
        cost_estimate=pl.CostEstimate(flops=flops, bytes_accessed=1 << 20, transcendentals=0),
        compiler_params=pltpu.CompilerParams(vmem_limit_bytes=16 << 20),
        name=name,
    )(*args)


def low_half():
    return lax.broadcasted_iota(jnp.int32, FIELD, 1) < HALF


def swap_halves(x):
    return pltpu.roll(x, HALF, 1)


def columns(x, index):
    return jnp.take_along_axis(x, jnp.broadcast_to(index, x.shape), axis=1)


def twice(row):
    return jnp.concatenate([row, row], axis=1)


def layer_rows(send_ref, core):
    lowest, highest = send_ref[0:1, :], send_ref[1:2, :]
    mine = jnp.where(core == 0, lowest, highest)
    other = jnp.where(core == 0, highest, lowest)
    return twice(mine), twice(other)


def apply_inverse(inverse_ref, scratch, vector):
    scratch[...] = vector
    sums = [None, None]
    for j in range(VALUES):
        term = inverse_ref[j] * scratch[j : j + 1, :]
        sums[j % 2] = term if sums[j % 2] is None else sums[j % 2] + term
    return sums[0] + sums[1]


def coupling(field, far, near, index, valid, faces):
    picked = [
        columns(field, index[f : f + 1, :]) * jnp.broadcast_to(valid[f : f + 1, :], FIELD)
        for f in range(4)
    ]
    stacked = jnp.concatenate(picked + [far, near], axis=0)
    return jnp.dot(faces, stacked, precision=HIGHEST, preferred_element_type=F32)


def share_kernel(send_ref, forcing_ref, gain_ref, state_ref, own_ref, out_ref, start_ref, _):
    core = lax.axis_index("c")
    mine, other = layer_rows(send_ref, core)
    low = low_half()
    fields = [forcing_ref[m] for m in range(STEPS)] + [gain_ref[0]]
    for m, field in enumerate(fields):
        own_ref[m] = columns(field, mine)
    for m in range(0, STEPS, 2):
        out_ref[m // 2] = jnp.where(low, columns(fields[m], other), columns(fields[m + 1], other))
    out_ref[STEPS // 2] = columns(fields[STEPS], other)
    start_ref[...] = columns(state_ref[...], mine)


def tables_kernel(
    send_ref, neighbor_ref, inverse_ref, blocks_ref, index_ref, valid_ref, place_ref, faces_ref,
    table_ref, _
):
    core = lax.axis_index("c")
    mine, _other = layer_rows(send_ref, core)
    order = jnp.concatenate([send_ref[0:1, :], send_ref[1:2, :]], axis=1)
    down = jnp.transpose(jnp.broadcast_to(order.astype(F32), (LANES, LANES)))
    across = lax.broadcasted_iota(jnp.int32, (LANES, LANES), 1).astype(F32)
    at = lax.broadcasted_iota(jnp.int32, (LANES, LANES), 0).astype(F32)
    place = jnp.sum(jnp.where(down == across, at, 0.0), axis=0, keepdims=True).astype(jnp.int32)
    place = jnp.broadcast_to(place, (8, LANES))
    place_ref[...] = place
    pad = jnp.zeros((2, LANES), jnp.int32)
    local = columns(jnp.concatenate([neighbor_ref[...], pad], axis=0), mine)
    valid_ref[...] = (local >= 0).astype(F32)
    lane = lax.broadcasted_iota(jnp.int32, (8, LANES), 1)
    spot = columns(place, jnp.clip(local, 0, LANES - 1))
    index_ref[...] = jnp.bitwise_and(spot, HALF - 1) + jnp.where(lane < HALF, 0, HALF)
    for f in range(4):
        faces_ref[:, f * VALUES : (f + 1) * VALUES] = blocks_ref[f]
    faces_ref[:, 4 * VALUES : 5 * VALUES] = jnp.where(core == 0, blocks_ref[4], blocks_ref[5])
    faces_ref[:, 5 * VALUES : 6 * VALUES] = jnp.where(core == 0, blocks_ref[5], blocks_ref[4])
    for j in range(VALUES):
        table_ref[j] = columns(inverse_ref[pl.ds(j, VALUES, stride=VALUES), :], mine)


def first_kernel(
    own_ref, got_ref, start_ref, table_ref, sources_ref, gain_ref, pair_ref, right_ref, scratch
):
    core = lax.axis_index("c")
    low = low_half()
    is_own = low == (core == 0)
    for m in range(STEPS + 1):
        got = got_ref[m // 2]
        turned = swap_halves(got)
        if m % 2 == 0:
            other = jnp.where(core == 0, turned, got)
        else:
            other = jnp.where(core == 0, got, turned)
        value = jnp.where(is_own, own_ref[m], other)
        if m < STEPS:
            sources_ref[m] = value
        else:
            gain_ref[...] = value
    first = jnp.logical_and(low, lax.axis_index("q") == 0)
    right = jnp.where(first, start_ref[...], 0.0) + sources_ref[0]
    right_ref[...] = right
    pair_ref[0] = jnp.zeros(FIELD, F32)
    pair_ref[1] = apply_inverse(table_ref, scratch, right)


def advance(plan, refs, sourced, scratch):
    (pair_ref, right_ref, far_ref, near_ref, index_ref, valid_ref, faces_ref, table_ref, sources_ref,
     pair_out, right_out) = refs
    active, stages = plan
    core = lax.axis_index("c")

    @pl.when(core == active)
    def _run():
        index, valid, faces = index_ref[...], valid_ref[...], faces_ref[...]
        field = pair_ref[1]
        right = right_ref[...]
        for stage, slot in stages:
            pair_out[0] = field
            summed = coupling(field, far_ref[slot], near_ref[slot], index, valid, faces)
            field = apply_inverse(table_ref, scratch, right - summed)
            if stage % 2 == 1 and stage < STAGES - 1:
                right = field
                if sourced:
                    right = right + sources_ref[(stage + 1) // 2]
                field = apply_inverse(table_ref, scratch, right)
        pair_out[1] = field
        right_out[...] = right

    @pl.when(core != active)
    def _keep():
        pair_out[...] = pair_ref[...]
        right_out[...] = right_ref[...]


def advance_kernel(plan, sourced, *refs):
    advance(plan, refs[:-1], sourced, refs[-1])


def ends_kernel(plan, count, *refs):
    (*inner, gain_ref, pair_out, right_out, chunk_ref, scratch) = refs
    advance(plan, (*inner, pair_out, right_out), True, scratch)
    low = low_half()
    gain, end = gain_ref[...], pair_out[1]
    summed = gain * swap_halves(end) + end
    chunk = jnp.where(low, gain * swap_halves(gain), summed)
    for q in range(count):
        chunk_ref[q] = chunk


def ends_last_kernel(plan, count, *refs):
    (*inner, gain_ref, shift_ref, pair_out, right_out, residual_ref, chunk_ref, scratch) = refs
    advance(plan, (*inner, pair_out, right_out), False, scratch)
    gain = gain_ref[...]
    residual = pair_out[1] - gain * shift_ref[...]
    residual_ref[...] = residual
    summed = gain * swap_halves(residual) + residual
    low = low_half()[:HALF // 2]
    chunk = jnp.where(low, swap_halves(summed)[: VALUES // 2], summed[VALUES // 2 :])
    for q in range(count):
        chunk_ref[q] = chunk


def chained(count, before, gain, residual):
    before = jnp.where(low_half(), swap_halves(before), before)
    return jnp.where(low_half(), before, swap_halves(gain * before + residual))


def restart_kernel(count, all_ref, end_ref, gain_ref, table_ref, shift_ref, coarse_ref, pair_ref, scratch):
    mine = lax.axis_index("q")
    before = jnp.zeros(FIELD, F32)
    for q in range(count):
        chunk = all_ref[q]
        before = jnp.where(q < mine, swap_halves(chunk) * before + chunk, before)
    gain, end = gain_ref[...], end_ref[1]
    shift = chained(count, before, gain, end)
    shift_ref[...] = shift
    coarse_ref[...] = gain * shift + end
    pair_ref[0] = jnp.zeros(FIELD, F32)
    pair_ref[1] = apply_inverse(table_ref, scratch, shift)


def finish_kernel(count, all_ref, gains_ref, residual_ref, gain_ref, coarse_ref, end_ref, out_ref, _):
    core = lax.axis_index("c")
    mine = lax.axis_index("q")
    low = low_half()
    before = jnp.zeros(FIELD, F32)
    for q in range(count):
        chunk = all_ref[q]
        summed = jnp.concatenate([swap_halves(chunk), chunk], axis=0)
        before = jnp.where(q < mine, swap_halves(gains_ref[q]) * before + summed, before)
    gain, residual = gain_ref[...], residual_ref[...]
    shift = chained(count, before, gain, residual)
    end = coarse_ref[...] + (gain * shift + residual)
    end_ref[...] = end
    out_ref[...] = jnp.where(
        core == 0,
        jnp.where(low, swap_halves(end), residual),
        jnp.where(low, end, swap_halves(residual)),
    )


def output_kernel(end_ref, residual_ref, got_ref, place_ref, end_out, residual_out, _):
    core = lax.axis_index("c")
    low = low_half()
    got = got_ref[...]
    turned = swap_halves(got)
    end, residual = end_ref[...], residual_ref[...]
    end = jnp.where(core == 0, jnp.where(low, end, turned), jnp.where(low, got, end))
    residual = jnp.where(
        core == 0, jnp.where(low, residual, got), jnp.where(low, turned, residual)
    )
    place = place_ref[0:1, :]
    end_out[0] = columns(end, place)
    residual_out[0] = columns(residual, place)


def plans():
    yield 1, [(0, 1)]
    for half in range(2, STAGES + 1):
        yield half % 2, [(half - 2, 0), (half - 1, 1)]
    yield (STAGES + 1) % 2, [(STAGES - 1, 0)]


def body(count, depth, initial_state, forcing, coarse_gain, block_inverse, face_blocks, neighbor, send_rows):
    def swap_cores(x):
        return lax.ppermute(x, "c", [(0, 1), (1, 0)])

    def halo(x, to):
        if to == 1:
            across = [(z + 1, depth + z) for z in range(depth - 1)]
        else:
            across = [(depth + z, z + 1) for z in range(depth - 1)]
        far = lax.ppermute(x, ("c", "space"), across)
        near = lax.ppermute(x, "c", [(1 - to, to)])
        return vmem(far), vmem(near)

    field, pair_shape = (FIELD, F32), ((2,) + FIELD, F32)
    own, sent, start = call(
        share_kernel, "share",
        [((STEPS + 1,) + FIELD, F32), ((STEPS // 2 + 1,) + FIELD, F32), field],
        send_rows, forcing, coarse_gain, initial_state,
    )
    got = swap_cores(sent)
    index, valid, place, faces, table = call(
        tables_kernel, "tables",
        [((8, LANES), jnp.int32), ((8, LANES), F32), ((8, LANES), jnp.int32),
         ((VALUES, 6 * VALUES), F32), ((VALUES,) + FIELD, F32)],
        send_rows, neighbor, vmem(block_inverse.reshape(VALUES * VALUES, LANES)), face_blocks,
    )
    index, valid, place, faces, table = map(vmem, (index, valid, place, faces, table))
    sources, gain, pair, right = call(
        first_kernel, "first", [((STEPS,) + FIELD, F32), field, pair_shape, field],
        vmem(own), vmem(got), vmem(start), table,
    )
    sources, gain = vmem(sources), vmem(gain)
    half_phases = list(plans())

    def inner(pair, right, to):
        pair, right = vmem(pair), vmem(right)
        far, near = halo(pair, to)
        return pair, right, far, near, index, valid, faces, table, sources

    for plan in half_phases[:-1]:
        pair, right = call(
            functools.partial(advance_kernel, plan, True), "advance", [pair_shape, field],
            *inner(pair, right, plan[0]),
        )
    plan = half_phases[-1]
    pair, _, chunk = call(
        functools.partial(ends_kernel, plan, count), "ends",
        [pair_shape, field, ((count,) + FIELD, F32)], *inner(pair, right, plan[0]), gain,
    )
    gathered = vmem(lax.all_to_all(chunk, "q", 0, 0))
    shift, coarse, pair = call(
        functools.partial(restart_kernel, count), "restart", [field, field, pair_shape],
        gathered, vmem(pair), gain, table,
    )
    right = shift = vmem(shift)
    for plan in half_phases[:-1]:
        pair, right = call(
            functools.partial(advance_kernel, plan, False), "advance", [pair_shape, field],
            *inner(pair, right, plan[0]),
        )
    plan = half_phases[-1]
    _, _, residual, chunk = call(
        functools.partial(ends_last_kernel, plan, count), "ends",
        [pair_shape, field, field, ((count, VALUES // 2, LANES), F32)],
        *inner(pair, right, plan[0]), gain, shift,
    )
    sums = vmem(lax.all_to_all(chunk, "q", 0, 0))
    residual = vmem(residual)
    end, sent = call(
        functools.partial(finish_kernel, count), "finish", [field, field],
        sums, gathered, residual, gain, vmem(coarse),
    )
    got = vmem(swap_cores(sent))
    return call(
        output_kernel, "output", [((1,) + FIELD, F32)] * 2, vmem(end), residual, got, place,
        keep=False,
    )


def solution(mesh):
    slices, depth = mesh.devices.shape
    count = slices // 2
    pairs = Mesh(mesh.devices.reshape(count, 2, depth), ("q", "c", "space"))
    tm = ("q", "c")
    return jax.shard_map(
        functools.partial(body, count, depth),
        mesh=pairs,
        in_specs=(
            P(None, "space"),
            P(tm, None, "space"),
            P(tm, None, "space"),
            P(None, None, "space"),
            P(),
            P(None, "space"),
            P(None, "space"),
        ),
        out_specs=(P(tm, None, "space"), P(tm, None, "space")),
        check_vma=False,
    )
```

time: 456 us -> 178 us (0.39)
  the two profiles are of different devices: /device:TPU:63 before, /device:TPU:97 now
where the time goes in v1:
time: 178 us; the launch traced here: 177 us
  waiting for transfers between devices  77.3 us (43%)
  starting transfers between devices  50.9 us (29%)
  blocking collectives  25.8 us (14%)
  Pallas kernels  15.2 us (9%)
  local copies, waits for them, and re-layouts  6.29 us (4%)
    ppermute x18, waiting for transfers between devices, halo(): far = lax.ppermute(x, ('c', 'space'), across)  70.4 us
    ppermute x18, starting transfers between devices, halo(): far = lax.ppermute(x, ('c', 'space'), across)  23.3 us
    ppermute x18, starting transfers between devices, halo(): near = lax.ppermute(x, 'c', [(1 - to, to)])  23.2 us
    all_to_all x1, blocking collectives, body(): gathered = vmem(lax.all_to_all(chunk, 'q', 0, 0))  15.5 us
    pallas_call x24, Pallas kernels, call(): pl.pallas_call(kernel, out_shape=shapes, in_specs=[whole] * len(args), ou...  15.2 us
    all_to_all x1, blocking collectives, body(): sums = vmem(lax.all_to_all(chunk, 'q', 0, 0))  10.3 us
    unnamed x14, local copies, waits for them, and re-layouts  6.29 us
    ppermute x18, waiting for transfers between devices, halo(): near = lax.ppermute(x, 'c', [(1 - to, to)])  5.64 us
  transfers between devices with their start and end apart: 38, of which 29 were waited for; matrix products, arithmetic and copies ran while one was open for 0% of the time, Pallas kernels for 1%

profile of v1, /device:TPU:97, one launch (start us, length us, event | category | flops | bytes accessed | tf_op | source)
XLA Modules:
  0.0 176.6 jit_solution(13067578609257377337)
XLA Ops:
  4.0 2.6 %collective-permute-start = (f32[3,64,128]{2,1,0:T(8,128)S(1)}, f32[3,64,128]{2,1,0:T(8,128)S(1)}, u32[]{:S(2)}, u32[]{:S(2)}) collective-permute-start(f32[3,64,128]{2,1,0:T(8,128)S(1)} %get-tuple-element.56), channel_id=1, source_target_pairs={{0,16},{16,0},{1,17},{17,1},{2,18},{18,2},{3,19},{19,3},{4,20},{20... | collective-permute-start | bytes 294920 | tf_op jit(solution)/shard_map/ppermute | solution.py:269
  6.6 1.6 copy-done
  14.5 5.2 %collective-permute-done.1.refs_2_ = f32[2,64,128]{2,1,0:T(8,128)S(1)} collective-permute-done((f32[2,64,128]{2,1,0:T(8,128)S(1)}, f32[2,64,128]{2,1,0:T(8,128)S(1)}, u32[]{:S(2)}, u32[]{:S(2)}) %collective-permute-start.1) | collective-permute-done | bytes 65568 | tf_op jit(solution)/shard_map/ppermute | solution.py:276
  22.9 1.3 collective-permute-done.3.refs_2_
  27.3 6.3 %collective-permute-done.5.refs_2_ = f32[2,64,128]{2,1,0:T(8,128)S(1)} collective-permute-done((f32[2,64,128]{2,1,0:T(8,128)S(1)}, f32[2,64,128]{2,1,0:T(8,128)S(1)}, u32[]{:S(2)}, u32[]{:S(2)}) %collective-permute-start.5) | collective-permute-done | bytes 65568 | tf_op jit(solution)/shard_map/ppermute | solution.py:276
  33.6 1.4 advance.18
  37.6 1.3 collective-permute-done.7.refs_2_
  42.1 6.3 %collective-permute-done.9.refs_2_ = f32[2,64,128]{2,1,0:T(8,128)S(1)} collective-permute-done((f32[2,64,128]{2,1,0:T(8,128)S(1)}, f32[2,64,128]{2,1,0:T(8,128)S(1)}, u32[]{:S(2)}, u32[]{:S(2)}) %collective-permute-start.9) | collective-permute-done | bytes 65568 | tf_op jit(solution)/shard_map/ppermute | solution.py:276
  48.4 1.4 advance.20
  56.8 6.3 %collective-permute-done.13.refs_2_ = f32[2,64,128]{2,1,0:T(8,128)S(1)} collective-permute-done((f32[2,64,128]{2,1,0:T(8,128)S(1)}, f32[2,64,128]{2,1,0:T(8,128)S(1)}, u32[]{:S(2)}, u32[]{:S(2)}) %collective-permute-start.13) | collective-permute-done | bytes 65568 | tf_op jit(solution)/shard_map/ppermute | solution.py:276
  63.1 1.4 advance.22
  71.5 6.1 %collective-permute-done.17.refs_2_ = f32[2,64,128]{2,1,0:T(8,128)S(1)} collective-permute-done((f32[2,64,128]{2,1,0:T(8,128)S(1)}, f32[2,64,128]{2,1,0:T(8,128)S(1)}, u32[]{:S(2)}, u32[]{:S(2)}) %collective-permute-start.17) | collective-permute-done | bytes 65568 | tf_op jit(solution)/shard_map/ppermute | solution.py:276
  78.8 15.5 %all_to_all.10.all_ref.gains_ref = f32[16,64,128]{2,1,0:T(8,128)S(1)} all-to-all(f32[16,64,128]{2,1,0:T(8,128)S(1)} %get-tuple-element.82), channel_id=1, replica_groups=mesh['q'=16,'c'=2,'space'=16] {'q'}, dimensions={0} | all-to-all | bytes 1048576 | tf_op jit(solution)/shard_map/all_to_all | solution.py:316
  97.9 4.9 %collective-permute-done.19.refs_2_ = f32[2,64,128]{2,1,0:T(8,128)S(1)} collective-permute-done((f32[2,64,128]{2,1,0:T(8,128)S(1)}, f32[2,64,128]{2,1,0:T(8,128)S(1)}, u32[]{:S(2)}, u32[]{:S(2)}) %collective-permute-start.19) | collective-permute-done | bytes 65568 | tf_op jit(solution)/shard_map/ppermute | solution.py:276
  110.6 6.2 %collective-permute-done.23.refs_2_ = f32[2,64,128]{2,1,0:T(8,128)S(1)} collective-permute-done((f32[2,64,128]{2,1,0:T(8,128)S(1)}, f32[2,64,128]{2,1,0:T(8,128)S(1)}, u32[]{:S(2)}, u32[]{:S(2)}) %collective-permute-start.23) | collective-permute-done | bytes 65568 | tf_op jit(solution)/shard_map/ppermute | solution.py:276
  116.8 1.4 advance.26
  120.7 1.3 collective-permute-done.25.refs_2_
  125.2 6.3 %collective-permute-done.27.refs_2_ = f32[2,64,128]{2,1,0:T(8,128)S(1)} collective-permute-done((f32[2,64,128]{2,1,0:T(8,128)S(1)}, f32[2,64,128]{2,1,0:T(8,128)S(1)}, u32[]{:S(2)}, u32[]{:S(2)}) %collective-permute-start.27) | collective-permute-done | bytes 65568 | tf_op jit(solution)/shard_map/ppermute | solution.py:276
  131.5 1.4 advance.28
  139.9 6.3 %collective-permute-done.31.refs_2_ = f32[2,64,128]{2,1,0:T(8,128)S(1)} collective-permute-done((f32[2,64,128]{2,1,0:T(8,128)S(1)}, f32[2,64,128]{2,1,0:T(8,128)S(1)}, u32[]{:S(2)}, u32[]{:S(2)}) %collective-permute-start.31) | collective-permute-done | bytes 65568 | tf_op jit(solution)/shard_map/ppermute | solution.py:276
  146.2 1.4 advance.30
  154.6 6.1 %collective-permute-done.35.refs_2_ = f32[2,64,128]{2,1,0:T(8,128)S(1)} collective-permute-done((f32[2,64,128]{2,1,0:T(8,128)S(1)}, f32[2,64,128]{2,1,0:T(8,128)S(1)}, u32[]{:S(2)}, u32[]{:S(2)}) %collective-permute-start.35) | collective-permute-done | bytes 65568 | tf_op jit(solution)/shard_map/ppermute | solution.py:276
  161.9 10.3 %all_to_all.11.all_ref = f32[16,32,128]{2,1,0:T(8,128)S(1)} all-to-all(f32[16,32,128]{2,1,0:T(8,128)S(1)} %get-tuple-element.102), channel_id=1, replica_groups=mesh['q'=16,'c'=2,'space'=16] {'q'}, dimensions={0} | all-to-all | bytes 524288 | tf_op jit(solution)/shard_map/all_to_all | solution.py:333
  172.7 1.9 %collective-permute-start.37 = (f32[64,128]{1,0:T(8,128)S(1)}, f32[64,128]{1,0:T(8,128)S(1)}, u32[]{:S(2)}, u32[]{:S(2)}) collective-permute-start(f32[64,128]{1,0:T(8,128)S(1)} %get-tuple-element.106), channel_id=1, source_target_pairs={{0,16},{16,0},{1,17},{17,1},{2,18},{18,2},{3,19},{19,3},{4,20},{20... | collective-permute-start | bytes 98312 | tf_op jit(solution)/shard_map/ppermute | solution.py:269
  (92 shorter events, 71.5 us)
Async XLA Ops:
  4.0 7.1 %collective-permute-start = (f32[3,64,128]{2,1,0:T(8,128)S(1)}, f32[3,64,128]{2,1,0:T(8,128)S(1)}, u32[]{:S(2)}, u32[]{:S(2)}) collective-permute-start(f32[3,64,128]{2,1,0:T(8,128)S(1)} %get-tuple-element.56), channel_id=1, source_target_pairs={{0,16},{16,0},{1,17},{17,1},{2,18},{18,2},{3,19},{19,3},{4,20},{20... | collective-permute-start | bytes 294920 | tf_op jit(solution)/shard_map/ppermute | solution.py:269
  11.3 3.1 %collective-permute-start.2 = (f32[2,64,128]{2,1,0:T(8,128)S(1)}, f32[2,64,128]{2,1,0:T(8,128)S(1)}, u32[]{:S(2)}, u32[]{:S(2)}) collective-permute-start(f32[2,64,128]{2,1,0:T(8,128)S(1)} %get-tuple-element.59.refs_0_), channel_id=1, source_target_pairs={{0,16},{1,17},{2,18},{3,19},{4,20},{5,21},{6,22},{7,23},{8,24},{9,... | collective-permute-start | bytes 196616 | tf_op jit(solution)/shard_map/ppermute | solution.py:277
  12.6 7.1 %collective-permute-start.1 = (f32[2,64,128]{2,1,0:T(8,128)S(1)}, f32[2,64,128]{2,1,0:T(8,128)S(1)}, u32[]{:S(2)}, u32[]{:S(2)}) collective-permute-start(f32[2,64,128]{2,1,0:T(8,128)S(1)} %get-tuple-element.59.refs_0_), channel_id=1, source_target_pairs={{1,16},{2,17},{3,18},{4,19},{5,20},{6,21},{7,22},{8,23},{9,24},{10... | collective-permute-start | bytes 196616 | tf_op jit(solution)/shard_map/ppermute | solution.py:276
  21.6 2.6 %collective-permute-start.3 = (f32[2,64,128]{2,1,0:T(8,128)S(1)}, f32[2,64,128]{2,1,0:T(8,128)S(1)}, u32[]{:S(2)}, u32[]{:S(2)}) collective-permute-start(f32[2,64,128]{2,1,0:T(8,128)S(1)} %get-tuple-element.65.refs_0_), channel_id=1, source_target_pairs={{16,1},{17,2},{18,3},{19,4},{20,5},{21,6},{22,7},{23,8},{24,9},{25... | collective-permute-start | bytes 196616 | tf_op jit(solution)/shard_map/ppermute | solution.py:276
  24.2 3.1 %collective-permute-start.6 = (f32[2,64,128]{2,1,0:T(8,128)S(1)}, f32[2,64,128]{2,1,0:T(8,128)S(1)}, u32[]{:S(2)}, u32[]{:S(2)}) collective-permute-start(f32[2,64,128]{2,1,0:T(8,128)S(1)} %get-tuple-element.67.refs_0_), channel_id=1, source_target_pairs={{0,16},{1,17},{2,18},{3,19},{4,20},{5,21},{6,22},{7,23},{8,24},{9,... | collective-permute-start | bytes 196616 | tf_op jit(solution)/shard_map/ppermute | solution.py:277
  25.5 8.1 %collective-permute-start.5 = (f32[2,64,128]{2,1,0:T(8,128)S(1)}, f32[2,64,128]{2,1,0:T(8,128)S(1)}, u32[]{:S(2)}, u32[]{:S(2)}) collective-permute-start(f32[2,64,128]{2,1,0:T(8,128)S(1)} %get-tuple-element.67.refs_0_), channel_id=1, source_target_pairs={{1,16},{2,17},{3,18},{4,19},{5,20},{6,21},{7,22},{8,23},{9,24},{10... | collective-permute-start | bytes 196616 | tf_op jit(solution)/shard_map/ppermute | solution.py:276
  36.3 2.6 %collective-permute-start.7 = (f32[2,64,128]{2,1,0:T(8,128)S(1)}, f32[2,64,128]{2,1,0:T(8,128)S(1)}, u32[]{:S(2)}, u32[]{:S(2)}) collective-permute-start(f32[2,64,128]{2,1,0:T(8,128)S(1)} %get-tuple-element.69.refs_0_), channel_id=1, source_target_pairs={{16,1},{17,2},{18,3},{19,4},{20,5},{21,6},{22,7},{23,8},{24,9},{25... | collective-permute-start | bytes 196616 | tf_op jit(solution)/shard_map/ppermute | solution.py:276
  38.9 3.1 %collective-permute-start.10 = (f32[2,64,128]{2,1,0:T(8,128)S(1)}, f32[2,64,128]{2,1,0:T(8,128)S(1)}, u32[]{:S(2)}, u32[]{:S(2)}) collective-permute-start(f32[2,64,128]{2,1,0:T(8,128)S(1)} %get-tuple-element.71.refs_0_), channel_id=1, source_target_pairs={{0,16},{1,17},{2,18},{3,19},{4,20},{5,21},{6,22},{7,23},{8,24},{9,... | collective-permute-start | bytes 196616 | tf_op jit(solution)/shard_map/ppermute | solution.py:277
  40.2 8.1 %collective-permute-start.9 = (f32[2,64,128]{2,1,0:T(8,128)S(1)}, f32[2,64,128]{2,1,0:T(8,128)S(1)}, u32[]{:S(2)}, u32[]{:S(2)}) collective-permute-start(f32[2,64,128]{2,1,0:T(8,128)S(1)} %get-tuple-element.71.refs_0_), channel_id=1, source_target_pairs={{1,16},{2,17},{3,18},{4,19},{5,20},{6,21},{7,22},{8,23},{9,24},{10... | collective-permute-start | bytes 196616 | tf_op jit(solution)/shard_map/ppermute | solution.py:276
  53.6 3.1 %collective-permute-start.14 = (f32[2,64,128]{2,1,0:T(8,128)S(1)}, f32[2,64,128]{2,1,0:T(8,128)S(1)}, u32[]{:S(2)}, u32[]{:S(2)}) collective-permute-start(f32[2,64,128]{2,1,0:T(8,128)S(1)} %get-tuple-element.75.refs_0_), channel_id=1, source_target_pairs={{0,16},{1,17},{2,18},{3,19},{4,20},{5,21},{6,22},{7,23},{8,24},{9,... | collective-permute-start | bytes 196616 | tf_op jit(solution)/shard_map/ppermute | solution.py:277
  54.9 8.1 %collective-permute-start.13 = (f32[2,64,128]{2,1,0:T(8,128)S(1)}, f32[2,64,128]{2,1,0:T(8,128)S(1)}, u32[]{:S(2)}, u32[]{:S(2)}) collective-permute-start(f32[2,64,128]{2,1,0:T(8,128)S(1)} %get-tuple-element.75.refs_0_), channel_id=1, source_target_pairs={{1,16},{2,17},{3,18},{4,19},{5,20},{6,21},{7,22},{8,23},{9,24},{10... | collective-permute-start | bytes 196616 | tf_op jit(solution)/shard_map/ppermute | solution.py:276
  68.4 3.1 %collective-permute-start.18 = (f32[2,64,128]{2,1,0:T(8,128)S(1)}, f32[2,64,128]{2,1,0:T(8,128)S(1)}, u32[]{:S(2)}, u32[]{:S(2)}) collective-permute-start(f32[2,64,128]{2,1,0:T(8,128)S(1)} %get-tuple-element.79.refs_0_), channel_id=1, source_target_pairs={{0,16},{1,17},{2,18},{3,19},{4,20},{5,21},{6,22},{7,23},{8,24},{9,... | collective-permute-start | bytes 196616 | tf_op jit(solution)/shard_map/ppermute | solution.py:277
  69.6 8.0 %collective-permute-start.17 = (f32[2,64,128]{2,1,0:T(8,128)S(1)}, f32[2,64,128]{2,1,0:T(8,128)S(1)}, u32[]{:S(2)}, u32[]{:S(2)}) collective-permute-start(f32[2,64,128]{2,1,0:T(8,128)S(1)} %get-tuple-element.79.refs_0_), channel_id=1, source_target_pairs={{1,16},{2,17},{3,18},{4,19},{5,20},{6,21},{7,22},{8,23},{9,24},{10... | collective-permute-start | bytes 196616 | tf_op jit(solution)/shard_map/ppermute | solution.py:276
  94.7 3.1 %collective-permute-start.20 = (f32[2,64,128]{2,1,0:T(8,128)S(1)}, f32[2,64,128]{2,1,0:T(8,128)S(1)}, u32[]{:S(2)}, u32[]{:S(2)}) collective-permute-start(f32[2,64,128]{2,1,0:T(8,128)S(1)} %get-tuple-element.84.refs_0_), channel_id=1, source_target_pairs={{0,16},{1,17},{2,18},{3,19},{4,20},{5,21},{6,22},{7,23},{8,24},{9,... | collective-permute-start | bytes 196616 | tf_op jit(solution)/shard_map/ppermute | solution.py:277
  96.0 6.8 %collective-permute-start.19 = (f32[2,64,128]{2,1,0:T(8,128)S(1)}, f32[2,64,128]{2,1,0:T(8,128)S(1)}, u32[]{:S(2)}, u32[]{:S(2)}) collective-permute-start(f32[2,64,128]{2,1,0:T(8,128)S(1)} %get-tuple-element.84.refs_0_), channel_id=1, source_target_pairs={{1,16},{2,17},{3,18},{4,19},{5,20},{6,21},{7,22},{8,23},{9,24},{10... | collective-permute-start | bytes 196616 | tf_op jit(solution)/shard_map/ppermute | solution.py:276
  107.3 3.3 %collective-permute-start.24 = (f32[2,64,128]{2,1,0:T(8,128)S(1)}, f32[2,64,128]{2,1,0:T(8,128)S(1)}, u32[]{:S(2)}, u32[]{:S(2)}) collective-permute-start(f32[2,64,128]{2,1,0:T(8,128)S(1)} %get-tuple-element.88.refs_0_), channel_id=1, source_target_pairs={{0,16},{1,17},{2,18},{3,19},{4,20},{5,21},{6,22},{7,23},{8,24},{9,... | collective-permute-start | bytes 196616 | tf_op jit(solution)/shard_map/ppermute | solution.py:277
  108.6 8.1 %collective-permute-start.23 = (f32[2,64,128]{2,1,0:T(8,128)S(1)}, f32[2,64,128]{2,1,0:T(8,128)S(1)}, u32[]{:S(2)}, u32[]{:S(2)}) collective-permute-start(f32[2,64,128]{2,1,0:T(8,128)S(1)} %get-tuple-element.88.refs_0_), channel_id=1, source_target_pairs={{1,16},{2,17},{3,18},{4,19},{5,20},{6,21},{7,22},{8,23},{9,24},{10... | collective-permute-start | bytes 196616 | tf_op jit(solution)/shard_map/ppermute | solution.py:276
  122.0 3.1 %collective-permute-start.28 = (f32[2,64,128]{2,1,0:T(8,128)S(1)}, f32[2,64,128]{2,1,0:T(8,128)S(1)}, u32[]{:S(2)}, u32[]{:S(2)}) collective-permute-start(f32[2,64,128]{2,1,0:T(8,128)S(1)} %get-tuple-element.92.refs_0_), channel_id=1, source_target_pairs={{0,16},{1,17},{2,18},{3,19},{4,20},{5,21},{6,22},{7,23},{8,24},{9,... | collective-permute-start | bytes 196616 | tf_op jit(solution)/shard_map/ppermute | solution.py:277
  123.3 8.1 %collective-permute-start.27 = (f32[2,64,128]{2,1,0:T(8,128)S(1)}, f32[2,64,128]{2,1,0:T(8,128)S(1)}, u32[]{:S(2)}, u32[]{:S(2)}) collective-permute-start(f32[2,64,128]{2,1,0:T(8,128)S(1)} %get-tuple-element.92.refs_0_), channel_id=1, source_target_pairs={{1,16},{2,17},{3,18},{4,19},{5,20},{6,21},{7,22},{8,23},{9,24},{10... | collective-permute-start | bytes 196616 | tf_op jit(solution)/shard_map/ppermute | solution.py:276
  136.8 3.1 %collective-permute-start.32 = (f32[2,64,128]{2,1,0:T(8,128)S(1)}, f32[2,64,128]{2,1,0:T(8,128)S(1)}, u32[]{:S(2)}, u32[]{:S(2)}) collective-permute-start(f32[2,64,128]{2,1,0:T(8,128)S(1)} %get-tuple-element.96.refs_0_), channel_id=1, source_target_pairs={{0,16},{1,17},{2,18},{3,19},{4,20},{5,21},{6,22},{7,23},{8,24},{9,... | collective-permute-start | bytes 196616 | tf_op jit(solution)/shard_map/ppermute | solution.py:277
  138.0 8.1 %collective-permute-start.31 = (f32[2,64,128]{2,1,0:T(8,128)S(1)}, f32[2,64,128]{2,1,0:T(8,128)S(1)}, u32[]{:S(2)}, u32[]{:S(2)}) collective-permute-start(f32[2,64,128]{2,1,0:T(8,128)S(1)} %get-tuple-element.96.refs_0_), channel_id=1, source_target_pairs={{1,16},{2,17},{3,18},{4,19},{5,20},{6,21},{7,22},{8,23},{9,24},{10... | collective-permute-start | bytes 196616 | tf_op jit(solution)/shard_map/ppermute | solution.py:276
  151.5 3.1 %collective-permute-start.36 = (f32[2,64,128]{2,1,0:T(8,128)S(1)}, f32[2,64,128]{2,1,0:T(8,128)S(1)}, u32[]{:S(2)}, u32[]{:S(2)}) collective-permute-start(f32[2,64,128]{2,1,0:T(8,128)S(1)} %get-tuple-element.100.refs_0_), channel_id=1, source_target_pairs={{0,16},{1,17},{2,18},{3,19},{4,20},{5,21},{6,22},{7,23},{8,24},{9,... | collective-permute-start | bytes 196616 | tf_op jit(solution)/shard_map/ppermute | solution.py:277
  152.8 8.0 %collective-permute-start.35 = (f32[2,64,128]{2,1,0:T(8,128)S(1)}, f32[2,64,128]{2,1,0:T(8,128)S(1)}, u32[]{:S(2)}, u32[]{:S(2)}) collective-permute-start(f32[2,64,128]{2,1,0:T(8,128)S(1)} %get-tuple-element.100.refs_0_), channel_id=1, source_target_pairs={{1,16},{2,17},{3,18},{4,19},{5,20},{6,21},{7,22},{8,23},{9,24},{10... | collective-permute-start | bytes 196616 | tf_op jit(solution)/shard_map/ppermute | solution.py:276
  172.7 3.1 %collective-permute-start.37 = (f32[64,128]{1,0:T(8,128)S(1)}, f32[64,128]{1,0:T(8,128)S(1)}, u32[]{:S(2)}, u32[]{:S(2)}) collective-permute-start(f32[64,128]{1,0:T(8,128)S(1)} %get-tuple-element.106), channel_id=1, source_target_pairs={{0,16},{16,0},{1,17},{17,1},{2,18},{18,2},{3,19},{19,3},{4,20},{20... | collective-permute-start | bytes 98312 | tf_op jit(solution)/shard_map/ppermute | solution.py:269
  (21 other events, 42.8 us)

commit v2 on v1

--- a/solution.py
+++ b/solution.py
@@ -22,22 +22,37 @@
     return pltpu.with_memory_space_constraint(x, pltpu.VMEM)
 
 
-def call(kernel, name, outs, *args, keep=True, flops=1 << 22):
+def hbm(x):
+    return pltpu.with_memory_space_constraint(x, pltpu.HBM)
+
+
+def call(kernel, name, outs, *args, keep=True, fetch=False, scratch=(FIELD,), flops=1 << 22):
     whole = pl.BlockSpec(memory_space=pltpu.VMEM)
     shapes = tuple(
         pltpu.VMEM(shape, dtype) if keep else jax.ShapeDtypeStruct(shape, dtype)
         for shape, dtype in outs
     )
+    held = [pltpu.VMEM(shape, F32) for shape in scratch]
+    if fetch:
+        held += [pltpu.VMEM(arg.shape, arg.dtype) for arg in args[:3]]
+        held += [pltpu.SemaphoreType.DMA((12,))]
     return pl.pallas_call(
         kernel,
         out_shape=shapes,
-        in_specs=[whole] * len(args),
+        in_specs=[pl.BlockSpec(memory_space=pl.ANY) if fetch else whole] * len(args),
         out_specs=(whole,) * len(shapes),
-        scratch_shapes=[pltpu.VMEM(FIELD, F32)],
+        scratch_shapes=held,
         cost_estimate=pl.CostEstimate(flops=flops, bytes_accessed=1 << 20, transcendentals=0),
         compiler_params=pltpu.CompilerParams(vmem_limit_bytes=16 << 20),
         name=name,
     )(*args)
+
+
+def fetched(copies):
+    for copy in copies:
+        copy.start()
+    for copy in copies:
+        copy.wait()
 
 
 def low_half():
@@ -72,33 +87,59 @@
     return sums[0] + sums[1]
 
 
-def coupling(field, far, near, index, valid, faces):
+def product(left, right):
+    return jnp.dot(left, right, precision=HIGHEST, preferred_element_type=F32)
+
+
+def own_faces(field, index, valid, faces):
     picked = [
         columns(field, index[f : f + 1, :]) * jnp.broadcast_to(valid[f : f + 1, :], FIELD)
         for f in range(4)
     ]
-    stacked = jnp.concatenate(picked + [far, near], axis=0)
-    return jnp.dot(faces, stacked, precision=HIGHEST, preferred_element_type=F32)
-
-
-def share_kernel(send_ref, forcing_ref, gain_ref, state_ref, own_ref, out_ref, start_ref, _):
-    core = lax.axis_index("c")
+    return product(faces[:, : 4 * VALUES], jnp.concatenate(picked, axis=0))
+
+
+def share_kernel(send_any, forcing_any, gain_any, state_any, own_ref, out_ref, start_ref, state_ref,
+                 send_ref, forcing_ref, gain_ref, sems):
+    core = lax.axis_index("c")
+    fetched([
+        pltpu.make_async_copy(send_any, send_ref, sems.at[0]),
+        pltpu.make_async_copy(forcing_any, forcing_ref, sems.at[1]),
+        pltpu.make_async_copy(gain_any, gain_ref, sems.at[2]),
+        pltpu.make_async_copy(state_any, state_ref, sems.at[3]),
+    ])
     mine, other = layer_rows(send_ref, core)
     low = low_half()
     fields = [forcing_ref[m] for m in range(STEPS)] + [gain_ref[0]]
-    for m, field in enumerate(fields):
-        own_ref[m] = columns(field, mine)
     for m in range(0, STEPS, 2):
         out_ref[m // 2] = jnp.where(low, columns(fields[m], other), columns(fields[m + 1], other))
     out_ref[STEPS // 2] = columns(fields[STEPS], other)
+    for m, field in enumerate(fields):
+        own_ref[m] = columns(field, mine)
     start_ref[...] = columns(state_ref[...], mine)
 
 
 def tables_kernel(
-    send_ref, neighbor_ref, inverse_ref, blocks_ref, index_ref, valid_ref, place_ref, faces_ref,
-    table_ref, _
+    send_any, neighbor_any, blocks_any, inverse_any, index_ref, valid_ref, place_ref, faces_ref,
+    table_ref, chunks_ref, send_ref, neighbor_ref, blocks_ref, sems
 ):
     core = lax.axis_index("c")
+    group = VALUES // 8
+    small = [
+        pltpu.make_async_copy(send_any, send_ref, sems.at[8]),
+        pltpu.make_async_copy(neighbor_any, neighbor_ref, sems.at[9]),
+        pltpu.make_async_copy(blocks_any, blocks_ref, sems.at[10]),
+    ]
+    large = [
+        pltpu.make_async_copy(
+            inverse_any.at[:, pl.ds(8 * k, 8), :], chunks_ref.at[k], sems.at[k]
+        )
+        for k in range(group)
+    ]
+    for copy in small + large:
+        copy.start()
+    for copy in small:
+        copy.wait()
     mine, _other = layer_rows(send_ref, core)
     order = jnp.concatenate([send_ref[0:1, :], send_ref[1:2, :]], axis=1)
     down = jnp.transpose(jnp.broadcast_to(order.astype(F32), (LANES, LANES)))
@@ -117,12 +158,15 @@
         faces_ref[:, f * VALUES : (f + 1) * VALUES] = blocks_ref[f]
     faces_ref[:, 4 * VALUES : 5 * VALUES] = jnp.where(core == 0, blocks_ref[4], blocks_ref[5])
     faces_ref[:, 5 * VALUES : 6 * VALUES] = jnp.where(core == 0, blocks_ref[5], blocks_ref[4])
-    for j in range(VALUES):
-        table_ref[j] = columns(inverse_ref[pl.ds(j, VALUES, stride=VALUES), :], mine)
+    for k in range(group):
+        large[k].wait()
+        for j in range(8):
+            table_ref[8 * k + j] = columns(chunks_ref[k, :, j, :], mine)
 
 
 def first_kernel(
-    own_ref, got_ref, start_ref, table_ref, sources_ref, gain_ref, pair_ref, right_ref, scratch
+    own_ref, got_ref, start_ref, index_ref, valid_ref, faces_ref, table_ref, sources_ref, gain_ref,
+    pair_ref, right_ref, ahead_ref, scratch
 ):
     core = lax.axis_index("c")
     low = low_half()
@@ -143,23 +187,32 @@
     right = jnp.where(first, start_ref[...], 0.0) + sources_ref[0]
     right_ref[...] = right
     pair_ref[0] = jnp.zeros(FIELD, F32)
-    pair_ref[1] = apply_inverse(table_ref, scratch, right)
+    field = apply_inverse(table_ref, scratch, right)
+    pair_ref[1] = field
+    ahead_ref[...] = own_faces(field, index_ref[...], valid_ref[...], faces_ref[...])
 
 
 def advance(plan, refs, sourced, scratch):
-    (pair_ref, right_ref, far_ref, near_ref, index_ref, valid_ref, faces_ref, table_ref, sources_ref,
-     pair_out, right_out) = refs
+    (pair_ref, right_ref, ahead_ref, near_ref, far_ref, index_ref, valid_ref, faces_ref, table_ref,
+     sources_ref, pair_out, right_out, ahead_out) = refs
     active, stages = plan
     core = lax.axis_index("c")
 
     @pl.when(core == active)
     def _run():
         index, valid, faces = index_ref[...], valid_ref[...], faces_ref[...]
+        layers = [
+            jnp.concatenate([ref[slot] for _, slot in stages], axis=1) for ref in (far_ref, near_ref)
+        ]
+        across = product(faces[:, 4 * VALUES :], jnp.concatenate(layers, axis=0))
         field = pair_ref[1]
         right = right_ref[...]
-        for stage, slot in stages:
+        summed = ahead_ref[...]
+        for place, (stage, _) in enumerate(stages):
             pair_out[0] = field
-            summed = coupling(field, far_ref[slot], near_ref[slot], index, valid, faces)
+            if place > 0:
+                summed = own_faces(field, index, valid, faces)
+            summed = summed + across[:, place * LANES : (place + 1) * LANES]
             field = apply_inverse(table_ref, scratch, right - summed)
             if stage % 2 == 1 and stage < STAGES - 1:
                 right = field
@@ -173,6 +226,7 @@
     def _keep():
         pair_out[...] = pair_ref[...]
         right_out[...] = right_ref[...]
+        ahead_out[...] = own_faces(pair_ref[1], index_ref[...], valid_ref[...], faces_ref[...])
 
 
 def advance_kernel(plan, sourced, *refs):
@@ -180,8 +234,8 @@
 
 
 def ends_kernel(plan, count, *refs):
-    (*inner, gain_ref, pair_out, right_out, chunk_ref, scratch) = refs
-    advance(plan, (*inner, pair_out, right_out), True, scratch)
+    (*inner, gain_ref, pair_out, chunk_ref, scratch, right_out, ahead_out) = refs
+    advance(plan, (*inner, pair_out, right_out, ahead_out), True, scratch)
     low = low_half()
     gain, end = gain_ref[...], pair_out[1]
     summed = gain * swap_halves(end) + end
@@ -191,8 +245,8 @@
 
 
 def ends_last_kernel(plan, count, *refs):
-    (*inner, gain_ref, shift_ref, pair_out, right_out, residual_ref, chunk_ref, scratch) = refs
-    advance(plan, (*inner, pair_out, right_out), False, scratch)
+    (*inner, gain_ref, shift_ref, pair_out, residual_ref, chunk_ref, scratch, right_out, ahead_out) = refs
+    advance(plan, (*inner, pair_out, right_out, ahead_out), False, scratch)
     gain = gain_ref[...]
     residual = pair_out[1] - gain * shift_ref[...]
     residual_ref[...] = residual
@@ -208,7 +262,10 @@
     return jnp.where(low_half(), before, swap_halves(gain * before + residual))
 
 
-def restart_kernel(count, all_ref, end_ref, gain_ref, table_ref, shift_ref, coarse_ref, pair_ref, scratch):
+def restart_kernel(
+    count, all_ref, end_ref, gain_ref, index_ref, valid_ref, faces_ref, table_ref, shift_ref,
+    coarse_ref, pair_ref, ahead_ref, scratch
+):
     mine = lax.axis_index("q")
     before = jnp.zeros(FIELD, F32)
     for q in range(count):
@@ -219,7 +276,9 @@
     shift_ref[...] = shift
     coarse_ref[...] = gain * shift + end
     pair_ref[0] = jnp.zeros(FIELD, F32)
-    pair_ref[1] = apply_inverse(table_ref, scratch, shift)
+    field = apply_inverse(table_ref, scratch, shift)
+    pair_ref[1] = field
+    ahead_ref[...] = own_faces(field, index_ref[...], valid_ref[...], faces_ref[...])
 
 
 def finish_kernel(count, all_ref, gains_ref, residual_ref, gain_ref, coarse_ref, end_ref, out_ref, _):
@@ -275,60 +334,60 @@
             across = [(depth + z, z + 1) for z in range(depth - 1)]
         far = lax.ppermute(x, ("c", "space"), across)
         near = lax.ppermute(x, "c", [(1 - to, to)])
-        return vmem(far), vmem(near)
+        return vmem(near), vmem(far)
 
     field, pair_shape = (FIELD, F32), ((2,) + FIELD, F32)
     own, sent, start = call(
         share_kernel, "share",
         [((STEPS + 1,) + FIELD, F32), ((STEPS // 2 + 1,) + FIELD, F32), field],
-        send_rows, forcing, coarse_gain, initial_state,
+        hbm(send_rows), hbm(forcing), hbm(coarse_gain), hbm(initial_state), fetch=True,
     )
     got = swap_cores(sent)
     index, valid, place, faces, table = call(
         tables_kernel, "tables",
         [((8, LANES), jnp.int32), ((8, LANES), F32), ((8, LANES), jnp.int32),
          ((VALUES, 6 * VALUES), F32), ((VALUES,) + FIELD, F32)],
-        send_rows, neighbor, vmem(block_inverse.reshape(VALUES * VALUES, LANES)), face_blocks,
+        hbm(send_rows), hbm(neighbor), hbm(face_blocks), hbm(block_inverse), fetch=True,
+        scratch=((VALUES // 8, VALUES, 8, LANES),),
     )
     index, valid, place, faces, table = map(vmem, (index, valid, place, faces, table))
-    sources, gain, pair, right = call(
-        first_kernel, "first", [((STEPS,) + FIELD, F32), field, pair_shape, field],
-        vmem(own), vmem(got), vmem(start), table,
+    operator = (index, valid, faces, table)
+    state = [pair_shape, field, field]
+    sources, gain, *now = call(
+        first_kernel, "first", [((STEPS,) + FIELD, F32), field, *state],
+        vmem(own), vmem(got), vmem(start), *operator,
     )
     sources, gain = vmem(sources), vmem(gain)
     half_phases = list(plans())
-
-    def inner(pair, right, to):
-        pair, right = vmem(pair), vmem(right)
-        far, near = halo(pair, to)
-        return pair, right, far, near, index, valid, faces, table, sources
+    final = half_phases[-1]
+
+    def inner(now, to):
+        now = [vmem(x) for x in now]
+        return (*now, *halo(now[0], to), *operator, sources)
 
     for plan in half_phases[:-1]:
-        pair, right = call(
-            functools.partial(advance_kernel, plan, True), "advance", [pair_shape, field],
-            *inner(pair, right, plan[0]),
+        now = call(
+            functools.partial(advance_kernel, plan, True), "advance", state, *inner(now, plan[0])
         )
-    plan = half_phases[-1]
-    pair, _, chunk = call(
-        functools.partial(ends_kernel, plan, count), "ends",
-        [pair_shape, field, ((count,) + FIELD, F32)], *inner(pair, right, plan[0]), gain,
+    pair, chunk = call(
+        functools.partial(ends_kernel, final, count), "ends",
+        [pair_shape, ((count,) + FIELD, F32)], *inner(now, final[0]), gain, scratch=(FIELD,) * 3,
     )
     gathered = vmem(lax.all_to_all(chunk, "q", 0, 0))
-    shift, coarse, pair = call(
-        functools.partial(restart_kernel, count), "restart", [field, field, pair_shape],
-        gathered, vmem(pair), gain, table,
-    )
-    right = shift = vmem(shift)
+    shift, coarse, *now = call(
+        functools.partial(restart_kernel, count), "restart", [field, field, pair_shape, field],
+        gathered, vmem(pair), gain, *operator,
+    )
+    shift = vmem(shift)
+    now = [now[0], shift, now[1]]
     for plan in half_phases[:-1]:
-        pair, right = call(
-            functools.partial(advance_kernel, plan, False), "advance", [pair_shape, field],
-            *inner(pair, right, plan[0]),
+        now = call(
+            functools.partial(advance_kernel, plan, False), "advance", state, *inner(now, plan[0])
         )
-    plan = half_phases[-1]
-    _, _, residual, chunk = call(
-        functools.partial(ends_last_kernel, plan, count), "ends",
-        [pair_shape, field, field, ((count, VALUES // 2, LANES), F32)],
-        *inner(pair, right, plan[0]), gain, shift,
+    pair, residual, chunk = call(
+        functools.partial(ends_last_kernel, final, count), "ends",
+        [pair_shape, field, ((count, VALUES // 2, LANES), F32)],
+        *inner(now, final[0]), gain, shift, scratch=(FIELD,) * 3,
     )
     sums = vmem(lax.all_to_all(chunk, "q", 0, 0))
     residual = vmem(residual)

time: 178 us -> 152 us (0.85)
  the two profiles are of different devices: /device:TPU:97 before, /device:TPU:385 now
where the time goes in v2:
time: 152 us; the launch traced here: 151 us
  starting transfers between devices  54.2 us (36%)
  waiting for transfers between devices  50.2 us (33%)
  blocking collectives  27.5 us (18%)
  Pallas kernels  18.4 us (12%)
    ppermute x18, waiting for transfers between devices, halo(): far = lax.ppermute(x, ('c', 'space'), across)  29.9 us
    ppermute x18, starting transfers between devices, halo(): near = lax.ppermute(x, 'c', [(1 - to, to)])  24.6 us
    ppermute x18, starting transfers between devices, halo(): far = lax.ppermute(x, ('c', 'space'), across)  23.4 us
    ppermute x18, waiting for transfers between devices, halo(): near = lax.ppermute(x, 'c', [(1 - to, to)])  19.4 us
    pallas_call x24, Pallas kernels, call(): pl.pallas_call(kernel, out_shape=shapes, in_specs=[pl.BlockSpec(memory_sp...  18.4 us
    all_to_all x1, blocking collectives, body(): gathered = vmem(lax.all_to_all(chunk, 'q', 0, 0))  16.7 us
    all_to_all x1, blocking collectives, body(): sums = vmem(lax.all_to_all(chunk, 'q', 0, 0))  10.7 us
    ppermute x2, starting transfers between devices, swap_cores(): return lax.ppermute(x, 'c', [(0, 1), (1, 0)])  6.22 us
  transfers between devices with their start and end apart: 38, of which 29 were waited for; matrix products, arithmetic and copies ran while one was open for 0% of the time, Pallas kernels for 2%

profile of v2, /device:TPU:385, one launch (start us, length us, event | category | flops | bytes accessed | tf_op | source)
XLA Modules:
  0.0 151.4 jit_solution(16875222258465589031)
XLA Ops:
  1.9 2.6 %collective-permute-start = (f32[3,64,128]{2,1,0:T(8,128)S(1)}, f32[3,64,128]{2,1,0:T(8,128)S(1)}, u32[]{:S(2)}, u32[]{:S(2)}) collective-permute-start(f32[3,64,128]{2,1,0:T(8,128)S(1)} %get-tuple-element.74), channel_id=1, source_target_pairs={{0,16},{16,0},{1,17},{17,1},{2,18},{18,2},{3,19},{19,3},{4,20},{20... | collective-permute-start | bytes 294920 | tf_op jit(solution)/shard_map/ppermute | solution.py:328
  4.5 3.0 %tables.1 = (s32[8,128]{1,0:T(8,128)S(1)}, f32[8,128]{1,0:T(8,128)S(1)}, s32[8,128]{1,0:T(8,128)S(1)}, f32[64,384]{1,0:T(8,128)S(1)}, f32[64,64,128]{2,1,0:T(8,128)S(1)}) custom-call(s32[2,64]{1,0:T(2,128)} %send_any.3, s32[6,128]{1,0:T(8,128)} %neighbor_any.1, f32[6,64,64]{2,1,0:T(8,128)} %blocks_any.1, f32[64,64,128]{2,1,0:T(8,128)} %inverse_any.1), custom_call_target="tpu_custom_call" | custom-call | flops 4194304 | bytes 1048576 | tf_op jit(solution)/shard_map/tables/pallas_call | solution.py:39
  10.7 3.0 %collective-permute-done.2.refs_4_ = f32[2,64,128]{2,1,0:T(8,128)S(1)} collective-permute-done((f32[2,64,128]{2,1,0:T(8,128)S(1)}, f32[2,64,128]{2,1,0:T(8,128)S(1)}, u32[]{:S(2)}, u32[]{:S(2)}) %collective-permute-start.2) | collective-permute-done | bytes 65568 | tf_op jit(solution)/shard_map/ppermute | solution.py:335
  14.8 1.4 collective-permute-start.4
  16.2 1.9 %collective-permute-start.3 = (f32[2,64,128]{2,1,0:T(8,128)S(1)}, f32[2,64,128]{2,1,0:T(8,128)S(1)}, u32[]{:S(2)}, u32[]{:S(2)}) collective-permute-start(f32[2,64,128]{2,1,0:T(8,128)S(1)} %get-tuple-element.84.refs_0_), channel_id=1, source_target_pairs={{16,0},{17,1},{18,2},{19,3},{20,4},{21,5},{22,6},{23,7},{24,8},{25... | collective-permute-start | bytes 196616 | tf_op jit(solution)/shard_map/ppermute | solution.py:336
  21.9 3.0 %collective-permute-done.6.refs_4_ = f32[2,64,128]{2,1,0:T(8,128)S(1)} collective-permute-done((f32[2,64,128]{2,1,0:T(8,128)S(1)}, f32[2,64,128]{2,1,0:T(8,128)S(1)}, u32[]{:S(2)}, u32[]{:S(2)}) %collective-permute-start.6) | collective-permute-done | bytes 65568 | tf_op jit(solution)/shard_map/ppermute | solution.py:335
  24.9 1.3 collective-permute-done.5.refs_3_
  33.7 3.0 %collective-permute-done.10.refs_4_ = f32[2,64,128]{2,1,0:T(8,128)S(1)} collective-permute-done((f32[2,64,128]{2,1,0:T(8,128)S(1)}, f32[2,64,128]{2,1,0:T(8,128)S(1)}, u32[]{:S(2)}, u32[]{:S(2)}) %collective-permute-start.10) | collective-permute-done | bytes 65568 | tf_op jit(solution)/shard_map/ppermute | solution.py:335
  45.6 3.0 %collective-permute-done.14.refs_4_ = f32[2,64,128]{2,1,0:T(8,128)S(1)} collective-permute-done((f32[2,64,128]{2,1,0:T(8,128)S(1)}, f32[2,64,128]{2,1,0:T(8,128)S(1)}, u32[]{:S(2)}, u32[]{:S(2)}) %collective-permute-start.14) | collective-permute-done | bytes 65568 | tf_op jit(solution)/shard_map/ppermute | solution.py:335
  48.5 1.3 collective-permute-done.13.refs_3_
  57.4 3.0 %collective-permute-done.18.refs_4_ = f32[2,64,128]{2,1,0:T(8,128)S(1)} collective-permute-done((f32[2,64,128]{2,1,0:T(8,128)S(1)}, f32[2,64,128]{2,1,0:T(8,128)S(1)}, u32[]{:S(2)}, u32[]{:S(2)}) %collective-permute-start.18) | collective-permute-done | bytes 65568 | tf_op jit(solution)/shard_map/ppermute | solution.py:335
  62.2 16.7 %all_to_all.10.all_ref.gains_ref = f32[16,64,128]{2,1,0:T(8,128)S(1)} all-to-all(f32[16,64,128]{2,1,0:T(8,128)S(1)} %get-tuple-element.109), channel_id=1, replica_groups=mesh['q'=16,'c'=2,'space'=16] {'q'}, dimensions={0} | all-to-all | bytes 1048576 | tf_op jit(solution)/shard_map/all_to_all | solution.py:376
  82.3 3.0 %collective-permute-done.20.refs_4_ = f32[2,64,128]{2,1,0:T(8,128)S(1)} collective-permute-done((f32[2,64,128]{2,1,0:T(8,128)S(1)}, f32[2,64,128]{2,1,0:T(8,128)S(1)}, u32[]{:S(2)}, u32[]{:S(2)}) %collective-permute-start.20) | collective-permute-done | bytes 65568 | tf_op jit(solution)/shard_map/ppermute | solution.py:335
  88.3 2.0 %collective-permute-start.21 = (f32[2,64,128]{2,1,0:T(8,128)S(1)}, f32[2,64,128]{2,1,0:T(8,128)S(1)}, u32[]{:S(2)}, u32[]{:S(2)}) collective-permute-start(f32[2,64,128]{2,1,0:T(8,128)S(1)} %get-tuple-element.114.refs_0_), channel_id=1, source_target_pairs={{16,0},{17,1},{18,2},{19,3},{20,4},{21,5},{22,6},{23,7},{24,8},{25... | collective-permute-start | bytes 196616 | tf_op jit(solution)/shard_map/ppermute | solution.py:336
  94.1 3.0 %collective-permute-done.24.refs_4_ = f32[2,64,128]{2,1,0:T(8,128)S(1)} collective-permute-done((f32[2,64,128]{2,1,0:T(8,128)S(1)}, f32[2,64,128]{2,1,0:T(8,128)S(1)}, u32[]{:S(2)}, u32[]{:S(2)}) %collective-permute-start.24) | collective-permute-done | bytes 65568 | tf_op jit(solution)/shard_map/ppermute | solution.py:335
  97.1 1.3 collective-permute-done.23.refs_3_
  106.0 3.0 %collective-permute-done.28.refs_4_ = f32[2,64,128]{2,1,0:T(8,128)S(1)} collective-permute-done((f32[2,64,128]{2,1,0:T(8,128)S(1)}, f32[2,64,128]{2,1,0:T(8,128)S(1)}, u32[]{:S(2)}, u32[]{:S(2)}) %collective-permute-start.28) | collective-permute-done | bytes 65568 | tf_op jit(solution)/shard_map/ppermute | solution.py:335
  108.9 1.3 collective-permute-done.27.refs_3_
  117.8 3.0 %collective-permute-done.32.refs_4_ = f32[2,64,128]{2,1,0:T(8,128)S(1)} collective-permute-done((f32[2,64,128]{2,1,0:T(8,128)S(1)}, f32[2,64,128]{2,1,0:T(8,128)S(1)}, u32[]{:S(2)}, u32[]{:S(2)}) %collective-permute-start.32) | collective-permute-done | bytes 65568 | tf_op jit(solution)/shard_map/ppermute | solution.py:335
  120.8 1.3 collective-permute-done.31.refs_3_
  129.6 3.0 %collective-permute-done.36.refs_4_ = f32[2,64,128]{2,1,0:T(8,128)S(1)} collective-permute-done((f32[2,64,128]{2,1,0:T(8,128)S(1)}, f32[2,64,128]{2,1,0:T(8,128)S(1)}, u32[]{:S(2)}, u32[]{:S(2)}) %collective-permute-start.36) | collective-permute-done | bytes 65568 | tf_op jit(solution)/shard_map/ppermute | solution.py:335
  132.6 1.3 collective-permute-done.35.refs_3_
  134.9 10.7 %all_to_all.11.all_ref = f32[16,32,128]{2,1,0:T(8,128)S(1)} all-to-all(f32[16,32,128]{2,1,0:T(8,128)S(1)} %get-tuple-element.138), channel_id=1, replica_groups=mesh['q'=16,'c'=2,'space'=16] {'q'}, dimensions={0} | all-to-all | bytes 524288 | tf_op jit(solution)/shard_map/all_to_all | solution.py:392
  146.1 3.6 %collective-permute-start.37 = (f32[64,128]{1,0:T(8,128)S(1)}, f32[64,128]{1,0:T(8,128)S(1)}, u32[]{:S(2)}, u32[]{:S(2)}) collective-permute-start(f32[64,128]{1,0:T(8,128)S(1)} %get-tuple-element.142), channel_id=1, source_target_pairs={{0,16},{16,0},{1,17},{17,1},{2,18},{18,2},{3,19},{19,3},{4,20},{20... | collective-permute-start | bytes 98312 | tf_op jit(solution)/shard_map/ppermute | solution.py:328
  (78 shorter events, 70.5 us)
Async XLA Ops:
  1.9 5.6 %collective-permute-start = (f32[3,64,128]{2,1,0:T(8,128)S(1)}, f32[3,64,128]{2,1,0:T(8,128)S(1)}, u32[]{:S(2)}, u32[]{:S(2)}) collective-permute-start(f32[3,64,128]{2,1,0:T(8,128)S(1)} %get-tuple-element.74), channel_id=1, source_target_pairs={{0,16},{16,0},{1,17},{17,1},{2,18},{18,2},{3,19},{19,3},{4,20},{20... | collective-permute-start | bytes 294920 | tf_op jit(solution)/shard_map/ppermute | solution.py:328
  8.1 5.6 %collective-permute-start.2 = (f32[2,64,128]{2,1,0:T(8,128)S(1)}, f32[2,64,128]{2,1,0:T(8,128)S(1)}, u32[]{:S(2)}, u32[]{:S(2)}) collective-permute-start(f32[2,64,128]{2,1,0:T(8,128)S(1)} %get-tuple-element.80.refs_0_), channel_id=1, source_target_pairs={{1,16},{2,17},{3,18},{4,19},{5,20},{6,21},{7,22},{8,23},{9,24},{10... | collective-permute-start | bytes 196616 | tf_op jit(solution)/shard_map/ppermute | solution.py:335
  9.4 5.0 %collective-permute-start.1 = (f32[2,64,128]{2,1,0:T(8,128)S(1)}, f32[2,64,128]{2,1,0:T(8,128)S(1)}, u32[]{:S(2)}, u32[]{:S(2)}) collective-permute-start(f32[2,64,128]{2,1,0:T(8,128)S(1)} %get-tuple-element.80.refs_0_), channel_id=1, source_target_pairs={{0,16},{1,17},{2,18},{3,19},{4,20},{5,21},{6,22},{7,23},{8,24},{9,... | collective-permute-start | bytes 196616 | tf_op jit(solution)/shard_map/ppermute | solution.py:336
  14.8 3.3 %collective-permute-start.4 = (f32[2,64,128]{2,1,0:T(8,128)S(1)}, f32[2,64,128]{2,1,0:T(8,128)S(1)}, u32[]{:S(2)}, u32[]{:S(2)}) collective-permute-start(f32[2,64,128]{2,1,0:T(8,128)S(1)} %get-tuple-element.84.refs_0_), channel_id=1, source_target_pairs={{16,1},{17,2},{18,3},{19,4},{20,5},{21,6},{22,7},{23,8},{24,9},{25... | collective-permute-start | bytes 196616 | tf_op jit(solution)/shard_map/ppermute | solution.py:335
  19.3 5.6 %collective-permute-start.6 = (f32[2,64,128]{2,1,0:T(8,128)S(1)}, f32[2,64,128]{2,1,0:T(8,128)S(1)}, u32[]{:S(2)}, u32[]{:S(2)}) collective-permute-start(f32[2,64,128]{2,1,0:T(8,128)S(1)} %get-tuple-element.87.refs_0_), channel_id=1, source_target_pairs={{1,16},{2,17},{3,18},{4,19},{5,20},{6,21},{7,22},{8,23},{9,24},{10... | collective-permute-start | bytes 196616 | tf_op jit(solution)/shard_map/ppermute | solution.py:335
  20.6 5.6 %collective-permute-start.5 = (f32[2,64,128]{2,1,0:T(8,128)S(1)}, f32[2,64,128]{2,1,0:T(8,128)S(1)}, u32[]{:S(2)}, u32[]{:S(2)}) collective-permute-start(f32[2,64,128]{2,1,0:T(8,128)S(1)} %get-tuple-element.87.refs_0_), channel_id=1, source_target_pairs={{0,16},{1,17},{2,18},{3,19},{4,20},{5,21},{6,22},{7,23},{8,24},{9,... | collective-permute-start | bytes 196616 | tf_op jit(solution)/shard_map/ppermute | solution.py:336
  31.1 5.6 %collective-permute-start.10 = (f32[2,64,128]{2,1,0:T(8,128)S(1)}, f32[2,64,128]{2,1,0:T(8,128)S(1)}, u32[]{:S(2)}, u32[]{:S(2)}) collective-permute-start(f32[2,64,128]{2,1,0:T(8,128)S(1)} %get-tuple-element.93.refs_0_), channel_id=1, source_target_pairs={{1,16},{2,17},{3,18},{4,19},{5,20},{6,21},{7,22},{8,23},{9,24},{10... | collective-permute-start | bytes 196616 | tf_op jit(solution)/shard_map/ppermute | solution.py:335
  32.4 5.6 %collective-permute-start.9 = (f32[2,64,128]{2,1,0:T(8,128)S(1)}, f32[2,64,128]{2,1,0:T(8,128)S(1)}, u32[]{:S(2)}, u32[]{:S(2)}) collective-permute-start(f32[2,64,128]{2,1,0:T(8,128)S(1)} %get-tuple-element.93.refs_0_), channel_id=1, source_target_pairs={{0,16},{1,17},{2,18},{3,19},{4,20},{5,21},{6,22},{7,23},{8,24},{9,... | collective-permute-start | bytes 196616 | tf_op jit(solution)/shard_map/ppermute | solution.py:336
  43.0 5.6 %collective-permute-start.14 = (f32[2,64,128]{2,1,0:T(8,128)S(1)}, f32[2,64,128]{2,1,0:T(8,128)S(1)}, u32[]{:S(2)}, u32[]{:S(2)}) collective-permute-start(f32[2,64,128]{2,1,0:T(8,128)S(1)} %get-tuple-element.99.refs_0_), channel_id=1, source_target_pairs={{1,16},{2,17},{3,18},{4,19},{5,20},{6,21},{7,22},{8,23},{9,24},{10... | collective-permute-start | bytes 196616 | tf_op jit(solution)/shard_map/ppermute | solution.py:335
  44.3 5.6 %collective-permute-start.13 = (f32[2,64,128]{2,1,0:T(8,128)S(1)}, f32[2,64,128]{2,1,0:T(8,128)S(1)}, u32[]{:S(2)}, u32[]{:S(2)}) collective-permute-start(f32[2,64,128]{2,1,0:T(8,128)S(1)} %get-tuple-element.99.refs_0_), channel_id=1, source_target_pairs={{0,16},{1,17},{2,18},{3,19},{4,20},{5,21},{6,22},{7,23},{8,24},{9,... | collective-permute-start | bytes 196616 | tf_op jit(solution)/shard_map/ppermute | solution.py:336
  54.8 5.6 %collective-permute-start.18 = (f32[2,64,128]{2,1,0:T(8,128)S(1)}, f32[2,64,128]{2,1,0:T(8,128)S(1)}, u32[]{:S(2)}, u32[]{:S(2)}) collective-permute-start(f32[2,64,128]{2,1,0:T(8,128)S(1)} %get-tuple-element.105.refs_0_), channel_id=1, source_target_pairs={{1,16},{2,17},{3,18},{4,19},{5,20},{6,21},{7,22},{8,23},{9,24},{10... | collective-permute-start | bytes 196616 | tf_op jit(solution)/shard_map/ppermute | solution.py:335
  56.1 5.6 %collective-permute-start.17 = (f32[2,64,128]{2,1,0:T(8,128)S(1)}, f32[2,64,128]{2,1,0:T(8,128)S(1)}, u32[]{:S(2)}, u32[]{:S(2)}) collective-permute-start(f32[2,64,128]{2,1,0:T(8,128)S(1)} %get-tuple-element.105.refs_0_), channel_id=1, source_target_pairs={{0,16},{1,17},{2,18},{3,19},{4,20},{5,21},{6,22},{7,23},{8,24},{9,... | collective-permute-start | bytes 196616 | tf_op jit(solution)/shard_map/ppermute | solution.py:336
  79.7 5.6 %collective-permute-start.20 = (f32[2,64,128]{2,1,0:T(8,128)S(1)}, f32[2,64,128]{2,1,0:T(8,128)S(1)}, u32[]{:S(2)}, u32[]{:S(2)}) collective-permute-start(f32[2,64,128]{2,1,0:T(8,128)S(1)} %get-tuple-element.111.refs_0_), channel_id=1, source_target_pairs={{1,16},{2,17},{3,18},{4,19},{5,20},{6,21},{7,22},{8,23},{9,24},{10... | collective-permute-start | bytes 196616 | tf_op jit(solution)/shard_map/ppermute | solution.py:335
  81.0 5.6 %collective-permute-start.19 = (f32[2,64,128]{2,1,0:T(8,128)S(1)}, f32[2,64,128]{2,1,0:T(8,128)S(1)}, u32[]{:S(2)}, u32[]{:S(2)}) collective-permute-start(f32[2,64,128]{2,1,0:T(8,128)S(1)} %get-tuple-element.111.refs_0_), channel_id=1, source_target_pairs={{0,16},{1,17},{2,18},{3,19},{4,20},{5,21},{6,22},{7,23},{8,24},{9,... | collective-permute-start | bytes 196616 | tf_op jit(solution)/shard_map/ppermute | solution.py:336
  87.0 3.3 %collective-permute-start.22 = (f32[2,64,128]{2,1,0:T(8,128)S(1)}, f32[2,64,128]{2,1,0:T(8,128)S(1)}, u32[]{:S(2)}, u32[]{:S(2)}) collective-permute-start(f32[2,64,128]{2,1,0:T(8,128)S(1)} %get-tuple-element.114.refs_0_), channel_id=1, source_target_pairs={{16,1},{17,2},{18,3},{19,4},{20,5},{21,6},{22,7},{23,8},{24,9},{25... | collective-permute-start | bytes 196616 | tf_op jit(solution)/shard_map/ppermute | solution.py:335
  91.5 5.6 %collective-permute-start.24 = (f32[2,64,128]{2,1,0:T(8,128)S(1)}, f32[2,64,128]{2,1,0:T(8,128)S(1)}, u32[]{:S(2)}, u32[]{:S(2)}) collective-permute-start(f32[2,64,128]{2,1,0:T(8,128)S(1)} %get-tuple-element.117.refs_0_), channel_id=1, source_target_pairs={{1,16},{2,17},{3,18},{4,19},{5,20},{6,21},{7,22},{8,23},{9,24},{10... | collective-permute-start | bytes 196616 | tf_op jit(solution)/shard_map/ppermute | solution.py:335
  92.8 5.6 %collective-permute-start.23 = (f32[2,64,128]{2,1,0:T(8,128)S(1)}, f32[2,64,128]{2,1,0:T(8,128)S(1)}, u32[]{:S(2)}, u32[]{:S(2)}) collective-permute-start(f32[2,64,128]{2,1,0:T(8,128)S(1)} %get-tuple-element.117.refs_0_), channel_id=1, source_target_pairs={{0,16},{1,17},{2,18},{3,19},{4,20},{5,21},{6,22},{7,23},{8,24},{9,... | collective-permute-start | bytes 196616 | tf_op jit(solution)/shard_map/ppermute | solution.py:336
  103.4 5.6 %collective-permute-start.28 = (f32[2,64,128]{2,1,0:T(8,128)S(1)}, f32[2,64,128]{2,1,0:T(8,128)S(1)}, u32[]{:S(2)}, u32[]{:S(2)}) collective-permute-start(f32[2,64,128]{2,1,0:T(8,128)S(1)} %get-tuple-element.123.refs_0_), channel_id=1, source_target_pairs={{1,16},{2,17},{3,18},{4,19},{5,20},{6,21},{7,22},{8,23},{9,24},{10... | collective-permute-start | bytes 196616 | tf_op jit(solution)/shard_map/ppermute | solution.py:335
  104.7 5.6 %collective-permute-start.27 = (f32[2,64,128]{2,1,0:T(8,128)S(1)}, f32[2,64,128]{2,1,0:T(8,128)S(1)}, u32[]{:S(2)}, u32[]{:S(2)}) collective-permute-start(f32[2,64,128]{2,1,0:T(8,128)S(1)} %get-tuple-element.123.refs_0_), channel_id=1, source_target_pairs={{0,16},{1,17},{2,18},{3,19},{4,20},{5,21},{6,22},{7,23},{8,24},{9,... | collective-permute-start | bytes 196616 | tf_op jit(solution)/shard_map/ppermute | solution.py:336
  115.2 5.6 %collective-permute-start.32 = (f32[2,64,128]{2,1,0:T(8,128)S(1)}, f32[2,64,128]{2,1,0:T(8,128)S(1)}, u32[]{:S(2)}, u32[]{:S(2)}) collective-permute-start(f32[2,64,128]{2,1,0:T(8,128)S(1)} %get-tuple-element.129.refs_0_), channel_id=1, source_target_pairs={{1,16},{2,17},{3,18},{4,19},{5,20},{6,21},{7,22},{8,23},{9,24},{10... | collective-permute-start | bytes 196616 | tf_op jit(solution)/shard_map/ppermute | solution.py:335
  116.5 5.6 %collective-permute-start.31 = (f32[2,64,128]{2,1,0:T(8,128)S(1)}, f32[2,64,128]{2,1,0:T(8,128)S(1)}, u32[]{:S(2)}, u32[]{:S(2)}) collective-permute-start(f32[2,64,128]{2,1,0:T(8,128)S(1)} %get-tuple-element.129.refs_0_), channel_id=1, source_target_pairs={{0,16},{1,17},{2,18},{3,19},{4,20},{5,21},{6,22},{7,23},{8,24},{9,... | collective-permute-start | bytes 196616 | tf_op jit(solution)/shard_map/ppermute | solution.py:336
  127.0 5.6 %collective-permute-start.36 = (f32[2,64,128]{2,1,0:T(8,128)S(1)}, f32[2,64,128]{2,1,0:T(8,128)S(1)}, u32[]{:S(2)}, u32[]{:S(2)}) collective-permute-start(f32[2,64,128]{2,1,0:T(8,128)S(1)} %get-tuple-element.135.refs_0_), channel_id=1, source_target_pairs={{1,16},{2,17},{3,18},{4,19},{5,20},{6,21},{7,22},{8,23},{9,24},{10... | collective-permute-start | bytes 196616 | tf_op jit(solution)/shard_map/ppermute | solution.py:335
  128.3 5.6 %collective-permute-start.35 = (f32[2,64,128]{2,1,0:T(8,128)S(1)}, f32[2,64,128]{2,1,0:T(8,128)S(1)}, u32[]{:S(2)}, u32[]{:S(2)}) collective-permute-start(f32[2,64,128]{2,1,0:T(8,128)S(1)} %get-tuple-element.135.refs_0_), channel_id=1, source_target_pairs={{0,16},{1,17},{2,18},{3,19},{4,20},{5,21},{6,22},{7,23},{8,24},{9,... | collective-permute-start | bytes 196616 | tf_op jit(solution)/shard_map/ppermute | solution.py:336
  146.1 4.5 %collective-permute-start.37 = (f32[64,128]{1,0:T(8,128)S(1)}, f32[64,128]{1,0:T(8,128)S(1)}, u32[]{:S(2)}, u32[]{:S(2)}) collective-permute-start(f32[64,128]{1,0:T(8,128)S(1)} %get-tuple-element.142), channel_id=1, source_target_pairs={{0,16},{16,0},{1,17},{17,1},{2,18},{18,2},{3,19},{19,3},{4,20},{20... | collective-permute-start | bytes 98312 | tf_op jit(solution)/shard_map/ppermute | solution.py:328
  (14 other events, 34.5 us)

commit v3 on v1

v3 whole, which is shorter than its diff:
```python
import functools

import jax
import jax.numpy as jnp
from jax import lax
from jax.experimental import pallas as pl
from jax.experimental.pallas import tpu as pltpu
from jax.sharding import Mesh, PartitionSpec as P


VALUES = 64
LANES = 128
HALF = 64
STEPS = 4
STAGES = 2 * STEPS
HIGHEST = lax.Precision.HIGHEST
F32 = jnp.float32
FIELD = (VALUES, LANES)


def vmem(x):
    return pltpu.with_memory_space_constraint(x, pltpu.VMEM)


def hbm(x):
    return pltpu.with_memory_space_constraint(x, pltpu.HBM)


def call(kernel, name, outs, *args, keep=True, fetch=False, scratch=(FIELD,), flops=1 << 22):
    whole = pl.BlockSpec(memory_space=pltpu.VMEM)
    shapes = tuple(
        pltpu.VMEM(shape, dtype) if keep else jax.ShapeDtypeStruct(shape, dtype)
        for shape, dtype in outs
    )
    held = [pltpu.VMEM(shape, F32) for shape in scratch]
    if fetch:
        held += [pltpu.SemaphoreType.DMA((16,))]
    return pl.pallas_call(
        kernel,
        out_shape=shapes,
        in_specs=[pl.BlockSpec(memory_space=pl.ANY) if fetch else whole] * len(args),
        out_specs=(whole,) * len(shapes),
        scratch_shapes=held,
        cost_estimate=pl.CostEstimate(flops=flops, bytes_accessed=1 << 20, transcendentals=0),
        compiler_params=pltpu.CompilerParams(vmem_limit_bytes=16 << 20),
        name=name,
    )(*args)


def low_half():
    return lax.broadcasted_iota(jnp.int32, FIELD, 1) < HALF


def swap_halves(x):
    return pltpu.roll(x, HALF, 1)


def columns(x, index):
    return jnp.take_along_axis(x, jnp.broadcast_to(index, x.shape), axis=1)


def twice(row):
    return jnp.concatenate([row, row], axis=1)


def layer_rows(send_ref, core):
    lowest, highest = send_ref[0:1, :], send_ref[1:2, :]
    mine = jnp.where(core == 0, lowest, highest)
    other = jnp.where(core == 0, highest, lowest)
    return twice(mine), twice(other)


def apply_inverse(inverse_ref, scratch, vector):
    scratch[...] = vector
    sums = [None, None]
    for j in range(VALUES):
        term = inverse_ref[j] * scratch[j : j + 1, :]
        sums[j % 2] = term if sums[j % 2] is None else sums[j % 2] + term
    return sums[0] + sums[1]


def product(left, right):
    return jnp.dot(left, right, precision=HIGHEST, preferred_element_type=F32)


def own_faces(field, index, valid, faces):
    picked = [
        columns(field, index[f : f + 1, :]) * jnp.broadcast_to(valid[f : f + 1, :], FIELD)
        for f in range(4)
    ]
    return product(faces[:, : 4 * VALUES], jnp.concatenate(picked, axis=0))


def share_kernel(send_any, forcing_any, gain_any, state_any, neighbor_any, blocks_any, inverse_any,
                 own_ref, out_ref, start_ref, send_ref, neighbor_ref, blocks_ref, inverse_ref,
                 state_ref, forcing_ref, gain_ref, sems):
    core = lax.axis_index("c")
    part = VALUES // 8
    first = [
        pltpu.make_async_copy(send_any, send_ref, sems.at[0]),
        pltpu.make_async_copy(forcing_any, forcing_ref, sems.at[1]),
        pltpu.make_async_copy(gain_any, gain_ref, sems.at[2]),
        pltpu.make_async_copy(state_any, state_ref, sems.at[3]),
    ]
    later = [
        pltpu.make_async_copy(neighbor_any, neighbor_ref, sems.at[4]),
        pltpu.make_async_copy(blocks_any, blocks_ref, sems.at[5]),
    ] + [
        pltpu.make_async_copy(
            inverse_any.at[pl.ds(part * k, part)], inverse_ref.at[pl.ds(part * k, part)],
            sems.at[8 + k],
        )
        for k in range(8)
    ]
    for copy in first + later:
        copy.start()
    for copy in first:
        copy.wait()
    mine, other = layer_rows(send_ref, core)
    low = low_half()
    fields = [forcing_ref[m] for m in range(STEPS)] + [gain_ref[0]]
    for m in range(0, STEPS, 2):
        out_ref[m // 2] = jnp.where(low, columns(fields[m], other), columns(fields[m + 1], other))
    out_ref[STEPS // 2] = columns(fields[STEPS], other)
    for m, field in enumerate(fields):
        own_ref[m] = columns(field, mine)
    start_ref[...] = columns(state_ref[...], mine)
    for copy in later:
        copy.wait()


def tables_kernel(
    send_ref, neighbor_ref, blocks_ref, inverse_ref, index_ref, valid_ref, place_ref, faces_ref,
    table_ref, _
):
    core = lax.axis_index("c")
    mine, _other = layer_rows(send_ref, core)
    order = jnp.concatenate([send_ref[0:1, :], send_ref[1:2, :]], axis=1)
    down = jnp.transpose(jnp.broadcast_to(order.astype(F32), (LANES, LANES)))
    across = lax.broadcasted_iota(jnp.int32, (LANES, LANES), 1).astype(F32)
    at = lax.broadcasted_iota(jnp.int32, (LANES, LANES), 0).astype(F32)
    place = jnp.sum(jnp.where(down == across, at, 0.0), axis=0, keepdims=True).astype(jnp.int32)
    place = jnp.broadcast_to(place, (8, LANES))
    place_ref[...] = place
    pad = jnp.zeros((2, LANES), jnp.int32)
    local = columns(jnp.concatenate([neighbor_ref[...], pad], axis=0), mine)
    valid_ref[...] = (local >= 0).astype(F32)
    lane = lax.broadcasted_iota(jnp.int32, (8, LANES), 1)
    spot = columns(place, jnp.clip(local, 0, LANES - 1))
    index_ref[...] = jnp.bitwise_and(spot, HALF - 1) + jnp.where(lane < HALF, 0, HALF)
    for f in range(4):
        faces_ref[:, f * VALUES : (f + 1) * VALUES] = blocks_ref[f]
    faces_ref[:, 4 * VALUES : 5 * VALUES] = jnp.where(core == 0, blocks_ref[4], blocks_ref[5])
    faces_ref[:, 5 * VALUES : 6 * VALUES] = jnp.where(core == 0, blocks_ref[5], blocks_ref[4])
    for j in range(VALUES):
        table_ref[j] = columns(inverse_ref[:, j, :], mine)


def packed(x):
    rows = VALUES // 2
    return jnp.where(low_half()[:rows], x[:rows], swap_halves(x)[rows:])


def unpacked(x):
    low, turned = low_half()[: VALUES // 2], swap_halves(x)
    return jnp.concatenate([jnp.where(low, x, turned), jnp.where(low, turned, x)], axis=0)


def first_kernel(
    own_ref, got_ref, start_ref, table_ref, sources_ref, gain_ref, pair_ref, right_ref, scratch
):
    core = lax.axis_index("c")
    low = low_half()
    is_own = low == (core == 0)
    for m in range(STEPS + 1):
        got = got_ref[m // 2]
        turned = swap_halves(got)
        if m % 2 == 0:
            other = jnp.where(core == 0, turned, got)
        else:
            other = jnp.where(core == 0, got, turned)
        value = jnp.where(is_own, own_ref[m], other)
        if m < STEPS:
            sources_ref[m] = value
        else:
            gain_ref[...] = value
    first = jnp.logical_and(low, lax.axis_index("q") == 0)
    right = jnp.where(first, start_ref[...], 0.0) + sources_ref[0]
    right_ref[...] = right
    begin(right, table_ref, pair_ref, scratch)


def begin(right, table_ref, pair_ref, scratch):
    @pl.when(lax.axis_index("c") == 0)
    def _field():
        pair_ref[0] = jnp.zeros(FIELD, F32)
        pair_ref[1] = apply_inverse(table_ref, scratch, right)

    @pl.when(lax.axis_index("c") != 0)
    def _later():
        pair_ref[...] = jnp.zeros((2,) + FIELD, F32)


def late_kernel(pair_ref, right_ref, index_ref, valid_ref, faces_ref, table_ref, pair_out, ahead_ref,
                scratch):
    core = lax.axis_index("c")

    @pl.when(core == 1)
    def _run():
        field = apply_inverse(table_ref, scratch, right_ref[...])
        pair_out[0] = pair_ref[0]
        pair_out[1] = field
        ahead_ref[...] = own_faces(field, index_ref[...], valid_ref[...], faces_ref[...])

    @pl.when(core == 0)
    def _keep():
        pair_out[...] = pair_ref[...]


def ahead_kernel(active, pair_ref, index_ref, valid_ref, faces_ref, ahead_ref, _):
    @pl.when(lax.axis_index("c") == active)
    def _run():
        ahead_ref[...] = own_faces(pair_ref[1], index_ref[...], valid_ref[...], faces_ref[...])


def advance(plan, refs, sourced, scratch):
    (pair_ref, right_ref, ahead_ref, near_ref, far_ref, index_ref, valid_ref, faces_ref, table_ref,
     sources_ref, pair_out, right_out) = refs
    active, stages = plan
    core = lax.axis_index("c")

    @pl.when(core == active)
    def _run():
        index, valid, faces = index_ref[...], valid_ref[...], faces_ref[...]
        layers = [
            jnp.concatenate([ref[slot] for _, slot in stages], axis=1) for ref in (far_ref, near_ref)
        ]
        across = product(faces[:, 4 * VALUES :], jnp.concatenate(layers, axis=0))
        field = pair_ref[1]
        right = right_ref[...]
        summed = ahead_ref[...]
        for place, (stage, _) in enumerate(stages):
            pair_out[0] = field
            if place > 0:
                summed = own_faces(field, index, valid, faces)
            summed = summed + across[:, place * LANES : (place + 1) * LANES]
            field = apply_inverse(table_ref, scratch, right - summed)
            if stage % 2 == 1 and stage < STAGES - 1:
                right = field
                if sourced:
                    right = right + sources_ref[(stage + 1) // 2]
                field = apply_inverse(table_ref, scratch, right)
        pair_out[1] = field
        right_out[...] = right

    @pl.when(core != active)
    def _keep():
        pair_out[...] = pair_ref[...]
        right_out[...] = right_ref[...]


def advance_kernel(plan, sourced, *refs):
    advance(plan, refs[:-1], sourced, refs[-1])


def ends_kernel(plan, sourced, count, *refs):
    if sourced:
        (*inner, gain_ref, residual_ref, chunk_ref, scratch, pair_out, right_out) = refs
    else:
        (*inner, gain_ref, shift_ref, residual_ref, chunk_ref, scratch, pair_out, right_out) = refs
    advance(plan, (*inner, pair_out, right_out), sourced, scratch)
    gain = gain_ref[...]
    residual = pair_out[1]
    if not sourced:
        residual = residual - gain * shift_ref[...]
    residual_ref[...] = residual
    rows = VALUES // 2
    chunk = packed(swap_halves(gain * swap_halves(residual) + residual))
    if sourced:
        gains = packed(gain * swap_halves(gain))
    for q in range(count):
        chunk_ref[q, :rows] = chunk
        if sourced:
            chunk_ref[q, rows:] = gains


def scanned(count, sums_ref, gains_ref):
    mine = lax.axis_index("q")
    rows = VALUES // 2
    before = jnp.zeros((rows, LANES), F32)
    for q in range(count):
        after = gains_ref[q, rows:] * before + sums_ref[q, :rows]
        before = jnp.where(q < mine, after, before)
    return unpacked(before)


def shifted(before, gain, residual):
    return jnp.where(low_half(), before, swap_halves(gain * before + residual))


def restart_kernel(
    count, sums_ref, end_ref, gain_ref, table_ref, shift_ref, coarse_ref, pair_ref,
    scratch
):
    gain, end = gain_ref[...], end_ref[...]
    shift = shifted(scanned(count, sums_ref, sums_ref), gain, end)
    shift_ref[...] = shift
    coarse_ref[...] = gain * shift + end
    begin(shift, table_ref, pair_ref, scratch)


def finish_kernel(count, sums_ref, gains_ref, residual_ref, gain_ref, coarse_ref, end_ref, out_ref, _):
    core = lax.axis_index("c")
    low = low_half()
    gain, residual = gain_ref[...], residual_ref[...]
    shift = shifted(scanned(count, sums_ref, gains_ref), gain, residual)
    end = coarse_ref[...] + (gain * shift + residual)
    end_ref[...] = end
    out_ref[...] = jnp.where(
        core == 0,
        jnp.where(low, swap_halves(end), residual),
        jnp.where(low, end, swap_halves(residual)),
    )


def output_kernel(end_ref, residual_ref, got_ref, place_ref, end_out, residual_out, _):
    core = lax.axis_index("c")
    low = low_half()
    got = got_ref[...]
    turned = swap_halves(got)
    end, residual = end_ref[...], residual_ref[...]
    end = jnp.where(core == 0, jnp.where(low, end, turned), jnp.where(low, got, end))
    residual = jnp.where(
        core == 0, jnp.where(low, residual, got), jnp.where(low, turned, residual)
    )
    place = place_ref[0:1, :]
    end_out[0] = columns(end, place)
    residual_out[0] = columns(residual, place)


def plans():
    yield 1, [(0, 1)]
    for half in range(2, STAGES + 1):
        yield half % 2, [(half - 2, 0), (half - 1, 1)]
    yield (STAGES + 1) % 2, [(STAGES - 1, 0)]


def body(count, depth, initial_state, forcing, coarse_gain, block_inverse, face_blocks, neighbor, send_rows):
    def swap_cores(x):
        return lax.ppermute(x, "c", [(0, 1), (1, 0)])

    def halo(x, to):
        if to == 1:
            across = [(z + 1, depth + z) for z in range(depth - 1)]
        else:
            across = [(depth + z, z + 1) for z in range(depth - 1)]
        far = lax.ppermute(x, ("c", "space"), across)
        near = lax.ppermute(x, "c", [(1 - to, to)])
        return vmem(near), vmem(far)

    field, pair_shape = (FIELD, F32), ((2,) + FIELD, F32)
    raw = (send_rows, neighbor, face_blocks, block_inverse)
    own, sent, start, *raw = call(
        share_kernel, "share",
        [((STEPS + 1,) + FIELD, F32), ((STEPS // 2 + 1,) + FIELD, F32), field,
         *((x.shape, x.dtype) for x in raw)],
        *map(hbm, (send_rows, forcing, coarse_gain, initial_state, *raw[1:])), fetch=True,
        scratch=(FIELD, forcing.shape, coarse_gain.shape),
    )
    got = swap_cores(sent)
    index, valid, place, faces, table = call(
        tables_kernel, "tables",
        [((8, LANES), jnp.int32), ((8, LANES), F32), ((8, LANES), jnp.int32),
         ((VALUES, 6 * VALUES), F32), ((VALUES,) + FIELD, F32)],
        *map(vmem, raw),
    )
    index, valid, place, faces, table = map(vmem, (index, valid, place, faces, table))
    sources, gain, pair, right = call(
        first_kernel, "first", [((STEPS,) + FIELD, F32), field, pair_shape, field],
        vmem(own), vmem(got), vmem(start), table,
    )
    sources, gain = vmem(sources), vmem(gain)
    half_phases = list(plans())

    def evolve(pair, right, sourced, shift):
        for number, plan in enumerate(half_phases):
            pair, right = vmem(pair), vmem(right)
            near, far = halo(pair, plan[0])
            if number == 0:
                pair, ahead = call(
                    late_kernel, "late", [pair_shape, field], pair, right, index, valid, faces, table
                )
            else:
                (ahead,) = call(
                    functools.partial(ahead_kernel, plan[0]), "ahead", [field], pair, index, valid,
                    faces,
                )
            args = (vmem(pair), right, vmem(ahead), near, far, index, valid, faces, table, sources)
            if number < len(half_phases) - 1:
                pair, right = call(
                    functools.partial(advance_kernel, plan, sourced), "advance",
                    [pair_shape, field], *args,
                )
        residual, chunk = call(
            functools.partial(ends_kernel, plan, sourced, count), "ends",
            [field, ((count, VALUES if sourced else VALUES // 2, LANES), F32)], *args, gain,
            *shift, scratch=(FIELD, (2,) + FIELD, FIELD),
        )
        return vmem(residual), vmem(lax.all_to_all(chunk, "q", 0, 0))

    end, sums = evolve(pair, right, True, ())
    shift, coarse, pair = call(
        functools.partial(restart_kernel, count), "restart", [field, field, pair_shape],
        sums, end, gain, table,
    )
    shift = vmem(shift)
    gains = sums
    residual, sums = evolve(pair, shift, False, (shift,))
    end, sent = call(
        functools.partial(finish_kernel, count), "finish", [field, field],
        sums, gains, residual, gain, vmem(coarse),
    )
    got = vmem(swap_cores(sent))
    return call(
        output_kernel, "output", [((1,) + FIELD, F32)] * 2, vmem(end), residual, got, place,
        keep=False,
    )


def solution(mesh):
    slices, depth = mesh.devices.shape
    count = slices // 2
    pairs = Mesh(mesh.devices.reshape(count, 2, depth), ("q", "c", "space"))
    tm = ("q", "c")
    return jax.shard_map(
        functools.partial(body, count, depth),
        mesh=pairs,
        in_specs=(
            P(None, "space"),
            P(tm, None, "space"),
            P(tm, None, "space"),
            P(None, None, "space"),
            P(),
            P(None, "space"),
            P(None, "space"),
        ),
        out_specs=(P(tm, None, "space"), P(tm, None, "space")),
        check_vma=False,
    )
```

time: 178 us -> 147 us (0.83)
  the two profiles are of different devices: /device:TPU:97 before, /device:TPU:385 now
where the time goes in v3:
time: 147 us; the launch traced here: 146 us
  starting transfers between devices  53.3 us (36%)
  waiting for transfers between devices  46.5 us (32%)
  blocking collectives  28.1 us (19%)
  Pallas kernels  17 us (12%)
    all_to_all x2, blocking collectives, evolve(): return (vmem(residual), vmem(lax.all_to_all(chunk, 'q', 0, 0)))  28.1 us
    ppermute x18, waiting for transfers between devices, halo(): far = lax.ppermute(x, ('c', 'space'), across)  26.9 us
    ppermute x18, starting transfers between devices, halo(): near = lax.ppermute(x, 'c', [(1 - to, to)])  24.2 us
    ppermute x18, starting transfers between devices, halo(): far = lax.ppermute(x, ('c', 'space'), across)  23.2 us
    ppermute x18, waiting for transfers between devices, halo(): near = lax.ppermute(x, 'c', [(1 - to, to)])  18.7 us
    pallas_call x42, Pallas kernels, call(): pl.pallas_call(kernel, out_shape=shapes, in_specs=[pl.BlockSpec(memory_sp...  17 us
    ppermute x2, starting transfers between devices, swap_cores(): return lax.ppermute(x, 'c', [(0, 1), (1, 0)])  5.95 us
  transfers between devices with their start and end apart: 38, of which 29 were waited for; matrix products, arithmetic and copies ran while one was open for 0% of the time, Pallas kernels for 4%

profile of v3, /device:TPU:385, one launch (start us, length us, event | category | flops | bytes accessed | tf_op | source)
XLA Modules:
  0.0 146.2 jit_solution(10908802222954599457)
XLA Ops:
  0.6 1.9 %share.1 = (f32[5,64,128]{2,1,0:T(8,128)S(1)}, f32[3,64,128]{2,1,0:T(8,128)S(1)}, f32[64,128]{1,0:T(8,128)S(1)}, s32[2,64]{1,0:T(2,128)S(1)}, s32[6,128]{1,0:T(8...) custom-call(s32[2,64]{1,0:T(2,128)} %send_any.1, f32[4,64,128]{2,1,0:T(8,128)} %forcing_any.1, ...), custom_call_target="tpu_custom_call" | custom-call | flops 4194304 | bytes 1048576 | tf_op jit(solution)/shard_map/share/pallas_call | solution.py:38
  2.5 2.6 %collective-permute-start = (f32[3,64,128]{2,1,0:T(8,128)S(1)}, f32[3,64,128]{2,1,0:T(8,128)S(1)}, u32[]{:S(2)}, u32[]{:S(2)}) collective-permute-start(f32[3,64,128]{2,1,0:T(8,128)S(1)} %get-tuple-element.64), channel_id=1, source_target_pairs={{0,16},{16,0},{1,17},{17,1},{2,18},{18,2},{3,19},{19,3},{4,20},{20... | collective-permute-start | bytes 294920 | tf_op jit(solution)/shard_map/ppermute | solution.py:350
  9.7 2.4 %collective-permute-done.2.refs_4_ = f32[2,64,128]{2,1,0:T(8,128)S(1)} collective-permute-done((f32[2,64,128]{2,1,0:T(8,128)S(1)}, f32[2,64,128]{2,1,0:T(8,128)S(1)}, u32[]{:S(2)}, u32[]{:S(2)}) %collective-permute-start.2) | collective-permute-done | bytes 65568 | tf_op jit(solution)/shard_map/ppermute | solution.py:357
  13.2 1.3 collective-permute-start.4
  14.5 1.7 %collective-permute-start.3 = (f32[2,64,128]{2,1,0:T(8,128)S(1)}, f32[2,64,128]{2,1,0:T(8,128)S(1)}, u32[]{:S(2)}, u32[]{:S(2)}) collective-permute-start(f32[2,64,128]{2,1,0:T(8,128)S(1)} %get-tuple-element.79.pair_ref.refs_0_), channel_id=1, source_target_pairs={{16,0},{17,1},{18,2},{19,3},{20,4},{21,5},{22,6},{23,7},{24,8},{25... | collective-permute-start | bytes 196616 | tf_op jit(solution)/shard_map/ppermute | solution.py:358
  20.0 2.6 %collective-permute-done.6.refs_4_ = f32[2,64,128]{2,1,0:T(8,128)S(1)} collective-permute-done((f32[2,64,128]{2,1,0:T(8,128)S(1)}, f32[2,64,128]{2,1,0:T(8,128)S(1)}, u32[]{:S(2)}, u32[]{:S(2)}) %collective-permute-start.6) | collective-permute-done | bytes 65568 | tf_op jit(solution)/shard_map/ppermute | solution.py:357
  22.6 1.6 %collective-permute-done.5.refs_3_ = f32[2,64,128]{2,1,0:T(8,128)S(1)} collective-permute-done((f32[2,64,128]{2,1,0:T(8,128)S(1)}, f32[2,64,128]{2,1,0:T(8,128)S(1)}, u32[]{:S(2)}, u32[]{:S(2)}) %collective-permute-start.5) | collective-permute-done | bytes 65568 | tf_op jit(solution)/shard_map/ppermute | solution.py:358
  26.6 1.3 collective-permute-start.7
  31.7 2.9 %collective-permute-done.10.refs_4_ = f32[2,64,128]{2,1,0:T(8,128)S(1)} collective-permute-done((f32[2,64,128]{2,1,0:T(8,128)S(1)}, f32[2,64,128]{2,1,0:T(8,128)S(1)}, u32[]{:S(2)}, u32[]{:S(2)}) %collective-permute-start.10) | collective-permute-done | bytes 65568 | tf_op jit(solution)/shard_map/ppermute | solution.py:357
  36.9 1.3 collective-permute-start.12
  38.2 1.3 collective-permute-start.11
  43.3 2.9 %collective-permute-done.14.refs_4_ = f32[2,64,128]{2,1,0:T(8,128)S(1)} collective-permute-done((f32[2,64,128]{2,1,0:T(8,128)S(1)}, f32[2,64,128]{2,1,0:T(8,128)S(1)}, u32[]{:S(2)}, u32[]{:S(2)}) %collective-permute-start.14) | collective-permute-done | bytes 65568 | tf_op jit(solution)/shard_map/ppermute | solution.py:357
  54.9 2.7 %collective-permute-done.18.refs_4_ = f32[2,64,128]{2,1,0:T(8,128)S(1)} collective-permute-done((f32[2,64,128]{2,1,0:T(8,128)S(1)}, f32[2,64,128]{2,1,0:T(8,128)S(1)}, u32[]{:S(2)}, u32[]{:S(2)}) %collective-permute-start.18) | collective-permute-done | bytes 65568 | tf_op jit(solution)/shard_map/ppermute | solution.py:357
  59.5 17.2 %all_to_all.10.sums_ref.gains_ref = f32[16,64,128]{2,1,0:T(8,128)S(1)} all-to-all(f32[16,64,128]{2,1,0:T(8,128)S(1)} %get-tuple-element.96), channel_id=1, replica_groups=mesh['q'=16,'c'=2,'space'=16] {'q'}, dimensions={0} | all-to-all | bytes 1048576 | tf_op jit(solution)/shard_map/all_to_all | solution.py:409
  78.2 1.5 %collective-permute-start.19 = (f32[2,64,128]{2,1,0:T(8,128)S(1)}, f32[2,64,128]{2,1,0:T(8,128)S(1)}, u32[]{:S(2)}, u32[]{:S(2)}) collective-permute-start(f32[2,64,128]{2,1,0:T(8,128)S(1)} %get-tuple-element.98.pair_ref), channel_id=1, source_target_pairs={{0,16},{1,17},{2,18},{3,19},{4,20},{5,21},{6,22},{7,23},{8,24},{9,... | collective-permute-start | bytes 196616 | tf_op jit(solution)/shard_map/ppermute | solution.py:358
  80.2 2.2 %collective-permute-done.20.refs_4_ = f32[2,64,128]{2,1,0:T(8,128)S(1)} collective-permute-done((f32[2,64,128]{2,1,0:T(8,128)S(1)}, f32[2,64,128]{2,1,0:T(8,128)S(1)}, u32[]{:S(2)}, u32[]{:S(2)}) %collective-permute-start.20) | collective-permute-done | bytes 65568 | tf_op jit(solution)/shard_map/ppermute | solution.py:357
  85.0 1.7 %collective-permute-start.21 = (f32[2,64,128]{2,1,0:T(8,128)S(1)}, f32[2,64,128]{2,1,0:T(8,128)S(1)}, u32[]{:S(2)}, u32[]{:S(2)}) collective-permute-start(f32[2,64,128]{2,1,0:T(8,128)S(1)} %get-tuple-element.102.pair_ref.refs_0_), channel_id=1, source_target_pairs={{16,0},{17,1},{18,2},{19,3},{20,4},{21,5},{22,6},{23,7},{24,8},{25... | collective-permute-start | bytes 196616 | tf_op jit(solution)/shard_map/ppermute | solution.py:358
  90.5 2.6 %collective-permute-done.24.refs_4_ = f32[2,64,128]{2,1,0:T(8,128)S(1)} collective-permute-done((f32[2,64,128]{2,1,0:T(8,128)S(1)}, f32[2,64,128]{2,1,0:T(8,128)S(1)}, u32[]{:S(2)}, u32[]{:S(2)}) %collective-permute-start.24) | collective-permute-done | bytes 65568 | tf_op jit(solution)/shard_map/ppermute | solution.py:357
  93.1 1.6 %collective-permute-done.23.refs_3_ = f32[2,64,128]{2,1,0:T(8,128)S(1)} collective-permute-done((f32[2,64,128]{2,1,0:T(8,128)S(1)}, f32[2,64,128]{2,1,0:T(8,128)S(1)}, u32[]{:S(2)}, u32[]{:S(2)}) %collective-permute-start.23) | collective-permute-done | bytes 65568 | tf_op jit(solution)/shard_map/ppermute | solution.py:358
  102.2 2.9 %collective-permute-done.28.refs_4_ = f32[2,64,128]{2,1,0:T(8,128)S(1)} collective-permute-done((f32[2,64,128]{2,1,0:T(8,128)S(1)}, f32[2,64,128]{2,1,0:T(8,128)S(1)}, u32[]{:S(2)}, u32[]{:S(2)}) %collective-permute-start.28) | collective-permute-done | bytes 65568 | tf_op jit(solution)/shard_map/ppermute | solution.py:357
  113.8 2.9 %collective-permute-done.32.refs_4_ = f32[2,64,128]{2,1,0:T(8,128)S(1)} collective-permute-done((f32[2,64,128]{2,1,0:T(8,128)S(1)}, f32[2,64,128]{2,1,0:T(8,128)S(1)}, u32[]{:S(2)}, u32[]{:S(2)}) %collective-permute-start.32) | collective-permute-done | bytes 65568 | tf_op jit(solution)/shard_map/ppermute | solution.py:357
  125.4 2.7 %collective-permute-done.36.refs_4_ = f32[2,64,128]{2,1,0:T(8,128)S(1)} collective-permute-done((f32[2,64,128]{2,1,0:T(8,128)S(1)}, f32[2,64,128]{2,1,0:T(8,128)S(1)}, u32[]{:S(2)}, u32[]{:S(2)}) %collective-permute-start.36) | collective-permute-done | bytes 65568 | tf_op jit(solution)/shard_map/ppermute | solution.py:357
  130.0 11.0 %all_to_all.11.sums_ref = f32[16,32,128]{2,1,0:T(8,128)S(1)} all-to-all(f32[16,32,128]{2,1,0:T(8,128)S(1)} %get-tuple-element.118), channel_id=1, replica_groups=mesh['q'=16,'c'=2,'space'=16] {'q'}, dimensions={0} | all-to-all | bytes 524288 | tf_op jit(solution)/shard_map/all_to_all | solution.py:409
  141.2 3.4 %collective-permute-start.37 = (f32[64,128]{1,0:T(8,128)S(1)}, f32[64,128]{1,0:T(8,128)S(1)}, u32[]{:S(2)}, u32[]{:S(2)}) collective-permute-start(f32[64,128]{1,0:T(8,128)S(1)} %get-tuple-element.122), channel_id=1, source_target_pairs={{0,16},{16,0},{1,17},{17,1},{2,18},{18,2},{3,19},{19,3},{4,20},{20... | collective-permute-start | bytes 98312 | tf_op jit(solution)/shard_map/ppermute | solution.py:350
  (96 shorter events, 69.0 us)
Async XLA Ops:
  2.5 3.9 %collective-permute-start = (f32[3,64,128]{2,1,0:T(8,128)S(1)}, f32[3,64,128]{2,1,0:T(8,128)S(1)}, u32[]{:S(2)}, u32[]{:S(2)}) collective-permute-start(f32[3,64,128]{2,1,0:T(8,128)S(1)} %get-tuple-element.64), channel_id=1, source_target_pairs={{0,16},{16,0},{1,17},{17,1},{2,18},{18,2},{3,19},{19,3},{4,20},{20... | collective-permute-start | bytes 294920 | tf_op jit(solution)/shard_map/ppermute | solution.py:350
  6.5 5.6 %collective-permute-start.2 = (f32[2,64,128]{2,1,0:T(8,128)S(1)}, f32[2,64,128]{2,1,0:T(8,128)S(1)}, u32[]{:S(2)}, u32[]{:S(2)}) collective-permute-start(f32[2,64,128]{2,1,0:T(8,128)S(1)} %get-tuple-element.71.pair_ref), channel_id=1, source_target_pairs={{1,16},{2,17},{3,18},{4,19},{5,20},{6,21},{7,22},{8,23},{9,24},{10... | collective-permute-start | bytes 196616 | tf_op jit(solution)/shard_map/ppermute | solution.py:357
  7.8 5.0 %collective-permute-start.1 = (f32[2,64,128]{2,1,0:T(8,128)S(1)}, f32[2,64,128]{2,1,0:T(8,128)S(1)}, u32[]{:S(2)}, u32[]{:S(2)}) collective-permute-start(f32[2,64,128]{2,1,0:T(8,128)S(1)} %get-tuple-element.71.pair_ref), channel_id=1, source_target_pairs={{0,16},{1,17},{2,18},{3,19},{4,20},{5,21},{6,22},{7,23},{8,24},{9,... | collective-permute-start | bytes 196616 | tf_op jit(solution)/shard_map/ppermute | solution.py:358
  13.2 3.0 %collective-permute-start.4 = (f32[2,64,128]{2,1,0:T(8,128)S(1)}, f32[2,64,128]{2,1,0:T(8,128)S(1)}, u32[]{:S(2)}, u32[]{:S(2)}) collective-permute-start(f32[2,64,128]{2,1,0:T(8,128)S(1)} %get-tuple-element.79.pair_ref.refs_0_), channel_id=1, source_target_pairs={{16,1},{17,2},{18,3},{19,4},{20,5},{21,6},{22,7},{23,8},{24,9},{25... | collective-permute-start | bytes 196616 | tf_op jit(solution)/shard_map/ppermute | solution.py:357
  17.0 5.6 %collective-permute-start.6 = (f32[2,64,128]{2,1,0:T(8,128)S(1)}, f32[2,64,128]{2,1,0:T(8,128)S(1)}, u32[]{:S(2)}, u32[]{:S(2)}) collective-permute-start(f32[2,64,128]{2,1,0:T(8,128)S(1)} %get-tuple-element.81.pair_ref.refs_0_), channel_id=1, source_target_pairs={{1,16},{2,17},{3,18},{4,19},{5,20},{6,21},{7,22},{8,23},{9,24},{10... | collective-permute-start | bytes 196616 | tf_op jit(solution)/shard_map/ppermute | solution.py:357
  18.3 5.8 %collective-permute-start.5 = (f32[2,64,128]{2,1,0:T(8,128)S(1)}, f32[2,64,128]{2,1,0:T(8,128)S(1)}, u32[]{:S(2)}, u32[]{:S(2)}) collective-permute-start(f32[2,64,128]{2,1,0:T(8,128)S(1)} %get-tuple-element.81.pair_ref.refs_0_), channel_id=1, source_target_pairs={{0,16},{1,17},{2,18},{3,19},{4,20},{5,21},{6,22},{7,23},{8,24},{9,... | collective-permute-start | bytes 196616 | tf_op jit(solution)/shard_map/ppermute | solution.py:358
  28.8 5.8 %collective-permute-start.10 = (f32[2,64,128]{2,1,0:T(8,128)S(1)}, f32[2,64,128]{2,1,0:T(8,128)S(1)}, u32[]{:S(2)}, u32[]{:S(2)}) collective-permute-start(f32[2,64,128]{2,1,0:T(8,128)S(1)} %get-tuple-element.85.pair_ref.refs_0_), channel_id=1, source_target_pairs={{1,16},{2,17},{3,18},{4,19},{5,20},{6,21},{7,22},{8,23},{9,24},{10... | collective-permute-start | bytes 196616 | tf_op jit(solution)/shard_map/ppermute | solution.py:357
  30.0 5.7 %collective-permute-start.9 = (f32[2,64,128]{2,1,0:T(8,128)S(1)}, f32[2,64,128]{2,1,0:T(8,128)S(1)}, u32[]{:S(2)}, u32[]{:S(2)}) collective-permute-start(f32[2,64,128]{2,1,0:T(8,128)S(1)} %get-tuple-element.85.pair_ref.refs_0_), channel_id=1, source_target_pairs={{0,16},{1,17},{2,18},{3,19},{4,20},{5,21},{6,22},{7,23},{8,24},{9,... | collective-permute-start | bytes 196616 | tf_op jit(solution)/shard_map/ppermute | solution.py:358
  40.4 5.8 %collective-permute-start.14 = (f32[2,64,128]{2,1,0:T(8,128)S(1)}, f32[2,64,128]{2,1,0:T(8,128)S(1)}, u32[]{:S(2)}, u32[]{:S(2)}) collective-permute-start(f32[2,64,128]{2,1,0:T(8,128)S(1)} %get-tuple-element.89.pair_ref.refs_0_), channel_id=1, source_target_pairs={{1,16},{2,17},{3,18},{4,19},{5,20},{6,21},{7,22},{8,23},{9,24},{10... | collective-permute-start | bytes 196616 | tf_op jit(solution)/shard_map/ppermute | solution.py:357
  41.7 5.7 %collective-permute-start.13 = (f32[2,64,128]{2,1,0:T(8,128)S(1)}, f32[2,64,128]{2,1,0:T(8,128)S(1)}, u32[]{:S(2)}, u32[]{:S(2)}) collective-permute-start(f32[2,64,128]{2,1,0:T(8,128)S(1)} %get-tuple-element.89.pair_ref.refs_0_), channel_id=1, source_target_pairs={{0,16},{1,17},{2,18},{3,19},{4,20},{5,21},{6,22},{7,23},{8,24},{9,... | collective-permute-start | bytes 196616 | tf_op jit(solution)/shard_map/ppermute | solution.py:358
  52.0 5.7 %collective-permute-start.18 = (f32[2,64,128]{2,1,0:T(8,128)S(1)}, f32[2,64,128]{2,1,0:T(8,128)S(1)}, u32[]{:S(2)}, u32[]{:S(2)}) collective-permute-start(f32[2,64,128]{2,1,0:T(8,128)S(1)} %get-tuple-element.93.pair_ref.refs_0_), channel_id=1, source_target_pairs={{1,16},{2,17},{3,18},{4,19},{5,20},{6,21},{7,22},{8,23},{9,24},{10... | collective-permute-start | bytes 196616 | tf_op jit(solution)/shard_map/ppermute | solution.py:357
  53.3 5.6 %collective-permute-start.17 = (f32[2,64,128]{2,1,0:T(8,128)S(1)}, f32[2,64,128]{2,1,0:T(8,128)S(1)}, u32[]{:S(2)}, u32[]{:S(2)}) collective-permute-start(f32[2,64,128]{2,1,0:T(8,128)S(1)} %get-tuple-element.93.pair_ref.refs_0_), channel_id=1, source_target_pairs={{0,16},{1,17},{2,18},{3,19},{4,20},{5,21},{6,22},{7,23},{8,24},{9,... | collective-permute-start | bytes 196616 | tf_op jit(solution)/shard_map/ppermute | solution.py:358
  76.9 5.6 %collective-permute-start.20 = (f32[2,64,128]{2,1,0:T(8,128)S(1)}, f32[2,64,128]{2,1,0:T(8,128)S(1)}, u32[]{:S(2)}, u32[]{:S(2)}) collective-permute-start(f32[2,64,128]{2,1,0:T(8,128)S(1)} %get-tuple-element.98.pair_ref), channel_id=1, source_target_pairs={{1,16},{2,17},{3,18},{4,19},{5,20},{6,21},{7,22},{8,23},{9,24},{10... | collective-permute-start | bytes 196616 | tf_op jit(solution)/shard_map/ppermute | solution.py:357
  78.2 5.1 %collective-permute-start.19 = (f32[2,64,128]{2,1,0:T(8,128)S(1)}, f32[2,64,128]{2,1,0:T(8,128)S(1)}, u32[]{:S(2)}, u32[]{:S(2)}) collective-permute-start(f32[2,64,128]{2,1,0:T(8,128)S(1)} %get-tuple-element.98.pair_ref), channel_id=1, source_target_pairs={{0,16},{1,17},{2,18},{3,19},{4,20},{5,21},{6,22},{7,23},{8,24},{9,... | collective-permute-start | bytes 196616 | tf_op jit(solution)/shard_map/ppermute | solution.py:358
  83.7 3.0 %collective-permute-start.22 = (f32[2,64,128]{2,1,0:T(8,128)S(1)}, f32[2,64,128]{2,1,0:T(8,128)S(1)}, u32[]{:S(2)}, u32[]{:S(2)}) collective-permute-start(f32[2,64,128]{2,1,0:T(8,128)S(1)} %get-tuple-element.102.pair_ref.refs_0_), channel_id=1, source_target_pairs={{16,1},{17,2},{18,3},{19,4},{20,5},{21,6},{22,7},{23,8},{24,9},{25... | collective-permute-start | bytes 196616 | tf_op jit(solution)/shard_map/ppermute | solution.py:357
  87.5 5.6 %collective-permute-start.24 = (f32[2,64,128]{2,1,0:T(8,128)S(1)}, f32[2,64,128]{2,1,0:T(8,128)S(1)}, u32[]{:S(2)}, u32[]{:S(2)}) collective-permute-start(f32[2,64,128]{2,1,0:T(8,128)S(1)} %get-tuple-element.104.pair_ref.refs_0_), channel_id=1, source_target_pairs={{1,16},{2,17},{3,18},{4,19},{5,20},{6,21},{7,22},{8,23},{9,24},{10... | collective-permute-start | bytes 196616 | tf_op jit(solution)/shard_map/ppermute | solution.py:357
  88.8 5.8 %collective-permute-start.23 = (f32[2,64,128]{2,1,0:T(8,128)S(1)}, f32[2,64,128]{2,1,0:T(8,128)S(1)}, u32[]{:S(2)}, u32[]{:S(2)}) collective-permute-start(f32[2,64,128]{2,1,0:T(8,128)S(1)} %get-tuple-element.104.pair_ref.refs_0_), channel_id=1, source_target_pairs={{0,16},{1,17},{2,18},{3,19},{4,20},{5,21},{6,22},{7,23},{8,24},{9,... | collective-permute-start | bytes 196616 | tf_op jit(solution)/shard_map/ppermute | solution.py:358
  99.2 5.8 %collective-permute-start.28 = (f32[2,64,128]{2,1,0:T(8,128)S(1)}, f32[2,64,128]{2,1,0:T(8,128)S(1)}, u32[]{:S(2)}, u32[]{:S(2)}) collective-permute-start(f32[2,64,128]{2,1,0:T(8,128)S(1)} %get-tuple-element.108.pair_ref.refs_0_), channel_id=1, source_target_pairs={{1,16},{2,17},{3,18},{4,19},{5,20},{6,21},{7,22},{8,23},{9,24},{10... | collective-permute-start | bytes 196616 | tf_op jit(solution)/shard_map/ppermute | solution.py:357
  100.5 5.7 %collective-permute-start.27 = (f32[2,64,128]{2,1,0:T(8,128)S(1)}, f32[2,64,128]{2,1,0:T(8,128)S(1)}, u32[]{:S(2)}, u32[]{:S(2)}) collective-permute-start(f32[2,64,128]{2,1,0:T(8,128)S(1)} %get-tuple-element.108.pair_ref.refs_0_), channel_id=1, source_target_pairs={{0,16},{1,17},{2,18},{3,19},{4,20},{5,21},{6,22},{7,23},{8,24},{9,... | collective-permute-start | bytes 196616 | tf_op jit(solution)/shard_map/ppermute | solution.py:358
  110.9 5.8 %collective-permute-start.32 = (f32[2,64,128]{2,1,0:T(8,128)S(1)}, f32[2,64,128]{2,1,0:T(8,128)S(1)}, u32[]{:S(2)}, u32[]{:S(2)}) collective-permute-start(f32[2,64,128]{2,1,0:T(8,128)S(1)} %get-tuple-element.112.pair_ref.refs_0_), channel_id=1, source_target_pairs={{1,16},{2,17},{3,18},{4,19},{5,20},{6,21},{7,22},{8,23},{9,24},{10... | collective-permute-start | bytes 196616 | tf_op jit(solution)/shard_map/ppermute | solution.py:357
  112.2 5.7 %collective-permute-start.31 = (f32[2,64,128]{2,1,0:T(8,128)S(1)}, f32[2,64,128]{2,1,0:T(8,128)S(1)}, u32[]{:S(2)}, u32[]{:S(2)}) collective-permute-start(f32[2,64,128]{2,1,0:T(8,128)S(1)} %get-tuple-element.112.pair_ref.refs_0_), channel_id=1, source_target_pairs={{0,16},{1,17},{2,18},{3,19},{4,20},{5,21},{6,22},{7,23},{8,24},{9,... | collective-permute-start | bytes 196616 | tf_op jit(solution)/shard_map/ppermute | solution.py:358
  122.5 5.7 %collective-permute-start.36 = (f32[2,64,128]{2,1,0:T(8,128)S(1)}, f32[2,64,128]{2,1,0:T(8,128)S(1)}, u32[]{:S(2)}, u32[]{:S(2)}) collective-permute-start(f32[2,64,128]{2,1,0:T(8,128)S(1)} %get-tuple-element.116.pair_ref.refs_0_), channel_id=1, source_target_pairs={{1,16},{2,17},{3,18},{4,19},{5,20},{6,21},{7,22},{8,23},{9,24},{10... | collective-permute-start | bytes 196616 | tf_op jit(solution)/shard_map/ppermute | solution.py:357
  123.8 5.6 %collective-permute-start.35 = (f32[2,64,128]{2,1,0:T(8,128)S(1)}, f32[2,64,128]{2,1,0:T(8,128)S(1)}, u32[]{:S(2)}, u32[]{:S(2)}) collective-permute-start(f32[2,64,128]{2,1,0:T(8,128)S(1)} %get-tuple-element.116.pair_ref.refs_0_), channel_id=1, source_target_pairs={{0,16},{1,17},{2,18},{3,19},{4,20},{5,21},{6,22},{7,23},{8,24},{9,... | collective-permute-start | bytes 196616 | tf_op jit(solution)/shard_map/ppermute | solution.py:358
  141.2 4.2 %collective-permute-start.37 = (f32[64,128]{1,0:T(8,128)S(1)}, f32[64,128]{1,0:T(8,128)S(1)}, u32[]{:S(2)}, u32[]{:S(2)}) collective-permute-start(f32[64,128]{1,0:T(8,128)S(1)} %get-tuple-element.122), channel_id=1, source_target_pairs={{0,16},{16,0},{1,17},{17,1},{2,18},{18,2},{3,19},{19,3},{4,20},{20... | collective-permute-start | bytes 98312 | tf_op jit(solution)/shard_map/ppermute | solution.py:350
  (14 other events, 34.0 us)

commit v4 on v3

--- a/solution.py
+++ b/solution.py
@@ -13,8 +13,8 @@
 HALF = 64
 STEPS = 4
 STAGES = 2 * STEPS
-HIGHEST = lax.Precision.HIGHEST
 F32 = jnp.float32
+BF16 = jnp.bfloat16
 FIELD = (VALUES, LANES)
 
 
@@ -79,8 +79,16 @@
     return sums[0] + sums[1]
 
 
-def product(left, right):
-    return jnp.dot(left, right, precision=HIGHEST, preferred_element_type=F32)
+def halves(x):
+    high = x.astype(BF16)
+    return high, (x - high.astype(F32)).astype(BF16)
+
+
+def product(faces, layers):
+    width = layers.shape[1]
+    parts = jnp.dot(faces, jnp.concatenate(halves(layers), axis=1), preferred_element_type=F32)
+    upper, lower = parts[:VALUES], parts[VALUES:]
+    return upper[:, :width] + ((upper[:, width:] + lower[:, :width]) + lower[:, width:])
 
 
 def own_faces(field, index, valid, faces):
@@ -148,10 +156,15 @@
     lane = lax.broadcasted_iota(jnp.int32, (8, LANES), 1)
     spot = columns(place, jnp.clip(local, 0, LANES - 1))
     index_ref[...] = jnp.bitwise_and(spot, HALF - 1) + jnp.where(lane < HALF, 0, HALF)
-    for f in range(4):
-        faces_ref[:, f * VALUES : (f + 1) * VALUES] = blocks_ref[f]
-    faces_ref[:, 4 * VALUES : 5 * VALUES] = jnp.where(core == 0, blocks_ref[4], blocks_ref[5])
-    faces_ref[:, 5 * VALUES : 6 * VALUES] = jnp.where(core == 0, blocks_ref[5], blocks_ref[4])
+    blocks = [blocks_ref[f] for f in range(4)]
+    blocks += [
+        jnp.where(core == 0, blocks_ref[4], blocks_ref[5]),
+        jnp.where(core == 0, blocks_ref[5], blocks_ref[4]),
+    ]
+    for f, block in enumerate(blocks):
+        high, low = halves(block)
+        faces_ref[:VALUES, f * VALUES : (f + 1) * VALUES] = high
+        faces_ref[VALUES:, f * VALUES : (f + 1) * VALUES] = low
     for j in range(VALUES):
         table_ref[j] = columns(inverse_ref[:, j, :], mine)
 
@@ -167,7 +180,7 @@
 
 
 def first_kernel(
-    own_ref, got_ref, start_ref, table_ref, sources_ref, gain_ref, pair_ref, right_ref, scratch
+    lead, own_ref, got_ref, start_ref, table_ref, sources_ref, gain_ref, field_ref, right_ref, scratch
 ):
     core = lax.axis_index("c")
     low = low_half()
@@ -187,34 +200,32 @@
     first = jnp.logical_and(low, lax.axis_index("q") == 0)
     right = jnp.where(first, start_ref[...], 0.0) + sources_ref[0]
     right_ref[...] = right
-    begin(right, table_ref, pair_ref, scratch)
-
-
-def begin(right, table_ref, pair_ref, scratch):
-    @pl.when(lax.axis_index("c") == 0)
+    begin(lead, right, table_ref, field_ref, scratch)
+
+
+def begin(lead, right, table_ref, field_ref, scratch):
+    @pl.when(lax.axis_index("c") == lead)
     def _field():
-        pair_ref[0] = jnp.zeros(FIELD, F32)
-        pair_ref[1] = apply_inverse(table_ref, scratch, right)
-
-    @pl.when(lax.axis_index("c") != 0)
+        field_ref[...] = apply_inverse(table_ref, scratch, right)
+
+    @pl.when(lax.axis_index("c") != lead)
     def _later():
-        pair_ref[...] = jnp.zeros((2,) + FIELD, F32)
-
-
-def late_kernel(pair_ref, right_ref, index_ref, valid_ref, faces_ref, table_ref, pair_out, ahead_ref,
-                scratch):
-    core = lax.axis_index("c")
-
-    @pl.when(core == 1)
+        field_ref[...] = jnp.zeros(FIELD, F32)
+
+
+def late_kernel(lead, field_ref, right_ref, index_ref, valid_ref, faces_ref, table_ref, field_out,
+                ahead_ref, scratch):
+    core = lax.axis_index("c")
+
+    @pl.when(core != lead)
     def _run():
         field = apply_inverse(table_ref, scratch, right_ref[...])
-        pair_out[0] = pair_ref[0]
-        pair_out[1] = field
+        field_out[...] = field
         ahead_ref[...] = own_faces(field, index_ref[...], valid_ref[...], faces_ref[...])
 
-    @pl.when(core == 0)
+    @pl.when(core == lead)
     def _keep():
-        pair_out[...] = pair_ref[...]
+        field_out[...] = field_ref[...]
 
 
 def ahead_kernel(active, pair_ref, index_ref, valid_ref, faces_ref, ahead_ref, _):
@@ -223,33 +234,51 @@
         ahead_ref[...] = own_faces(pair_ref[1], index_ref[...], valid_ref[...], faces_ref[...])
 
 
-def advance(plan, refs, sourced, scratch):
-    (pair_ref, right_ref, ahead_ref, near_ref, far_ref, index_ref, valid_ref, faces_ref, table_ref,
-     sources_ref, pair_out, right_out) = refs
-    active, stages = plan
+def across_faces(faces, far, near):
+    return product(faces[:, 4 * VALUES :], jnp.concatenate([far, near], axis=0))
+
+
+def open_kernel(lead, field_ref, right_ref, ahead_ref, near_ref, far_ref, faces_ref, table_ref,
+                pair_out, scratch):
+    core = lax.axis_index("c")
+
+    @pl.when(core != lead)
+    def _run():
+        summed = ahead_ref[...] + across_faces(faces_ref[...], far_ref[...], near_ref[...])
+        pair_out[0] = field_ref[...]
+        pair_out[1] = apply_inverse(table_ref, scratch, right_ref[...] - summed)
+
+    @pl.when(core == lead)
+    def _keep():
+        pair_out[0] = jnp.zeros(FIELD, F32)
+        pair_out[1] = field_ref[...]
+
+
+def advance_kernel(stage, active, sourced, pair_ref, right_ref, ahead_ref, near_ref, far_ref,
+                   index_ref, valid_ref, faces_ref, table_ref, sources_ref, pair_out, right_out,
+                   scratch):
     core = lax.axis_index("c")
 
     @pl.when(core == active)
     def _run():
         index, valid, faces = index_ref[...], valid_ref[...], faces_ref[...]
-        layers = [
-            jnp.concatenate([ref[slot] for _, slot in stages], axis=1) for ref in (far_ref, near_ref)
-        ]
-        across = product(faces[:, 4 * VALUES :], jnp.concatenate(layers, axis=0))
-        field = pair_ref[1]
+        far, near = (jnp.concatenate([ref[0], ref[1]], axis=1) for ref in (far_ref, near_ref))
+        across = across_faces(faces, far, near)
         right = right_ref[...]
-        summed = ahead_ref[...]
-        for place, (stage, _) in enumerate(stages):
-            pair_out[0] = field
-            if place > 0:
-                summed = own_faces(field, index, valid, faces)
-            summed = summed + across[:, place * LANES : (place + 1) * LANES]
+
+        def taken(summed, right, stage):
             field = apply_inverse(table_ref, scratch, right - summed)
-            if stage % 2 == 1 and stage < STAGES - 1:
+            if stage % 2 == 1:
                 right = field
                 if sourced:
                     right = right + sources_ref[(stage + 1) // 2]
                 field = apply_inverse(table_ref, scratch, right)
+            return field, right
+
+        field, right = taken(ahead_ref[...] + across[:, :LANES], right, stage)
+        pair_out[0] = field
+        summed = own_faces(field, index, valid, faces) + across[:, LANES:]
+        field, right = taken(summed, right, stage + 1)
         pair_out[1] = field
         right_out[...] = right
 
@@ -259,18 +288,51 @@
         right_out[...] = right_ref[...]
 
 
-def advance_kernel(plan, sourced, *refs):
-    advance(plan, refs[:-1], sourced, refs[-1])
-
-
-def ends_kernel(plan, sourced, count, *refs):
+def last_kernel(lead, pair_ref, right_ref, ahead_ref, near_ref, far_ref, faces_ref, table_ref,
+                field_out, scratch):
+    core = lax.axis_index("c")
+
+    @pl.when(core == lead)
+    def _run():
+        summed = ahead_ref[...] + across_faces(faces_ref[...], far_ref[0], near_ref[0])
+        field_out[...] = apply_inverse(table_ref, scratch, right_ref[...] - summed)
+
+    @pl.when(core != lead)
+    def _keep():
+        field_out[...] = pair_ref[1]
+
+
+def tail_kernel(lead, field_ref, right_ref, near_ref, far_ref, index_ref, valid_ref, faces_ref,
+                table_ref, out_ref, scratch):
+    core = lax.axis_index("c")
+    out_ref[...] = own_faces(field_ref[...], index_ref[...], valid_ref[...], faces_ref[...])
+
+    @pl.when(core == lead)
+    def _run():
+        summed = out_ref[...] + across_faces(faces_ref[...], far_ref[1], near_ref[1])
+        out_ref[...] = apply_inverse(table_ref, scratch, right_ref[...] - summed)
+
+
+def ends_kernel(lead, sourced, count, *refs):
     if sourced:
-        (*inner, gain_ref, residual_ref, chunk_ref, scratch, pair_out, right_out) = refs
+        (right_ref, tail_ref, near_ref, far_ref, faces_ref, table_ref, gain_ref, residual_ref,
+         chunk_ref, scratch, end_ref) = refs
     else:
-        (*inner, gain_ref, shift_ref, residual_ref, chunk_ref, scratch, pair_out, right_out) = refs
-    advance(plan, (*inner, pair_out, right_out), sourced, scratch)
+        (right_ref, tail_ref, near_ref, far_ref, faces_ref, table_ref, gain_ref, shift_ref,
+         residual_ref, chunk_ref, scratch, end_ref) = refs
+    core = lax.axis_index("c")
+
+    @pl.when(core != lead)
+    def _run():
+        summed = tail_ref[...] + across_faces(faces_ref[...], far_ref[...], near_ref[...])
+        end_ref[...] = apply_inverse(table_ref, scratch, right_ref[...] - summed)
+
+    @pl.when(core == lead)
+    def _keep():
+        end_ref[...] = tail_ref[...]
+
     gain = gain_ref[...]
-    residual = pair_out[1]
+    residual = end_ref[...]
     if not sourced:
         residual = residual - gain * shift_ref[...]
     residual_ref[...] = residual
@@ -299,14 +361,13 @@
 
 
 def restart_kernel(
-    count, sums_ref, end_ref, gain_ref, table_ref, shift_ref, coarse_ref, pair_ref,
-    scratch
+    lead, count, sums_ref, end_ref, gain_ref, table_ref, shift_ref, coarse_ref, field_ref, scratch
 ):
     gain, end = gain_ref[...], end_ref[...]
     shift = shifted(scanned(count, sums_ref, sums_ref), gain, end)
     shift_ref[...] = shift
     coarse_ref[...] = gain * shift + end
-    begin(shift, table_ref, pair_ref, scratch)
+    begin(lead, shift, table_ref, field_ref, scratch)
 
 
 def finish_kernel(count, sums_ref, gains_ref, residual_ref, gain_ref, coarse_ref, end_ref, out_ref, _):
@@ -338,13 +399,6 @@
     residual_out[0] = columns(residual, place)
 
 
-def plans():
-    yield 1, [(0, 1)]
-    for half in range(2, STAGES + 1):
-        yield half % 2, [(half - 2, 0), (half - 1, 1)]
-    yield (STAGES + 1) % 2, [(STAGES - 1, 0)]
-
-
 def body(count, depth, initial_state, forcing, coarse_gain, block_inverse, face_blocks, neighbor, send_rows):
     def swap_cores(x):
         return lax.ppermute(x, "c", [(0, 1), (1, 0)])
@@ -371,51 +425,68 @@
     index, valid, place, faces, table = call(
         tables_kernel, "tables",
         [((8, LANES), jnp.int32), ((8, LANES), F32), ((8, LANES), jnp.int32),
-         ((VALUES, 6 * VALUES), F32), ((VALUES,) + FIELD, F32)],
+         ((2 * VALUES, 6 * VALUES), BF16), ((VALUES,) + FIELD, F32)],
         *map(vmem, raw),
     )
     index, valid, place, faces, table = map(vmem, (index, valid, place, faces, table))
-    sources, gain, pair, right = call(
-        first_kernel, "first", [((STEPS,) + FIELD, F32), field, pair_shape, field],
+    operator = (index, valid, faces, table)
+    sources, gain, begun, right = call(
+        functools.partial(first_kernel, 0), "first", [((STEPS,) + FIELD, F32), field, field, field],
         vmem(own), vmem(got), vmem(start), table,
     )
     sources, gain = vmem(sources), vmem(gain)
-    half_phases = list(plans())
-
-    def evolve(pair, right, sourced, shift):
-        for number, plan in enumerate(half_phases):
-            pair, right = vmem(pair), vmem(right)
-            near, far = halo(pair, plan[0])
-            if number == 0:
-                pair, ahead = call(
-                    late_kernel, "late", [pair_shape, field], pair, right, index, valid, faces, table
+
+    def evolve(lead, now, right, sourced, shift):
+        other = 1 - lead
+        right = vmem(right)
+        now = vmem(now)
+        near, far = halo(now, other)
+        now, ahead = call(
+            functools.partial(late_kernel, lead), "late", [field, field], now, right, *operator
+        )
+        (pair,) = call(
+            functools.partial(open_kernel, lead), "open", [pair_shape],
+            vmem(now), right, vmem(ahead), near, far, faces, table,
+        )
+        for stage in range(STAGES - 1):
+            active = (lead, other)[stage % 2]
+            pair = vmem(pair)
+            near, far = halo(pair, active)
+            (ahead,) = call(
+                functools.partial(ahead_kernel, active), "ahead", [field], pair, index, valid, faces
+            )
+            ahead = vmem(ahead)
+            if stage < STAGES - 2:
+                pair, right = call(
+                    functools.partial(advance_kernel, stage, active, sourced), "advance",
+                    [pair_shape, field], pair, right, ahead, near, far, *operator, sources,
                 )
-            else:
-                (ahead,) = call(
-                    functools.partial(ahead_kernel, plan[0]), "ahead", [field], pair, index, valid,
-                    faces,
-                )
-            args = (vmem(pair), right, vmem(ahead), near, far, index, valid, faces, table, sources)
-            if number < len(half_phases) - 1:
-                pair, right = call(
-                    functools.partial(advance_kernel, plan, sourced), "advance",
-                    [pair_shape, field], *args,
-                )
+                right = vmem(right)
+        (now,) = call(
+            functools.partial(last_kernel, lead), "last", [field],
+            pair, right, ahead, near, far, faces, table,
+        )
+        now = vmem(now)
+        tail_halo = near, far
+        near, far = halo(now, other)
+        (tail,) = call(
+            functools.partial(tail_kernel, lead), "tail", [field], now, right, *tail_halo, *operator
+        )
+        rows = VALUES if sourced else VALUES // 2
         residual, chunk = call(
-            functools.partial(ends_kernel, plan, sourced, count), "ends",
-            [field, ((count, VALUES if sourced else VALUES // 2, LANES), F32)], *args, gain,
-            *shift, scratch=(FIELD, (2,) + FIELD, FIELD),
+            functools.partial(ends_kernel, lead, sourced, count), "ends",
+            [field, ((count, rows, LANES), F32)],
+            right, vmem(tail), near, far, faces, table, gain, *shift, scratch=(FIELD, FIELD),
         )
         return vmem(residual), vmem(lax.all_to_all(chunk, "q", 0, 0))
 
-    end, sums = evolve(pair, right, True, ())
-    shift, coarse, pair = call(
-        functools.partial(restart_kernel, count), "restart", [field, field, pair_shape],
-        sums, end, gain, table,
+    end, gains = evolve(0, begun, right, True, ())
+    shift, coarse, begun = call(
+        functools.partial(restart_kernel, 0, count), "restart", [field, field, field],
+        gains, end, gain, table,
     )
     shift = vmem(shift)
-    gains = sums
-    residual, sums = evolve(pair, shift, False, (shift,))
+    residual, sums = evolve(0, begun, shift, False, (shift,))
     end, sent = call(
         functools.partial(finish_kernel, count), "finish", [field, field],
         sums, gains, residual, gain, vmem(coarse),

time: 147 us -> 144 us (0.980)
  Pallas kernels: 17 us -> 14.7 us
    pallas_call x42, Pallas kernels: 17 us -> 14.7 us  [call(): pl.pallas_call(kernel, out_shape=shapes, in_specs=[pl.BlockSpec(memory_sp...]
  transfers between devices with their start and end apart: 38 -> 38, of which waited for: 29 -> 29; matrix products, arithmetic and copies ran while one was open for 0% -> 0% of each run, Pallas kernels for 4% -> 3%
where the time goes in v4:
time: 144 us; the launch traced here: 143 us
  starting transfers between devices  53.4 us (37%)
  waiting for transfers between devices  46.2 us (32%)
  blocking collectives  27.7 us (19%)
  Pallas kernels  14.7 us (10%)
    all_to_all x2, blocking collectives, evolve(): return (vmem(residual), vmem(lax.all_to_all(chunk, 'q', 0, 0)))  27.7 us
    ppermute x18, waiting for transfers between devices, halo(): far = lax.ppermute(x, ('c', 'space'), across)  25.6 us
    ppermute x18, starting transfers between devices, halo(): near = lax.ppermute(x, 'c', [(1 - to, to)])  24.2 us
    ppermute x18, starting transfers between devices, halo(): far = lax.ppermute(x, ('c', 'space'), across)  23.2 us
    ppermute x18, waiting for transfers between devices, halo(): near = lax.ppermute(x, 'c', [(1 - to, to)])  19.7 us
    pallas_call x42, Pallas kernels, call(): pl.pallas_call(kernel, out_shape=shapes, in_specs=[pl.BlockSpec(memory_sp...  14.7 us
    ppermute x2, starting transfers between devices, swap_cores(): return lax.ppermute(x, 'c', [(0, 1), (1, 0)])  5.98 us
  transfers between devices with their start and end apart: 38, of which 29 were waited for; matrix products, arithmetic and copies ran while one was open for 0% of the time, Pallas kernels for 3%

profile of v4, /device:TPU:385, one launch (start us, length us, event | category | flops | bytes accessed | tf_op | source)
XLA Modules:
  0.0 143.3 jit_solution(6378582558570574387)
XLA Ops:
  0.6 1.9 %share.1 = (f32[5,64,128]{2,1,0:T(8,128)S(1)}, f32[3,64,128]{2,1,0:T(8,128)S(1)}, f32[64,128]{1,0:T(8,128)S(1)}, s32[2,64]{1,0:T(2,128)S(1)}, s32[6,128]{1,0:T(8...) custom-call(s32[2,64]{1,0:T(2,128)} %send_any.1, f32[4,64,128]{2,1,0:T(8,128)} %forcing_any.1, ...), custom_call_target="tpu_custom_call" | custom-call | flops 4194304 | bytes 1048576 | tf_op jit(solution)/shard_map/share/pallas_call | solution.py:38
  2.5 2.6 %collective-permute-start = (f32[3,64,128]{2,1,0:T(8,128)S(1)}, f32[3,64,128]{2,1,0:T(8,128)S(1)}, u32[]{:S(2)}, u32[]{:S(2)}) collective-permute-start(f32[3,64,128]{2,1,0:T(8,128)S(1)} %get-tuple-element.56), channel_id=1, source_target_pairs={{0,16},{16,0},{1,17},{17,1},{2,18},{18,2},{3,19},{19,3},{4,20},{20... | collective-permute-start | bytes 294920 | tf_op jit(solution)/shard_map/ppermute | solution.py:404
  9.6 2.2 %collective-permute-done.2.far_ref = f32[64,128]{1,0:T(8,128)S(1)} collective-permute-done((f32[64,128]{1,0:T(8,128)S(1)}, f32[64,128]{1,0:T(8,128)S(1)}, u32[]{:S(2)}, u32[]{:S(2)}) %collective-permute-start.2) | collective-permute-done | bytes 32800 | tf_op jit(solution)/shard_map/ppermute | solution.py:411
  13.0 1.3 collective-permute-start.4
  14.3 1.8 %collective-permute-start.3 = (f32[2,64,128]{2,1,0:T(8,128)S(1)}, f32[2,64,128]{2,1,0:T(8,128)S(1)}, u32[]{:S(2)}, u32[]{:S(2)}) collective-permute-start(f32[2,64,128]{2,1,0:T(8,128)S(1)} %open.2.pair_ref), channel_id=1, source_target_pairs={{16,0},{17,1},{18,2},{19,3},{20,4},{21,5},{22,6},{23,7},{24,8},{25... | collective-permute-start | bytes 196616 | tf_op jit(solution)/shard_map/ppermute | solution.py:412
  19.8 2.7 %collective-permute-done.6.far_ref = f32[2,64,128]{2,1,0:T(8,128)S(1)} collective-permute-done((f32[2,64,128]{2,1,0:T(8,128)S(1)}, f32[2,64,128]{2,1,0:T(8,128)S(1)}, u32[]{:S(2)}, u32[]{:S(2)}) %collective-permute-start.6) | collective-permute-done | bytes 65568 | tf_op jit(solution)/shard_map/ppermute | solution.py:411
  22.5 1.4 collective-permute-done.5.near_ref
  26.1 1.3 collective-permute-start.7
  31.2 2.8 %collective-permute-done.10.far_ref = f32[2,64,128]{2,1,0:T(8,128)S(1)} collective-permute-done((f32[2,64,128]{2,1,0:T(8,128)S(1)}, f32[2,64,128]{2,1,0:T(8,128)S(1)}, u32[]{:S(2)}, u32[]{:S(2)}) %collective-permute-start.10) | collective-permute-done | bytes 65568 | tf_op jit(solution)/shard_map/ppermute | solution.py:411
  42.4 2.8 %collective-permute-done.14.far_ref = f32[2,64,128]{2,1,0:T(8,128)S(1)} collective-permute-done((f32[2,64,128]{2,1,0:T(8,128)S(1)}, f32[2,64,128]{2,1,0:T(8,128)S(1)}, u32[]{:S(2)}, u32[]{:S(2)}) %collective-permute-start.14) | collective-permute-done | bytes 65568 | tf_op jit(solution)/shard_map/ppermute | solution.py:411
  53.7 2.4 %collective-permute-done.18.refs_3_ = f32[64,128]{1,0:T(8,128)S(1)} collective-permute-done((f32[64,128]{1,0:T(8,128)S(1)}, f32[64,128]{1,0:T(8,128)S(1)}, u32[]{:S(2)}, u32[]{:S(2)}) %collective-permute-start.18) | collective-permute-done | bytes 32800 | tf_op jit(solution)/shard_map/ppermute | solution.py:411
  56.0 1.5 %collective-permute-done.17.refs_2_ = f32[64,128]{1,0:T(8,128)S(1)} collective-permute-done((f32[64,128]{1,0:T(8,128)S(1)}, f32[64,128]{1,0:T(8,128)S(1)}, u32[]{:S(2)}, u32[]{:S(2)}) %collective-permute-start.17) | collective-permute-done | bytes 32800 | tf_op jit(solution)/shard_map/ppermute | solution.py:412
  58.1 16.8 %all_to_all.10.sums_ref.gains_ref = f32[16,64,128]{2,1,0:T(8,128)S(1)} all-to-all(f32[16,64,128]{2,1,0:T(8,128)S(1)} %get-tuple-element.84), channel_id=1, replica_groups=mesh['q'=16,'c'=2,'space'=16] {'q'}, dimensions={0} | all-to-all | bytes 1048576 | tf_op jit(solution)/shard_map/all_to_all | solution.py:481
  78.1 2.2 %collective-permute-done.20.far_ref = f32[64,128]{1,0:T(8,128)S(1)} collective-permute-done((f32[64,128]{1,0:T(8,128)S(1)}, f32[64,128]{1,0:T(8,128)S(1)}, u32[]{:S(2)}, u32[]{:S(2)}) %collective-permute-start.20) | collective-permute-done | bytes 32800 | tf_op jit(solution)/shard_map/ppermute | solution.py:411
  80.3 1.3 collective-permute-done.19.near_ref
  83.2 1.8 %collective-permute-start.21 = (f32[2,64,128]{2,1,0:T(8,128)S(1)}, f32[2,64,128]{2,1,0:T(8,128)S(1)}, u32[]{:S(2)}, u32[]{:S(2)}) collective-permute-start(f32[2,64,128]{2,1,0:T(8,128)S(1)} %open.3.pair_ref), channel_id=1, source_target_pairs={{16,0},{17,1},{18,2},{19,3},{20,4},{21,5},{22,6},{23,7},{24,8},{25... | collective-permute-start | bytes 196616 | tf_op jit(solution)/shard_map/ppermute | solution.py:412
  88.7 2.7 %collective-permute-done.24.far_ref = f32[2,64,128]{2,1,0:T(8,128)S(1)} collective-permute-done((f32[2,64,128]{2,1,0:T(8,128)S(1)}, f32[2,64,128]{2,1,0:T(8,128)S(1)}, u32[]{:S(2)}, u32[]{:S(2)}) %collective-permute-start.24) | collective-permute-done | bytes 65568 | tf_op jit(solution)/shard_map/ppermute | solution.py:411
  91.5 1.4 collective-permute-done.23.near_ref
  100.1 2.8 %collective-permute-done.28.far_ref = f32[2,64,128]{2,1,0:T(8,128)S(1)} collective-permute-done((f32[2,64,128]{2,1,0:T(8,128)S(1)}, f32[2,64,128]{2,1,0:T(8,128)S(1)}, u32[]{:S(2)}, u32[]{:S(2)}) %collective-permute-start.28) | collective-permute-done | bytes 65568 | tf_op jit(solution)/shard_map/ppermute | solution.py:411
  111.3 2.8 %collective-permute-done.32.far_ref = f32[2,64,128]{2,1,0:T(8,128)S(1)} collective-permute-done((f32[2,64,128]{2,1,0:T(8,128)S(1)}, f32[2,64,128]{2,1,0:T(8,128)S(1)}, u32[]{:S(2)}, u32[]{:S(2)}) %collective-permute-start.32) | collective-permute-done | bytes 65568 | tf_op jit(solution)/shard_map/ppermute | solution.py:411
  122.6 2.4 %collective-permute-done.36.refs_3_ = f32[64,128]{1,0:T(8,128)S(1)} collective-permute-done((f32[64,128]{1,0:T(8,128)S(1)}, f32[64,128]{1,0:T(8,128)S(1)}, u32[]{:S(2)}, u32[]{:S(2)}) %collective-permute-start.36) | collective-permute-done | bytes 32800 | tf_op jit(solution)/shard_map/ppermute | solution.py:411
  125.0 1.5 %collective-permute-done.35.refs_2_ = f32[64,128]{1,0:T(8,128)S(1)} collective-permute-done((f32[64,128]{1,0:T(8,128)S(1)}, f32[64,128]{1,0:T(8,128)S(1)}, u32[]{:S(2)}, u32[]{:S(2)}) %collective-permute-start.35) | collective-permute-done | bytes 32800 | tf_op jit(solution)/shard_map/ppermute | solution.py:412
  127.0 11.0 %all_to_all.11.sums_ref = f32[16,32,128]{2,1,0:T(8,128)S(1)} all-to-all(f32[16,32,128]{2,1,0:T(8,128)S(1)} %get-tuple-element.102), channel_id=1, replica_groups=mesh['q'=16,'c'=2,'space'=16] {'q'}, dimensions={0} | all-to-all | bytes 524288 | tf_op jit(solution)/shard_map/all_to_all | solution.py:481
  138.3 3.4 %collective-permute-start.37 = (f32[64,128]{1,0:T(8,128)S(1)}, f32[64,128]{1,0:T(8,128)S(1)}, u32[]{:S(2)}, u32[]{:S(2)}) collective-permute-start(f32[64,128]{1,0:T(8,128)S(1)} %get-tuple-element.106), channel_id=1, source_target_pairs={{0,16},{16,0},{1,17},{17,1},{2,18},{18,2},{3,19},{19,3},{4,20},{20... | collective-permute-start | bytes 98312 | tf_op jit(solution)/shard_map/ppermute | solution.py:404
  (96 shorter events, 67.6 us)
Async XLA Ops:
  2.5 3.8 %collective-permute-start = (f32[3,64,128]{2,1,0:T(8,128)S(1)}, f32[3,64,128]{2,1,0:T(8,128)S(1)}, u32[]{:S(2)}, u32[]{:S(2)}) collective-permute-start(f32[3,64,128]{2,1,0:T(8,128)S(1)} %get-tuple-element.56), channel_id=1, source_target_pairs={{0,16},{16,0},{1,17},{17,1},{2,18},{18,2},{3,19},{19,3},{4,20},{20... | collective-permute-start | bytes 294920 | tf_op jit(solution)/shard_map/ppermute | solution.py:404
  6.5 5.2 %collective-permute-start.2 = (f32[64,128]{1,0:T(8,128)S(1)}, f32[64,128]{1,0:T(8,128)S(1)}, u32[]{:S(2)}, u32[]{:S(2)}) collective-permute-start(f32[64,128]{1,0:T(8,128)S(1)} %get-tuple-element.63.field_ref), channel_id=1, source_target_pairs={{1,16},{2,17},{3,18},{4,19},{5,20},{6,21},{7,22},{8,23},{9,24},{10... | collective-permute-start | bytes 98312 | tf_op jit(solution)/shard_map/ppermute | solution.py:411
  7.8 4.9 %collective-permute-start.1 = (f32[64,128]{1,0:T(8,128)S(1)}, f32[64,128]{1,0:T(8,128)S(1)}, u32[]{:S(2)}, u32[]{:S(2)}) collective-permute-start(f32[64,128]{1,0:T(8,128)S(1)} %get-tuple-element.63.field_ref), channel_id=1, source_target_pairs={{0,16},{1,17},{2,18},{3,19},{4,20},{5,21},{6,22},{7,23},{8,24},{9,... | collective-permute-start | bytes 98312 | tf_op jit(solution)/shard_map/ppermute | solution.py:412
  13.0 3.1 %collective-permute-start.4 = (f32[2,64,128]{2,1,0:T(8,128)S(1)}, f32[2,64,128]{2,1,0:T(8,128)S(1)}, u32[]{:S(2)}, u32[]{:S(2)}) collective-permute-start(f32[2,64,128]{2,1,0:T(8,128)S(1)} %open.2.pair_ref), channel_id=1, source_target_pairs={{16,1},{17,2},{18,3},{19,4},{20,5},{21,6},{22,7},{23,8},{24,9},{25... | collective-permute-start | bytes 196616 | tf_op jit(solution)/shard_map/ppermute | solution.py:411
  17.0 5.6 %collective-permute-start.6 = (f32[2,64,128]{2,1,0:T(8,128)S(1)}, f32[2,64,128]{2,1,0:T(8,128)S(1)}, u32[]{:S(2)}, u32[]{:S(2)}) collective-permute-start(f32[2,64,128]{2,1,0:T(8,128)S(1)} %get-tuple-element.71.pair_ref), channel_id=1, source_target_pairs={{1,16},{2,17},{3,18},{4,19},{5,20},{6,21},{7,22},{8,23},{9,24},{10... | collective-permute-start | bytes 196616 | tf_op jit(solution)/shard_map/ppermute | solution.py:411
  18.3 5.7 %collective-permute-start.5 = (f32[2,64,128]{2,1,0:T(8,128)S(1)}, f32[2,64,128]{2,1,0:T(8,128)S(1)}, u32[]{:S(2)}, u32[]{:S(2)}) collective-permute-start(f32[2,64,128]{2,1,0:T(8,128)S(1)} %get-tuple-element.71.pair_ref), channel_id=1, source_target_pairs={{0,16},{1,17},{2,18},{3,19},{4,20},{5,21},{6,22},{7,23},{8,24},{9,... | collective-permute-start | bytes 196616 | tf_op jit(solution)/shard_map/ppermute | solution.py:412
  28.3 5.6 %collective-permute-start.10 = (f32[2,64,128]{2,1,0:T(8,128)S(1)}, f32[2,64,128]{2,1,0:T(8,128)S(1)}, u32[]{:S(2)}, u32[]{:S(2)}) collective-permute-start(f32[2,64,128]{2,1,0:T(8,128)S(1)} %get-tuple-element.75.pair_ref), channel_id=1, source_target_pairs={{1,16},{2,17},{3,18},{4,19},{5,20},{6,21},{7,22},{8,23},{9,24},{10... | collective-permute-start | bytes 196616 | tf_op jit(solution)/shard_map/ppermute | solution.py:411
  29.6 5.6 %collective-permute-start.9 = (f32[2,64,128]{2,1,0:T(8,128)S(1)}, f32[2,64,128]{2,1,0:T(8,128)S(1)}, u32[]{:S(2)}, u32[]{:S(2)}) collective-permute-start(f32[2,64,128]{2,1,0:T(8,128)S(1)} %get-tuple-element.75.pair_ref), channel_id=1, source_target_pairs={{0,16},{1,17},{2,18},{3,19},{4,20},{5,21},{6,22},{7,23},{8,24},{9,... | collective-permute-start | bytes 196616 | tf_op jit(solution)/shard_map/ppermute | solution.py:412
  39.6 5.6 %collective-permute-start.14 = (f32[2,64,128]{2,1,0:T(8,128)S(1)}, f32[2,64,128]{2,1,0:T(8,128)S(1)}, u32[]{:S(2)}, u32[]{:S(2)}) collective-permute-start(f32[2,64,128]{2,1,0:T(8,128)S(1)} %get-tuple-element.79.pair_ref), channel_id=1, source_target_pairs={{1,16},{2,17},{3,18},{4,19},{5,20},{6,21},{7,22},{8,23},{9,24},{10... | collective-permute-start | bytes 196616 | tf_op jit(solution)/shard_map/ppermute | solution.py:411
  40.9 5.6 %collective-permute-start.13 = (f32[2,64,128]{2,1,0:T(8,128)S(1)}, f32[2,64,128]{2,1,0:T(8,128)S(1)}, u32[]{:S(2)}, u32[]{:S(2)}) collective-permute-start(f32[2,64,128]{2,1,0:T(8,128)S(1)} %get-tuple-element.79.pair_ref), channel_id=1, source_target_pairs={{0,16},{1,17},{2,18},{3,19},{4,20},{5,21},{6,22},{7,23},{8,24},{9,... | collective-permute-start | bytes 196616 | tf_op jit(solution)/shard_map/ppermute | solution.py:412
  50.8 5.2 %collective-permute-start.18 = (f32[64,128]{1,0:T(8,128)S(1)}, f32[64,128]{1,0:T(8,128)S(1)}, u32[]{:S(2)}, u32[]{:S(2)}) collective-permute-start(f32[64,128]{1,0:T(8,128)S(1)} %last.2.field_ref), channel_id=1, source_target_pairs={{1,16},{2,17},{3,18},{4,19},{5,20},{6,21},{7,22},{8,23},{9,24},{10... | collective-permute-start | bytes 98312 | tf_op jit(solution)/shard_map/ppermute | solution.py:411
  52.1 5.5 %collective-permute-start.17 = (f32[64,128]{1,0:T(8,128)S(1)}, f32[64,128]{1,0:T(8,128)S(1)}, u32[]{:S(2)}, u32[]{:S(2)}) collective-permute-start(f32[64,128]{1,0:T(8,128)S(1)} %last.2.field_ref), channel_id=1, source_target_pairs={{0,16},{1,17},{2,18},{3,19},{4,20},{5,21},{6,22},{7,23},{8,24},{9,... | collective-permute-start | bytes 98312 | tf_op jit(solution)/shard_map/ppermute | solution.py:412
  75.1 5.2 %collective-permute-start.20 = (f32[64,128]{1,0:T(8,128)S(1)}, f32[64,128]{1,0:T(8,128)S(1)}, u32[]{:S(2)}, u32[]{:S(2)}) collective-permute-start(f32[64,128]{1,0:T(8,128)S(1)} %get-tuple-element.86.field_ref), channel_id=1, source_target_pairs={{1,16},{2,17},{3,18},{4,19},{5,20},{6,21},{7,22},{8,23},{9,24},{10... | collective-permute-start | bytes 98312 | tf_op jit(solution)/shard_map/ppermute | solution.py:411
  76.4 5.3 %collective-permute-start.19 = (f32[64,128]{1,0:T(8,128)S(1)}, f32[64,128]{1,0:T(8,128)S(1)}, u32[]{:S(2)}, u32[]{:S(2)}) collective-permute-start(f32[64,128]{1,0:T(8,128)S(1)} %get-tuple-element.86.field_ref), channel_id=1, source_target_pairs={{0,16},{1,17},{2,18},{3,19},{4,20},{5,21},{6,22},{7,23},{8,24},{9,... | collective-permute-start | bytes 98312 | tf_op jit(solution)/shard_map/ppermute | solution.py:412
  81.9 3.1 %collective-permute-start.22 = (f32[2,64,128]{2,1,0:T(8,128)S(1)}, f32[2,64,128]{2,1,0:T(8,128)S(1)}, u32[]{:S(2)}, u32[]{:S(2)}) collective-permute-start(f32[2,64,128]{2,1,0:T(8,128)S(1)} %open.3.pair_ref), channel_id=1, source_target_pairs={{16,1},{17,2},{18,3},{19,4},{20,5},{21,6},{22,7},{23,8},{24,9},{25... | collective-permute-start | bytes 196616 | tf_op jit(solution)/shard_map/ppermute | solution.py:411
  85.9 5.6 %collective-permute-start.24 = (f32[2,64,128]{2,1,0:T(8,128)S(1)}, f32[2,64,128]{2,1,0:T(8,128)S(1)}, u32[]{:S(2)}, u32[]{:S(2)}) collective-permute-start(f32[2,64,128]{2,1,0:T(8,128)S(1)} %get-tuple-element.90.pair_ref), channel_id=1, source_target_pairs={{1,16},{2,17},{3,18},{4,19},{5,20},{6,21},{7,22},{8,23},{9,24},{10... | collective-permute-start | bytes 196616 | tf_op jit(solution)/shard_map/ppermute | solution.py:411
  87.2 5.7 %collective-permute-start.23 = (f32[2,64,128]{2,1,0:T(8,128)S(1)}, f32[2,64,128]{2,1,0:T(8,128)S(1)}, u32[]{:S(2)}, u32[]{:S(2)}) collective-permute-start(f32[2,64,128]{2,1,0:T(8,128)S(1)} %get-tuple-element.90.pair_ref), channel_id=1, source_target_pairs={{0,16},{1,17},{2,18},{3,19},{4,20},{5,21},{6,22},{7,23},{8,24},{9,... | collective-permute-start | bytes 196616 | tf_op jit(solution)/shard_map/ppermute | solution.py:412
  97.2 5.6 %collective-permute-start.28 = (f32[2,64,128]{2,1,0:T(8,128)S(1)}, f32[2,64,128]{2,1,0:T(8,128)S(1)}, u32[]{:S(2)}, u32[]{:S(2)}) collective-permute-start(f32[2,64,128]{2,1,0:T(8,128)S(1)} %get-tuple-element.94.pair_ref), channel_id=1, source_target_pairs={{1,16},{2,17},{3,18},{4,19},{5,20},{6,21},{7,22},{8,23},{9,24},{10... | collective-permute-start | bytes 196616 | tf_op jit(solution)/shard_map/ppermute | solution.py:411
  98.5 5.5 %collective-permute-start.27 = (f32[2,64,128]{2,1,0:T(8,128)S(1)}, f32[2,64,128]{2,1,0:T(8,128)S(1)}, u32[]{:S(2)}, u32[]{:S(2)}) collective-permute-start(f32[2,64,128]{2,1,0:T(8,128)S(1)} %get-tuple-element.94.pair_ref), channel_id=1, source_target_pairs={{0,16},{1,17},{2,18},{3,19},{4,20},{5,21},{6,22},{7,23},{8,24},{9,... | collective-permute-start | bytes 196616 | tf_op jit(solution)/shard_map/ppermute | solution.py:412
  108.5 5.6 %collective-permute-start.32 = (f32[2,64,128]{2,1,0:T(8,128)S(1)}, f32[2,64,128]{2,1,0:T(8,128)S(1)}, u32[]{:S(2)}, u32[]{:S(2)}) collective-permute-start(f32[2,64,128]{2,1,0:T(8,128)S(1)} %get-tuple-element.98.pair_ref), channel_id=1, source_target_pairs={{1,16},{2,17},{3,18},{4,19},{5,20},{6,21},{7,22},{8,23},{9,24},{10... | collective-permute-start | bytes 196616 | tf_op jit(solution)/shard_map/ppermute | solution.py:411
  109.8 5.6 %collective-permute-start.31 = (f32[2,64,128]{2,1,0:T(8,128)S(1)}, f32[2,64,128]{2,1,0:T(8,128)S(1)}, u32[]{:S(2)}, u32[]{:S(2)}) collective-permute-start(f32[2,64,128]{2,1,0:T(8,128)S(1)} %get-tuple-element.98.pair_ref), channel_id=1, source_target_pairs={{0,16},{1,17},{2,18},{3,19},{4,20},{5,21},{6,22},{7,23},{8,24},{9,... | collective-permute-start | bytes 196616 | tf_op jit(solution)/shard_map/ppermute | solution.py:412
  119.7 5.2 %collective-permute-start.36 = (f32[64,128]{1,0:T(8,128)S(1)}, f32[64,128]{1,0:T(8,128)S(1)}, u32[]{:S(2)}, u32[]{:S(2)}) collective-permute-start(f32[64,128]{1,0:T(8,128)S(1)} %last.3.field_ref), channel_id=1, source_target_pairs={{1,16},{2,17},{3,18},{4,19},{5,20},{6,21},{7,22},{8,23},{9,24},{10... | collective-permute-start | bytes 98312 | tf_op jit(solution)/shard_map/ppermute | solution.py:411
  121.0 5.5 %collective-permute-start.35 = (f32[64,128]{1,0:T(8,128)S(1)}, f32[64,128]{1,0:T(8,128)S(1)}, u32[]{:S(2)}, u32[]{:S(2)}) collective-permute-start(f32[64,128]{1,0:T(8,128)S(1)} %last.3.field_ref), channel_id=1, source_target_pairs={{0,16},{1,17},{2,18},{3,19},{4,20},{5,21},{6,22},{7,23},{8,24},{9,... | collective-permute-start | bytes 98312 | tf_op jit(solution)/shard_map/ppermute | solution.py:412
  138.3 4.2 %collective-permute-start.37 = (f32[64,128]{1,0:T(8,128)S(1)}, f32[64,128]{1,0:T(8,128)S(1)}, u32[]{:S(2)}, u32[]{:S(2)}) collective-permute-start(f32[64,128]{1,0:T(8,128)S(1)} %get-tuple-element.106), channel_id=1, source_target_pairs={{0,16},{16,0},{1,17},{17,1},{2,18},{18,2},{3,19},{19,3},{4,20},{20... | collective-permute-start | bytes 98312 | tf_op jit(solution)/shard_map/ppermute | solution.py:404
  (14 other events, 34.2 us)

commit v5 on v4

--- a/solution.py
+++ b/solution.py
@@ -13,6 +13,8 @@
 HALF = 64
 STEPS = 4
 STAGES = 2 * STEPS
+GX = 8
+GY = 8
 F32 = jnp.float32
 BF16 = jnp.bfloat16
 FIELD = (VALUES, LANES)
@@ -26,13 +28,14 @@
     return pltpu.with_memory_space_constraint(x, pltpu.HBM)
 
 
-def call(kernel, name, outs, *args, keep=True, fetch=False, scratch=(FIELD,), flops=1 << 22):
+def call(kernel, name, outs, *args, keep=True, fetch=False, scratch=(FIELD,), ints=(), flops=1 << 22):
     whole = pl.BlockSpec(memory_space=pltpu.VMEM)
     shapes = tuple(
         pltpu.VMEM(shape, dtype) if keep else jax.ShapeDtypeStruct(shape, dtype)
         for shape, dtype in outs
     )
     held = [pltpu.VMEM(shape, F32) for shape in scratch]
+    held += [pltpu.VMEM(shape, jnp.int32) for shape in ints]
     if fetch:
         held += [pltpu.SemaphoreType.DMA((16,))]
     return pl.pallas_call(
@@ -59,15 +62,23 @@
     return jnp.take_along_axis(x, jnp.broadcast_to(index, x.shape), axis=1)
 
 
-def twice(row):
-    return jnp.concatenate([row, row], axis=1)
-
-
-def layer_rows(send_ref, core):
-    lowest, highest = send_ref[0:1, :], send_ref[1:2, :]
-    mine = jnp.where(core == 0, lowest, highest)
-    other = jnp.where(core == 0, highest, lowest)
-    return twice(mine), twice(other)
+def raster(neighbor):
+    ahead = jnp.concatenate([neighbor, jnp.zeros((2, LANES), jnp.int32)], axis=0)
+    level = jnp.where(ahead[4:5, :] >= LANES, 0, HALF)
+    steps = (ahead >= 0).astype(jnp.int32)
+    span = 1
+    while span < max(GX, GY):
+        on = ahead >= 0
+        spot = jnp.clip(ahead, 0, LANES - 1)
+        steps = steps + jnp.where(on, jnp.take_along_axis(steps, spot, axis=1), 0)
+        ahead = jnp.where(on, jnp.take_along_axis(ahead, spot, axis=1), -1)
+        span *= 2
+    place = level + GX * steps[2:3, :] + steps[0:1, :]
+    down = jnp.transpose(jnp.broadcast_to(place.astype(F32), (LANES, LANES)))
+    across = lax.broadcasted_iota(jnp.int32, (LANES, LANES), 1).astype(F32)
+    at = lax.broadcasted_iota(jnp.int32, (LANES, LANES), 0).astype(F32)
+    order = jnp.sum(jnp.where(down == across, at, 0.0), axis=0, keepdims=True).astype(jnp.int32)
+    return jnp.broadcast_to(place, (8, LANES)), jnp.broadcast_to(order, (8, LANES))
 
 
 def apply_inverse(inverse_ref, scratch, vector):
@@ -91,29 +102,29 @@
     return upper[:, :width] + ((upper[:, width:] + lower[:, :width]) + lower[:, width:])
 
 
-def own_faces(field, index, valid, faces):
+def own_faces(field, faces):
+    lane = lax.broadcasted_iota(jnp.int32, FIELD, 1)
+    x = jnp.bitwise_and(lane, GX - 1)
+    y = jnp.bitwise_and(lane, GX * GY - GX)
     picked = [
-        columns(field, index[f : f + 1, :]) * jnp.broadcast_to(valid[f : f + 1, :], FIELD)
-        for f in range(4)
+        jnp.where(inside, pltpu.roll(field, by % LANES, 1), 0.0)
+        for inside, by in ((x > 0, 1), (x < GX - 1, -1), (y > 0, GX), (y < GX * GY - GX, -GX))
     ]
     return product(faces[:, : 4 * VALUES], jnp.concatenate(picked, axis=0))
 
 
-def share_kernel(send_any, forcing_any, gain_any, state_any, neighbor_any, blocks_any, inverse_any,
-                 own_ref, out_ref, start_ref, send_ref, neighbor_ref, blocks_ref, inverse_ref,
-                 state_ref, forcing_ref, gain_ref, sems):
+def share_kernel(neighbor_any, forcing_any, gain_any, state_any, blocks_any, inverse_any,
+                 own_ref, out_ref, start_ref, mine_ref, place_ref, blocks_ref, inverse_ref,
+                 state_ref, forcing_ref, gain_ref, neighbor_ref, sems):
     core = lax.axis_index("c")
     part = VALUES // 8
     first = [
-        pltpu.make_async_copy(send_any, send_ref, sems.at[0]),
+        pltpu.make_async_copy(neighbor_any, neighbor_ref, sems.at[0]),
         pltpu.make_async_copy(forcing_any, forcing_ref, sems.at[1]),
         pltpu.make_async_copy(gain_any, gain_ref, sems.at[2]),
         pltpu.make_async_copy(state_any, state_ref, sems.at[3]),
     ]
-    later = [
-        pltpu.make_async_copy(neighbor_any, neighbor_ref, sems.at[4]),
-        pltpu.make_async_copy(blocks_any, blocks_ref, sems.at[5]),
-    ] + [
+    later = [pltpu.make_async_copy(blocks_any, blocks_ref, sems.at[4])] + [
         pltpu.make_async_copy(
             inverse_any.at[pl.ds(part * k, part)], inverse_ref.at[pl.ds(part * k, part)],
             sems.at[8 + k],
@@ -122,13 +133,23 @@
     ]
     for copy in first + later:
         copy.start()
-    for copy in first:
+    first[0].wait()
+    place, order = raster(neighbor_ref[...])
+    turned = pltpu.roll(order, HALF, 1)
+    low = lax.broadcasted_iota(jnp.int32, (8, LANES), 1) < HALF
+    lowest, highest = jnp.where(low, order, turned), jnp.where(low, turned, order)
+    mine = jnp.where(core == 0, lowest, highest)
+    other = jnp.where(core == 0, highest, lowest)
+    mine_ref[...] = mine
+    place_ref[...] = place
+    mine, other = mine[0:1, :], other[0:1, :]
+    for copy in first[1:]:
         copy.wait()
-    mine, other = layer_rows(send_ref, core)
-    low = low_half()
     fields = [forcing_ref[m] for m in range(STEPS)] + [gain_ref[0]]
     for m in range(0, STEPS, 2):
-        out_ref[m // 2] = jnp.where(low, columns(fields[m], other), columns(fields[m + 1], other))
+        out_ref[m // 2] = jnp.where(
+            low_half(), columns(fields[m], other), columns(fields[m + 1], other)
+        )
     out_ref[STEPS // 2] = columns(fields[STEPS], other)
     for m, field in enumerate(fields):
         own_ref[m] = columns(field, mine)
@@ -137,25 +158,9 @@
         copy.wait()
 
 
-def tables_kernel(
-    send_ref, neighbor_ref, blocks_ref, inverse_ref, index_ref, valid_ref, place_ref, faces_ref,
-    table_ref, _
-):
-    core = lax.axis_index("c")
-    mine, _other = layer_rows(send_ref, core)
-    order = jnp.concatenate([send_ref[0:1, :], send_ref[1:2, :]], axis=1)
-    down = jnp.transpose(jnp.broadcast_to(order.astype(F32), (LANES, LANES)))
-    across = lax.broadcasted_iota(jnp.int32, (LANES, LANES), 1).astype(F32)
-    at = lax.broadcasted_iota(jnp.int32, (LANES, LANES), 0).astype(F32)
-    place = jnp.sum(jnp.where(down == across, at, 0.0), axis=0, keepdims=True).astype(jnp.int32)
-    place = jnp.broadcast_to(place, (8, LANES))
-    place_ref[...] = place
-    pad = jnp.zeros((2, LANES), jnp.int32)
-    local = columns(jnp.concatenate([neighbor_ref[...], pad], axis=0), mine)
-    valid_ref[...] = (local >= 0).astype(F32)
-    lane = lax.broadcasted_iota(jnp.int32, (8, LANES), 1)
-    spot = columns(place, jnp.clip(local, 0, LANES - 1))
-    index_ref[...] = jnp.bitwise_and(spot, HALF - 1) + jnp.where(lane < HALF, 0, HALF)
+def tables_kernel(mine_ref, blocks_ref, inverse_ref, faces_ref, table_ref, _):
+    core = lax.axis_index("c")
+    mine = jnp.concatenate([mine_ref[...]] * (VALUES // 8), axis=0)
     blocks = [blocks_ref[f] for f in range(4)]
     blocks += [
         jnp.where(core == 0, blocks_ref[4], blocks_ref[5]),
@@ -213,7 +218,7 @@
         field_ref[...] = jnp.zeros(FIELD, F32)
 
 
-def late_kernel(lead, field_ref, right_ref, index_ref, valid_ref, faces_ref, table_ref, field_out,
+def late_kernel(lead, field_ref, right_ref, faces_ref, table_ref, field_out,
                 ahead_ref, scratch):
     core = lax.axis_index("c")
 
@@ -221,17 +226,17 @@
     def _run():
         field = apply_inverse(table_ref, scratch, right_ref[...])
         field_out[...] = field
-        ahead_ref[...] = own_faces(field, index_ref[...], valid_ref[...], faces_ref[...])
+        ahead_ref[...] = own_faces(field, faces_ref[...])
 
     @pl.when(core == lead)
     def _keep():
         field_out[...] = field_ref[...]
 
 
-def ahead_kernel(active, pair_ref, index_ref, valid_ref, faces_ref, ahead_ref, _):
+def ahead_kernel(active, pair_ref, faces_ref, ahead_ref, _):
     @pl.when(lax.axis_index("c") == active)
     def _run():
-        ahead_ref[...] = own_faces(pair_ref[1], index_ref[...], valid_ref[...], faces_ref[...])
+        ahead_ref[...] = own_faces(pair_ref[1], faces_ref[...])
 
 
 def across_faces(faces, far, near):
@@ -255,13 +260,13 @@
 
 
 def advance_kernel(stage, active, sourced, pair_ref, right_ref, ahead_ref, near_ref, far_ref,
-                   index_ref, valid_ref, faces_ref, table_ref, sources_ref, pair_out, right_out,
+                   faces_ref, table_ref, sources_ref, pair_out, right_out,
                    scratch):
     core = lax.axis_index("c")
 
     @pl.when(core == active)
     def _run():
-        index, valid, faces = index_ref[...], valid_ref[...], faces_ref[...]
+        faces = faces_ref[...]
         far, near = (jnp.concatenate([ref[0], ref[1]], axis=1) for ref in (far_ref, near_ref))
         across = across_faces(faces, far, near)
         right = right_ref[...]
@@ -277,7 +282,7 @@
 
         field, right = taken(ahead_ref[...] + across[:, :LANES], right, stage)
         pair_out[0] = field
-        summed = own_faces(field, index, valid, faces) + across[:, LANES:]
+        summed = own_faces(field, faces) + across[:, LANES:]
         field, right = taken(summed, right, stage + 1)
         pair_out[1] = field
         right_out[...] = right
@@ -302,10 +307,10 @@
         field_out[...] = pair_ref[1]
 
 
-def tail_kernel(lead, field_ref, right_ref, near_ref, far_ref, index_ref, valid_ref, faces_ref,
+def tail_kernel(lead, field_ref, right_ref, near_ref, far_ref, faces_ref,
                 table_ref, out_ref, scratch):
     core = lax.axis_index("c")
-    out_ref[...] = own_faces(field_ref[...], index_ref[...], valid_ref[...], faces_ref[...])
+    out_ref[...] = own_faces(field_ref[...], faces_ref[...])
 
     @pl.when(core == lead)
     def _run():
@@ -413,23 +418,20 @@
         return vmem(near), vmem(far)
 
     field, pair_shape = (FIELD, F32), ((2,) + FIELD, F32)
-    raw = (send_rows, neighbor, face_blocks, block_inverse)
-    own, sent, start, *raw = call(
+    index, raw = ((8, LANES), jnp.int32), (face_blocks, block_inverse)
+    own, sent, start, mine, place, *raw = call(
         share_kernel, "share",
-        [((STEPS + 1,) + FIELD, F32), ((STEPS // 2 + 1,) + FIELD, F32), field,
+        [((STEPS + 1,) + FIELD, F32), ((STEPS // 2 + 1,) + FIELD, F32), field, index, index,
          *((x.shape, x.dtype) for x in raw)],
-        *map(hbm, (send_rows, forcing, coarse_gain, initial_state, *raw[1:])), fetch=True,
-        scratch=(FIELD, forcing.shape, coarse_gain.shape),
+        *map(hbm, (neighbor, forcing, coarse_gain, initial_state, *raw)), fetch=True,
+        scratch=(FIELD, forcing.shape, coarse_gain.shape), ints=(neighbor.shape,),
     )
     got = swap_cores(sent)
-    index, valid, place, faces, table = call(
+    faces, table = call(
         tables_kernel, "tables",
-        [((8, LANES), jnp.int32), ((8, LANES), F32), ((8, LANES), jnp.int32),
-         ((2 * VALUES, 6 * VALUES), BF16), ((VALUES,) + FIELD, F32)],
-        *map(vmem, raw),
-    )
-    index, valid, place, faces, table = map(vmem, (index, valid, place, faces, table))
-    operator = (index, valid, faces, table)
+        [((2 * VALUES, 6 * VALUES), BF16), ((VALUES,) + FIELD, F32)], *map(vmem, (mine, *raw)),
+    )
+    operator = faces, table = vmem(faces), vmem(table)
     sources, gain, begun, right = call(
         functools.partial(first_kernel, 0), "first", [((STEPS,) + FIELD, F32), field, field, field],
         vmem(own), vmem(got), vmem(start), table,
@@ -453,7 +455,7 @@
             pair = vmem(pair)
             near, far = halo(pair, active)
             (ahead,) = call(
-                functools.partial(ahead_kernel, active), "ahead", [field], pair, index, valid, faces
+                functools.partial(ahead_kernel, active), "ahead", [field], pair, faces
             )
             ahead = vmem(ahead)
             if stage < STAGES - 2:
@@ -493,7 +495,7 @@
     )
     got = vmem(swap_cores(sent))
     return call(
-        output_kernel, "output", [((1,) + FIELD, F32)] * 2, vmem(end), residual, got, place,
+        output_kernel, "output", [((1,) + FIELD, F32)] * 2, vmem(end), residual, got, vmem(place),
         keep=False,
     )
 

time: 144 us -> 145 us (level)
  no operation moved by 1% of the time
where the time goes in v5:
time: 145 us; the launch traced here: 144 us
  starting transfers between devices  53.5 us (37%)
  waiting for transfers between devices  46.2 us (32%)
  blocking collectives  27.7 us (19%)
  Pallas kernels  14.8 us (10%)
    all_to_all x2, blocking collectives, evolve(): return (vmem(residual), vmem(lax.all_to_all(chunk, 'q', 0, 0)))  27.7 us
    ppermute x18, waiting for transfers between devices, halo(): far = lax.ppermute(x, ('c', 'space'), across)  25.7 us
    ppermute x18, starting transfers between devices, halo(): near = lax.ppermute(x, 'c', [(1 - to, to)])  24.2 us
    ppermute x18, starting transfers between devices, halo(): far = lax.ppermute(x, ('c', 'space'), across)  23.4 us
    ppermute x18, waiting for transfers between devices, halo(): near = lax.ppermute(x, 'c', [(1 - to, to)])  19.7 us
    pallas_call x42, Pallas kernels, call(): pl.pallas_call(kernel, out_shape=shapes, in_specs=[pl.BlockSpec(memory_sp...  14.8 us
    ppermute x2, starting transfers between devices, swap_cores(): return lax.ppermute(x, 'c', [(0, 1), (1, 0)])  5.98 us
  transfers between devices with their start and end apart: 38, of which 29 were waited for; matrix products, arithmetic and copies ran while one was open for 0% of the time, Pallas kernels for 3%

profile of v5, /device:TPU:385, one launch (start us, length us, event | category | flops | bytes accessed | tf_op | source)
XLA Modules:
  0.0 143.6 jit_solution(2815475687078977274)
XLA Ops:
  0.6 1.9 %share.1 = (f32[5,64,128]{2,1,0:T(8,128)S(1)}, f32[3,64,128]{2,1,0:T(8,128)S(1)}, f32[64,128]{1,0:T(8,128)S(1)}, s32[8,128]{1,0:T(8,128)S(1)}, s32[8,128]{1,0:T(...) custom-call(s32[6,128]{1,0:T(8,128)} %neighbor_any.1, f32[4,64,128]{2,1,0:T(8,128)} %forcing_any.1, ...), custom_call_target="tpu_custom_call" | custom-call | flops 4194304 | bytes 1048576 | tf_op jit(solution)/shard_map/share/pallas_call | solution.py:41
  2.5 2.6 %collective-permute-start = (f32[3,64,128]{2,1,0:T(8,128)S(1)}, f32[3,64,128]{2,1,0:T(8,128)S(1)}, u32[]{:S(2)}, u32[]{:S(2)}) collective-permute-start(f32[3,64,128]{2,1,0:T(8,128)S(1)} %get-tuple-element.53), channel_id=1, source_target_pairs={{0,16},{16,0},{1,17},{17,1},{2,18},{18,2},{3,19},{19,3},{4,20},{20... | collective-permute-start | bytes 294920 | tf_op jit(solution)/shard_map/ppermute | solution.py:409
  5.1 1.5 %tables.1 = (bf16[128,384]{1,0:T(8,128)(2,1)S(1)}, f32[64,64,128]{2,1,0:T(8,128)S(1)}) custom-call(s32[8,128]{1,0:T(8,128)S(1)} %get-tuple-element.55.mine_ref, f32[6,64,64]{2,1,0:T(8,128)S(1)} %get-tuple-element.56.blocks_ref, f32[64,64,128]{2,1,0:T(8,128)S(1)} %get-tuple-element.57.inverse_ref), custom_call_target="tpu_custom_call" | custom-call | flops 4194304 | bytes 1048576 | tf_op jit(solution)/shard_map/tables/pallas_call | solution.py:41
  9.8 2.2 %collective-permute-done.2.far_ref = f32[64,128]{1,0:T(8,128)S(1)} collective-permute-done((f32[64,128]{1,0:T(8,128)S(1)}, f32[64,128]{1,0:T(8,128)S(1)}, u32[]{:S(2)}, u32[]{:S(2)}) %collective-permute-start.2) | collective-permute-done | bytes 32800 | tf_op jit(solution)/shard_map/ppermute | solution.py:416
  14.6 1.8 %collective-permute-start.3 = (f32[2,64,128]{2,1,0:T(8,128)S(1)}, f32[2,64,128]{2,1,0:T(8,128)S(1)}, u32[]{:S(2)}, u32[]{:S(2)}) collective-permute-start(f32[2,64,128]{2,1,0:T(8,128)S(1)} %open.2.pair_ref), channel_id=1, source_target_pairs={{16,0},{17,1},{18,2},{19,3},{20,4},{21,5},{22,6},{23,7},{24,8},{25... | collective-permute-start | bytes 196616 | tf_op jit(solution)/shard_map/ppermute | solution.py:417
  20.1 2.7 %collective-permute-done.6.far_ref = f32[2,64,128]{2,1,0:T(8,128)S(1)} collective-permute-done((f32[2,64,128]{2,1,0:T(8,128)S(1)}, f32[2,64,128]{2,1,0:T(8,128)S(1)}, u32[]{:S(2)}, u32[]{:S(2)}) %collective-permute-start.6) | collective-permute-done | bytes 65568 | tf_op jit(solution)/shard_map/ppermute | solution.py:416
  22.8 1.4 collective-permute-done.5.near_ref
  31.4 2.8 %collective-permute-done.10.far_ref = f32[2,64,128]{2,1,0:T(8,128)S(1)} collective-permute-done((f32[2,64,128]{2,1,0:T(8,128)S(1)}, f32[2,64,128]{2,1,0:T(8,128)S(1)}, u32[]{:S(2)}, u32[]{:S(2)}) %collective-permute-start.10) | collective-permute-done | bytes 65568 | tf_op jit(solution)/shard_map/ppermute | solution.py:416
  42.7 2.8 %collective-permute-done.14.far_ref = f32[2,64,128]{2,1,0:T(8,128)S(1)} collective-permute-done((f32[2,64,128]{2,1,0:T(8,128)S(1)}, f32[2,64,128]{2,1,0:T(8,128)S(1)}, u32[]{:S(2)}, u32[]{:S(2)}) %collective-permute-start.14) | collective-permute-done | bytes 65568 | tf_op jit(solution)/shard_map/ppermute | solution.py:416
  53.9 2.4 %collective-permute-done.18.refs_3_ = f32[64,128]{1,0:T(8,128)S(1)} collective-permute-done((f32[64,128]{1,0:T(8,128)S(1)}, f32[64,128]{1,0:T(8,128)S(1)}, u32[]{:S(2)}, u32[]{:S(2)}) %collective-permute-start.18) | collective-permute-done | bytes 32800 | tf_op jit(solution)/shard_map/ppermute | solution.py:416
  56.3 1.5 %collective-permute-done.17.refs_2_ = f32[64,128]{1,0:T(8,128)S(1)} collective-permute-done((f32[64,128]{1,0:T(8,128)S(1)}, f32[64,128]{1,0:T(8,128)S(1)}, u32[]{:S(2)}, u32[]{:S(2)}) %collective-permute-start.17) | collective-permute-done | bytes 32800 | tf_op jit(solution)/shard_map/ppermute | solution.py:417
  58.3 16.8 %all_to_all.10.sums_ref.gains_ref = f32[16,64,128]{2,1,0:T(8,128)S(1)} all-to-all(f32[16,64,128]{2,1,0:T(8,128)S(1)} %get-tuple-element.78), channel_id=1, replica_groups=mesh['q'=16,'c'=2,'space'=16] {'q'}, dimensions={0} | all-to-all | bytes 1048576 | tf_op jit(solution)/shard_map/all_to_all | solution.py:483
  78.4 2.2 %collective-permute-done.20.far_ref = f32[64,128]{1,0:T(8,128)S(1)} collective-permute-done((f32[64,128]{1,0:T(8,128)S(1)}, f32[64,128]{1,0:T(8,128)S(1)}, u32[]{:S(2)}, u32[]{:S(2)}) %collective-permute-start.20) | collective-permute-done | bytes 32800 | tf_op jit(solution)/shard_map/ppermute | solution.py:416
  80.5 1.3 collective-permute-done.19.near_ref
  83.5 1.8 %collective-permute-start.21 = (f32[2,64,128]{2,1,0:T(8,128)S(1)}, f32[2,64,128]{2,1,0:T(8,128)S(1)}, u32[]{:S(2)}, u32[]{:S(2)}) collective-permute-start(f32[2,64,128]{2,1,0:T(8,128)S(1)} %open.3.pair_ref), channel_id=1, source_target_pairs={{16,0},{17,1},{18,2},{19,3},{20,4},{21,5},{22,6},{23,7},{24,8},{25... | collective-permute-start | bytes 196616 | tf_op jit(solution)/shard_map/ppermute | solution.py:417
  89.0 2.7 %collective-permute-done.24.far_ref = f32[2,64,128]{2,1,0:T(8,128)S(1)} collective-permute-done((f32[2,64,128]{2,1,0:T(8,128)S(1)}, f32[2,64,128]{2,1,0:T(8,128)S(1)}, u32[]{:S(2)}, u32[]{:S(2)}) %collective-permute-start.24) | collective-permute-done | bytes 65568 | tf_op jit(solution)/shard_map/ppermute | solution.py:416
  91.7 1.4 collective-permute-done.23.near_ref
  94.0 1.5 %collective-permute-start.26 = (f32[2,64,128]{2,1,0:T(8,128)S(1)}, f32[2,64,128]{2,1,0:T(8,128)S(1)}, u32[]{:S(2)}, u32[]{:S(2)}) collective-permute-start(f32[2,64,128]{2,1,0:T(8,128)S(1)} %get-tuple-element.86.pair_ref), channel_id=1, source_target_pairs={{16,1},{17,2},{18,3},{19,4},{20,5},{21,6},{22,7},{23,8},{24,9},{25... | collective-permute-start | bytes 196616 | tf_op jit(solution)/shard_map/ppermute | solution.py:416
  100.5 2.8 %collective-permute-done.28.far_ref = f32[2,64,128]{2,1,0:T(8,128)S(1)} collective-permute-done((f32[2,64,128]{2,1,0:T(8,128)S(1)}, f32[2,64,128]{2,1,0:T(8,128)S(1)}, u32[]{:S(2)}, u32[]{:S(2)}) %collective-permute-start.28) | collective-permute-done | bytes 65568 | tf_op jit(solution)/shard_map/ppermute | solution.py:416
  111.7 2.8 %collective-permute-done.32.far_ref = f32[2,64,128]{2,1,0:T(8,128)S(1)} collective-permute-done((f32[2,64,128]{2,1,0:T(8,128)S(1)}, f32[2,64,128]{2,1,0:T(8,128)S(1)}, u32[]{:S(2)}, u32[]{:S(2)}) %collective-permute-start.32) | collective-permute-done | bytes 65568 | tf_op jit(solution)/shard_map/ppermute | solution.py:416
  122.9 2.4 %collective-permute-done.36.refs_3_ = f32[64,128]{1,0:T(8,128)S(1)} collective-permute-done((f32[64,128]{1,0:T(8,128)S(1)}, f32[64,128]{1,0:T(8,128)S(1)}, u32[]{:S(2)}, u32[]{:S(2)}) %collective-permute-start.36) | collective-permute-done | bytes 32800 | tf_op jit(solution)/shard_map/ppermute | solution.py:416
  125.3 1.5 %collective-permute-done.35.refs_2_ = f32[64,128]{1,0:T(8,128)S(1)} collective-permute-done((f32[64,128]{1,0:T(8,128)S(1)}, f32[64,128]{1,0:T(8,128)S(1)}, u32[]{:S(2)}, u32[]{:S(2)}) %collective-permute-start.35) | collective-permute-done | bytes 32800 | tf_op jit(solution)/shard_map/ppermute | solution.py:417
  127.4 11.0 %all_to_all.11.sums_ref = f32[16,32,128]{2,1,0:T(8,128)S(1)} all-to-all(f32[16,32,128]{2,1,0:T(8,128)S(1)} %get-tuple-element.96), channel_id=1, replica_groups=mesh['q'=16,'c'=2,'space'=16] {'q'}, dimensions={0} | all-to-all | bytes 524288 | tf_op jit(solution)/shard_map/all_to_all | solution.py:483
  138.6 3.4 %collective-permute-start.37 = (f32[64,128]{1,0:T(8,128)S(1)}, f32[64,128]{1,0:T(8,128)S(1)}, u32[]{:S(2)}, u32[]{:S(2)}) collective-permute-start(f32[64,128]{1,0:T(8,128)S(1)} %get-tuple-element.100), channel_id=1, source_target_pairs={{0,16},{16,0},{1,17},{17,1},{2,18},{18,2},{3,19},{19,3},{4,20},{20... | collective-permute-start | bytes 98312 | tf_op jit(solution)/shard_map/ppermute | solution.py:409
  (96 shorter events, 67.5 us)
Async XLA Ops:
  2.5 4.1 %collective-permute-start = (f32[3,64,128]{2,1,0:T(8,128)S(1)}, f32[3,64,128]{2,1,0:T(8,128)S(1)}, u32[]{:S(2)}, u32[]{:S(2)}) collective-permute-start(f32[3,64,128]{2,1,0:T(8,128)S(1)} %get-tuple-element.53), channel_id=1, source_target_pairs={{0,16},{16,0},{1,17},{17,1},{2,18},{18,2},{3,19},{19,3},{4,20},{20... | collective-permute-start | bytes 294920 | tf_op jit(solution)/shard_map/ppermute | solution.py:409
  6.8 5.2 %collective-permute-start.2 = (f32[64,128]{1,0:T(8,128)S(1)}, f32[64,128]{1,0:T(8,128)S(1)}, u32[]{:S(2)}, u32[]{:S(2)}) collective-permute-start(f32[64,128]{1,0:T(8,128)S(1)} %get-tuple-element.59.field_ref), channel_id=1, source_target_pairs={{1,16},{2,17},{3,18},{4,19},{5,20},{6,21},{7,22},{8,23},{9,24},{10... | collective-permute-start | bytes 98312 | tf_op jit(solution)/shard_map/ppermute | solution.py:416
  8.1 4.9 %collective-permute-start.1 = (f32[64,128]{1,0:T(8,128)S(1)}, f32[64,128]{1,0:T(8,128)S(1)}, u32[]{:S(2)}, u32[]{:S(2)}) collective-permute-start(f32[64,128]{1,0:T(8,128)S(1)} %get-tuple-element.59.field_ref), channel_id=1, source_target_pairs={{0,16},{1,17},{2,18},{3,19},{4,20},{5,21},{6,22},{7,23},{8,24},{9,... | collective-permute-start | bytes 98312 | tf_op jit(solution)/shard_map/ppermute | solution.py:417
  13.3 3.1 %collective-permute-start.4 = (f32[2,64,128]{2,1,0:T(8,128)S(1)}, f32[2,64,128]{2,1,0:T(8,128)S(1)}, u32[]{:S(2)}, u32[]{:S(2)}) collective-permute-start(f32[2,64,128]{2,1,0:T(8,128)S(1)} %open.2.pair_ref), channel_id=1, source_target_pairs={{16,1},{17,2},{18,3},{19,4},{20,5},{21,6},{22,7},{23,8},{24,9},{25... | collective-permute-start | bytes 196616 | tf_op jit(solution)/shard_map/ppermute | solution.py:416
  17.2 5.6 %collective-permute-start.6 = (f32[2,64,128]{2,1,0:T(8,128)S(1)}, f32[2,64,128]{2,1,0:T(8,128)S(1)}, u32[]{:S(2)}, u32[]{:S(2)}) collective-permute-start(f32[2,64,128]{2,1,0:T(8,128)S(1)} %get-tuple-element.65.pair_ref), channel_id=1, source_target_pairs={{1,16},{2,17},{3,18},{4,19},{5,20},{6,21},{7,22},{8,23},{9,24},{10... | collective-permute-start | bytes 196616 | tf_op jit(solution)/shard_map/ppermute | solution.py:416
  18.5 5.6 %collective-permute-start.5 = (f32[2,64,128]{2,1,0:T(8,128)S(1)}, f32[2,64,128]{2,1,0:T(8,128)S(1)}, u32[]{:S(2)}, u32[]{:S(2)}) collective-permute-start(f32[2,64,128]{2,1,0:T(8,128)S(1)} %get-tuple-element.65.pair_ref), channel_id=1, source_target_pairs={{0,16},{1,17},{2,18},{3,19},{4,20},{5,21},{6,22},{7,23},{8,24},{9,... | collective-permute-start | bytes 196616 | tf_op jit(solution)/shard_map/ppermute | solution.py:417
  28.6 5.6 %collective-permute-start.10 = (f32[2,64,128]{2,1,0:T(8,128)S(1)}, f32[2,64,128]{2,1,0:T(8,128)S(1)}, u32[]{:S(2)}, u32[]{:S(2)}) collective-permute-start(f32[2,64,128]{2,1,0:T(8,128)S(1)} %get-tuple-element.69.pair_ref), channel_id=1, source_target_pairs={{1,16},{2,17},{3,18},{4,19},{5,20},{6,21},{7,22},{8,23},{9,24},{10... | collective-permute-start | bytes 196616 | tf_op jit(solution)/shard_map/ppermute | solution.py:416
  29.9 5.5 %collective-permute-start.9 = (f32[2,64,128]{2,1,0:T(8,128)S(1)}, f32[2,64,128]{2,1,0:T(8,128)S(1)}, u32[]{:S(2)}, u32[]{:S(2)}) collective-permute-start(f32[2,64,128]{2,1,0:T(8,128)S(1)} %get-tuple-element.69.pair_ref), channel_id=1, source_target_pairs={{0,16},{1,17},{2,18},{3,19},{4,20},{5,21},{6,22},{7,23},{8,24},{9,... | collective-permute-start | bytes 196616 | tf_op jit(solution)/shard_map/ppermute | solution.py:417
  39.8 5.6 %collective-permute-start.14 = (f32[2,64,128]{2,1,0:T(8,128)S(1)}, f32[2,64,128]{2,1,0:T(8,128)S(1)}, u32[]{:S(2)}, u32[]{:S(2)}) collective-permute-start(f32[2,64,128]{2,1,0:T(8,128)S(1)} %get-tuple-element.73.pair_ref), channel_id=1, source_target_pairs={{1,16},{2,17},{3,18},{4,19},{5,20},{6,21},{7,22},{8,23},{9,24},{10... | collective-permute-start | bytes 196616 | tf_op jit(solution)/shard_map/ppermute | solution.py:416
  41.1 5.5 %collective-permute-start.13 = (f32[2,64,128]{2,1,0:T(8,128)S(1)}, f32[2,64,128]{2,1,0:T(8,128)S(1)}, u32[]{:S(2)}, u32[]{:S(2)}) collective-permute-start(f32[2,64,128]{2,1,0:T(8,128)S(1)} %get-tuple-element.73.pair_ref), channel_id=1, source_target_pairs={{0,16},{1,17},{2,18},{3,19},{4,20},{5,21},{6,22},{7,23},{8,24},{9,... | collective-permute-start | bytes 196616 | tf_op jit(solution)/shard_map/ppermute | solution.py:417
  51.0 5.2 %collective-permute-start.18 = (f32[64,128]{1,0:T(8,128)S(1)}, f32[64,128]{1,0:T(8,128)S(1)}, u32[]{:S(2)}, u32[]{:S(2)}) collective-permute-start(f32[64,128]{1,0:T(8,128)S(1)} %last.2.field_ref), channel_id=1, source_target_pairs={{1,16},{2,17},{3,18},{4,19},{5,20},{6,21},{7,22},{8,23},{9,24},{10... | collective-permute-start | bytes 98312 | tf_op jit(solution)/shard_map/ppermute | solution.py:416
  52.3 5.4 %collective-permute-start.17 = (f32[64,128]{1,0:T(8,128)S(1)}, f32[64,128]{1,0:T(8,128)S(1)}, u32[]{:S(2)}, u32[]{:S(2)}) collective-permute-start(f32[64,128]{1,0:T(8,128)S(1)} %last.2.field_ref), channel_id=1, source_target_pairs={{0,16},{1,17},{2,18},{3,19},{4,20},{5,21},{6,22},{7,23},{8,24},{9,... | collective-permute-start | bytes 98312 | tf_op jit(solution)/shard_map/ppermute | solution.py:417
  75.3 5.2 %collective-permute-start.20 = (f32[64,128]{1,0:T(8,128)S(1)}, f32[64,128]{1,0:T(8,128)S(1)}, u32[]{:S(2)}, u32[]{:S(2)}) collective-permute-start(f32[64,128]{1,0:T(8,128)S(1)} %get-tuple-element.80.field_ref), channel_id=1, source_target_pairs={{1,16},{2,17},{3,18},{4,19},{5,20},{6,21},{7,22},{8,23},{9,24},{10... | collective-permute-start | bytes 98312 | tf_op jit(solution)/shard_map/ppermute | solution.py:416
  76.6 5.3 %collective-permute-start.19 = (f32[64,128]{1,0:T(8,128)S(1)}, f32[64,128]{1,0:T(8,128)S(1)}, u32[]{:S(2)}, u32[]{:S(2)}) collective-permute-start(f32[64,128]{1,0:T(8,128)S(1)} %get-tuple-element.80.field_ref), channel_id=1, source_target_pairs={{0,16},{1,17},{2,18},{3,19},{4,20},{5,21},{6,22},{7,23},{8,24},{9,... | collective-permute-start | bytes 98312 | tf_op jit(solution)/shard_map/ppermute | solution.py:417
  82.2 3.1 %collective-permute-start.22 = (f32[2,64,128]{2,1,0:T(8,128)S(1)}, f32[2,64,128]{2,1,0:T(8,128)S(1)}, u32[]{:S(2)}, u32[]{:S(2)}) collective-permute-start(f32[2,64,128]{2,1,0:T(8,128)S(1)} %open.3.pair_ref), channel_id=1, source_target_pairs={{16,1},{17,2},{18,3},{19,4},{20,5},{21,6},{22,7},{23,8},{24,9},{25... | collective-permute-start | bytes 196616 | tf_op jit(solution)/shard_map/ppermute | solution.py:416
  86.1 5.6 %collective-permute-start.24 = (f32[2,64,128]{2,1,0:T(8,128)S(1)}, f32[2,64,128]{2,1,0:T(8,128)S(1)}, u32[]{:S(2)}, u32[]{:S(2)}) collective-permute-start(f32[2,64,128]{2,1,0:T(8,128)S(1)} %get-tuple-element.84.pair_ref), channel_id=1, source_target_pairs={{1,16},{2,17},{3,18},{4,19},{5,20},{6,21},{7,22},{8,23},{9,24},{10... | collective-permute-start | bytes 196616 | tf_op jit(solution)/shard_map/ppermute | solution.py:416
  87.4 5.6 %collective-permute-start.23 = (f32[2,64,128]{2,1,0:T(8,128)S(1)}, f32[2,64,128]{2,1,0:T(8,128)S(1)}, u32[]{:S(2)}, u32[]{:S(2)}) collective-permute-start(f32[2,64,128]{2,1,0:T(8,128)S(1)} %get-tuple-element.84.pair_ref), channel_id=1, source_target_pairs={{0,16},{1,17},{2,18},{3,19},{4,20},{5,21},{6,22},{7,23},{8,24},{9,... | collective-permute-start | bytes 196616 | tf_op jit(solution)/shard_map/ppermute | solution.py:417
  97.6 5.6 %collective-permute-start.28 = (f32[2,64,128]{2,1,0:T(8,128)S(1)}, f32[2,64,128]{2,1,0:T(8,128)S(1)}, u32[]{:S(2)}, u32[]{:S(2)}) collective-permute-start(f32[2,64,128]{2,1,0:T(8,128)S(1)} %get-tuple-element.88.pair_ref), channel_id=1, source_target_pairs={{1,16},{2,17},{3,18},{4,19},{5,20},{6,21},{7,22},{8,23},{9,24},{10... | collective-permute-start | bytes 196616 | tf_op jit(solution)/shard_map/ppermute | solution.py:416
  98.9 5.5 %collective-permute-start.27 = (f32[2,64,128]{2,1,0:T(8,128)S(1)}, f32[2,64,128]{2,1,0:T(8,128)S(1)}, u32[]{:S(2)}, u32[]{:S(2)}) collective-permute-start(f32[2,64,128]{2,1,0:T(8,128)S(1)} %get-tuple-element.88.pair_ref), channel_id=1, source_target_pairs={{0,16},{1,17},{2,18},{3,19},{4,20},{5,21},{6,22},{7,23},{8,24},{9,... | collective-permute-start | bytes 196616 | tf_op jit(solution)/shard_map/ppermute | solution.py:417
  108.9 5.6 %collective-permute-start.32 = (f32[2,64,128]{2,1,0:T(8,128)S(1)}, f32[2,64,128]{2,1,0:T(8,128)S(1)}, u32[]{:S(2)}, u32[]{:S(2)}) collective-permute-start(f32[2,64,128]{2,1,0:T(8,128)S(1)} %get-tuple-element.92.pair_ref), channel_id=1, source_target_pairs={{1,16},{2,17},{3,18},{4,19},{5,20},{6,21},{7,22},{8,23},{9,24},{10... | collective-permute-start | bytes 196616 | tf_op jit(solution)/shard_map/ppermute | solution.py:416
  110.2 5.5 %collective-permute-start.31 = (f32[2,64,128]{2,1,0:T(8,128)S(1)}, f32[2,64,128]{2,1,0:T(8,128)S(1)}, u32[]{:S(2)}, u32[]{:S(2)}) collective-permute-start(f32[2,64,128]{2,1,0:T(8,128)S(1)} %get-tuple-element.92.pair_ref), channel_id=1, source_target_pairs={{0,16},{1,17},{2,18},{3,19},{4,20},{5,21},{6,22},{7,23},{8,24},{9,... | collective-permute-start | bytes 196616 | tf_op jit(solution)/shard_map/ppermute | solution.py:417
  120.1 5.2 %collective-permute-start.36 = (f32[64,128]{1,0:T(8,128)S(1)}, f32[64,128]{1,0:T(8,128)S(1)}, u32[]{:S(2)}, u32[]{:S(2)}) collective-permute-start(f32[64,128]{1,0:T(8,128)S(1)} %last.3.field_ref), channel_id=1, source_target_pairs={{1,16},{2,17},{3,18},{4,19},{5,20},{6,21},{7,22},{8,23},{9,24},{10... | collective-permute-start | bytes 98312 | tf_op jit(solution)/shard_map/ppermute | solution.py:416
  121.4 5.5 %collective-permute-start.35 = (f32[64,128]{1,0:T(8,128)S(1)}, f32[64,128]{1,0:T(8,128)S(1)}, u32[]{:S(2)}, u32[]{:S(2)}) collective-permute-start(f32[64,128]{1,0:T(8,128)S(1)} %last.3.field_ref), channel_id=1, source_target_pairs={{0,16},{1,17},{2,18},{3,19},{4,20},{5,21},{6,22},{7,23},{8,24},{9,... | collective-permute-start | bytes 98312 | tf_op jit(solution)/shard_map/ppermute | solution.py:417
  138.6 4.2 %collective-permute-start.37 = (f32[64,128]{1,0:T(8,128)S(1)}, f32[64,128]{1,0:T(8,128)S(1)}, u32[]{:S(2)}, u32[]{:S(2)}) collective-permute-start(f32[64,128]{1,0:T(8,128)S(1)} %get-tuple-element.100), channel_id=1, source_target_pairs={{0,16},{16,0},{1,17},{17,1},{2,18},{18,2},{3,19},{19,3},{4,20},{20... | collective-permute-start | bytes 98312 | tf_op jit(solution)/shard_map/ppermute | solution.py:409
  (14 other events, 34.4 us)

commit v6 on v5

--- a/solution.py
+++ b/solution.py
@@ -15,6 +15,7 @@
 STAGES = 2 * STEPS
 GX = 8
 GY = 8
+SQUARED = 16
 F32 = jnp.float32
 BF16 = jnp.bfloat16
 FIELD = (VALUES, LANES)
@@ -28,7 +29,7 @@
     return pltpu.with_memory_space_constraint(x, pltpu.HBM)
 
 
-def call(kernel, name, outs, *args, keep=True, fetch=False, scratch=(FIELD,), ints=(), flops=1 << 22):
+def call(kernel, name, outs, *args, keep=True, fetch=False, alias={}, scratch=(FIELD,), ints=(), flops=1 << 22):
     whole = pl.BlockSpec(memory_space=pltpu.VMEM)
     shapes = tuple(
         pltpu.VMEM(shape, dtype) if keep else jax.ShapeDtypeStruct(shape, dtype)
@@ -44,6 +45,7 @@
         in_specs=[pl.BlockSpec(memory_space=pl.ANY) if fetch else whole] * len(args),
         out_specs=(whole,) * len(shapes),
         scratch_shapes=held,
+        input_output_aliases=alias,
         cost_estimate=pl.CostEstimate(flops=flops, bytes_accessed=1 << 20, transcendentals=0),
         compiler_params=pltpu.CompilerParams(vmem_limit_bytes=16 << 20),
         name=name,
@@ -83,11 +85,10 @@
 
 def apply_inverse(inverse_ref, scratch, vector):
     scratch[...] = vector
-    sums = [None, None]
-    for j in range(VALUES):
-        term = inverse_ref[j] * scratch[j : j + 1, :]
-        sums[j % 2] = term if sums[j % 2] is None else sums[j % 2] + term
-    return sums[0] + sums[1]
+    total = inverse_ref[0] * scratch[0:1, :]
+    for j in range(1, VALUES):
+        total = total + inverse_ref[j] * scratch[j : j + 1, :]
+    return total
 
 
 def halves(x):
@@ -233,10 +234,33 @@
         field_out[...] = field_ref[...]
 
 
-def ahead_kernel(active, pair_ref, faces_ref, ahead_ref, _):
+def ahead_right_kernel(active, left, pair_ref, right_ref, faces_ref, table_ref, ahead_ref, right_out, scratch):
     @pl.when(lax.axis_index("c") == active)
     def _run():
         ahead_ref[...] = own_faces(pair_ref[1], faces_ref[...])
+        right_out[...] = right_ref[...]
+
+    @pl.when(lax.axis_index("c") != active)
+    def _right():
+        if left:
+            right_out[...] = apply_inverse(table_ref, scratch, right_ref[...])
+        else:
+            right_out[...] = right_ref[...]
+
+
+def square(begin, table_ref, square_ref, scratch):
+    @pl.loop(begin, begin + SQUARED)
+    def _column(j):
+        square_ref[j] = apply_inverse(table_ref, scratch, table_ref[j])
+
+
+def ahead_square_kernel(active, begin, pair_ref, faces_ref, table_ref, *refs):
+    ahead_ref, square_ref, scratch = refs[-3:]
+
+    @pl.when(lax.axis_index("c") == active)
+    def _run():
+        ahead_ref[...] = own_faces(pair_ref[1], faces_ref[...])
+        square(begin, table_ref, square_ref, scratch)
 
 
 def across_faces(faces, far, near):
@@ -293,6 +317,37 @@
         right_out[...] = right_ref[...]
 
 
+def advance_squared_kernel(stage, active, pair_ref, right_ref, ahead_ref, near_ref, far_ref,
+                           faces_ref, table_ref, square_ref, pair_out, right_out, scratch, other):
+    core = lax.axis_index("c")
+
+    @pl.when(core == active)
+    def _run():
+        faces = faces_ref[...]
+        far, near = (jnp.concatenate([ref[0], ref[1]], axis=1) for ref in (far_ref, near_ref))
+        across = across_faces(faces, far, near)
+        right = right_ref[...]
+        vector = right - (ahead_ref[...] + across[:, :LANES])
+        if stage % 2 == 0:
+            field = apply_inverse(table_ref, scratch, vector)
+            pair_out[0] = field
+            vector = right - (own_faces(field, faces) + across[:, LANES:])
+            pair_out[1] = apply_inverse(square_ref, other, vector)
+            right_out[...] = vector
+        else:
+            field = apply_inverse(square_ref, scratch, vector)
+            pair_out[0] = field
+            right = apply_inverse(table_ref, scratch, vector)
+            right_out[...] = right
+            vector = right - (own_faces(field, faces) + across[:, LANES:])
+            pair_out[1] = apply_inverse(table_ref, other, vector)
+
+    @pl.when(core != active)
+    def _keep():
+        pair_out[...] = pair_ref[...]
+        right_out[...] = right_ref[...]
+
+
 def last_kernel(lead, pair_ref, right_ref, ahead_ref, near_ref, far_ref, faces_ref, table_ref,
                 field_out, scratch):
     core = lax.axis_index("c")
@@ -307,8 +362,11 @@
         field_out[...] = pair_ref[1]
 
 
-def tail_kernel(lead, field_ref, right_ref, near_ref, far_ref, faces_ref,
-                table_ref, out_ref, scratch):
+def tail_kernel(lead, begin, field_ref, right_ref, near_ref, far_ref, faces_ref, table_ref, *refs):
+    if begin is None:
+        out_ref, scratch = refs
+    else:
+        _, out_ref, square_ref, scratch = refs
     core = lax.axis_index("c")
     out_ref[...] = own_faces(field_ref[...], faces_ref[...])
 
@@ -316,6 +374,11 @@
     def _run():
         summed = out_ref[...] + across_faces(faces_ref[...], far_ref[1], near_ref[1])
         out_ref[...] = apply_inverse(table_ref, scratch, right_ref[...] - summed)
+
+    if begin is not None:
+        @pl.when(core != lead)
+        def _square():
+            square(begin, table_ref, square_ref, scratch)
 
 
 def ends_kernel(lead, sourced, count, *refs):
@@ -365,14 +428,25 @@
     return jnp.where(low_half(), before, swap_halves(gain * before + residual))
 
 
-def restart_kernel(
-    lead, count, sums_ref, end_ref, gain_ref, table_ref, shift_ref, coarse_ref, field_ref, scratch
-):
+def restart_kernel(lead, sums_ref, end_ref, gain_ref, table_ref, field_ref, scratch):
+    @pl.when(lax.axis_index("c") == lead)
+    def _field():
+        before = scanned(sums_ref.shape[0], sums_ref, sums_ref)
+        shift = shifted(before, gain_ref[...], end_ref[...])
+        field_ref[...] = apply_inverse(table_ref, scratch, shift)
+
+    @pl.when(lax.axis_index("c") != lead)
+    def _later():
+        field_ref[...] = jnp.zeros(FIELD, F32)
+
+
+def late_restart_kernel(lead, field_ref, sums_ref, end_ref, gain_ref, faces_ref, table_ref, field_out,
+                        ahead_ref, shift_ref, coarse_ref, scratch):
     gain, end = gain_ref[...], end_ref[...]
-    shift = shifted(scanned(count, sums_ref, sums_ref), gain, end)
+    shift = shifted(scanned(sums_ref.shape[0], sums_ref, sums_ref), gain, end)
     shift_ref[...] = shift
     coarse_ref[...] = gain * shift + end
-    begin(lead, shift, table_ref, field_ref, scratch)
+    late_kernel(lead, field_ref, shift_ref, faces_ref, table_ref, field_out, ahead_ref, scratch)
 
 
 def finish_kernel(count, sums_ref, gains_ref, residual_ref, gain_ref, coarse_ref, end_ref, out_ref, _):
@@ -417,6 +491,7 @@
         near = lax.ppermute(x, "c", [(1 - to, to)])
         return vmem(near), vmem(far)
 
+    lead, other = 0, 1
     field, pair_shape = (FIELD, F32), ((2,) + FIELD, F32)
     index, raw = ((8, LANES), jnp.int32), (face_blocks, block_inverse)
     own, sent, start, mine, place, *raw = call(
@@ -433,62 +508,90 @@
     )
     operator = faces, table = vmem(faces), vmem(table)
     sources, gain, begun, right = call(
-        functools.partial(first_kernel, 0), "first", [((STEPS,) + FIELD, F32), field, field, field],
+        functools.partial(first_kernel, lead), "first", [((STEPS,) + FIELD, F32), field, field, field],
         vmem(own), vmem(got), vmem(start), table,
     )
     sources, gain = vmem(sources), vmem(gain)
 
-    def evolve(lead, now, right, sourced, shift):
-        other = 1 - lead
-        right = vmem(right)
+    def evolve(now, right=None, restart=(), squared=None):
+        sourced = squared is None
         now = vmem(now)
         near, far = halo(now, other)
-        now, ahead = call(
-            functools.partial(late_kernel, lead), "late", [field, field], now, right, *operator
-        )
+        if sourced:
+            right = vmem(right)
+            now, ahead = call(
+                functools.partial(late_kernel, lead), "late", [field] * 2, now, right, *operator
+            )
+        else:
+            now, ahead, right, coarse = call(
+                functools.partial(late_restart_kernel, lead), "late", [field] * 4, now, *restart,
+                *operator,
+            )
+            right = shift = vmem(right)
         (pair,) = call(
             functools.partial(open_kernel, lead), "open", [pair_shape],
-            vmem(now), right, vmem(ahead), near, far, faces, table,
+            vmem(now), right, vmem(ahead), near, far, *operator,
         )
         for stage in range(STAGES - 1):
             active = (lead, other)[stage % 2]
             pair = vmem(pair)
             near, far = halo(pair, active)
-            (ahead,) = call(
-                functools.partial(ahead_kernel, active), "ahead", [field], pair, faces
-            )
-            ahead = vmem(ahead)
-            if stage < STAGES - 2:
-                pair, right = call(
-                    functools.partial(advance_kernel, stage, active, sourced), "advance",
-                    [pair_shape, field], pair, right, ahead, near, far, *operator, sources,
+            if sourced:
+                ahead, squared = call(
+                    functools.partial(ahead_square_kernel, active, stage // 2 * SQUARED), "ahead",
+                    [field, square_shape], pair, *operator, *(() if stage == 0 else (squared,)),
+                    alias={} if stage == 0 else {3: 1},
+                )
+                squared = vmem(squared)
+            else:
+                left = active == other and stage < STAGES - 2
+                ahead, right = call(
+                    functools.partial(ahead_right_kernel, active, left), "ahead", [field] * 2,
+                    pair, right, *operator,
                 )
                 right = vmem(right)
-        (now,) = call(
-            functools.partial(last_kernel, lead), "last", [field],
-            pair, right, ahead, near, far, faces, table,
-        )
+            ahead = vmem(ahead)
+            args = pair, right, ahead, near, far, *operator
+            if stage < STAGES - 2:
+                if sourced:
+                    pair, right = call(
+                        functools.partial(advance_kernel, stage, active, True), "advance",
+                        [pair_shape, field], *args, sources,
+                    )
+                else:
+                    pair, right = call(
+                        functools.partial(advance_squared_kernel, stage, active), "advance",
+                        [pair_shape, field], *args, squared, scratch=(FIELD, FIELD),
+                    )
+                right = vmem(right)
+        (now,) = call(functools.partial(last_kernel, lead), "last", [field], *args)
         now = vmem(now)
-        tail_halo = near, far
+        args = now, right, near, far, *operator
         near, far = halo(now, other)
-        (tail,) = call(
-            functools.partial(tail_kernel, lead), "tail", [field], now, right, *tail_halo, *operator
-        )
+        if sourced:
+            tail, squared = call(
+                functools.partial(tail_kernel, lead, VALUES - SQUARED), "tail",
+                [field, square_shape], *args, squared, alias={6: 1},
+            )
+        else:
+            (tail,) = call(functools.partial(tail_kernel, lead, None), "tail", [field], *args)
         rows = VALUES if sourced else VALUES // 2
         residual, chunk = call(
             functools.partial(ends_kernel, lead, sourced, count), "ends",
             [field, ((count, rows, LANES), F32)],
-            right, vmem(tail), near, far, faces, table, gain, *shift, scratch=(FIELD, FIELD),
+            right, vmem(tail), near, far, *operator, gain, *(() if sourced else (shift,)),
+            scratch=(FIELD, FIELD),
         )
-        return vmem(residual), vmem(lax.all_to_all(chunk, "q", 0, 0))
-
-    end, gains = evolve(0, begun, right, True, ())
-    shift, coarse, begun = call(
-        functools.partial(restart_kernel, 0, count), "restart", [field, field, field],
-        gains, end, gain, table,
-    )
-    shift = vmem(shift)
-    residual, sums = evolve(0, begun, shift, False, (shift,))
+        gathered = vmem(lax.all_to_all(chunk, "q", 0, 0))
+        return vmem(residual), gathered, vmem(squared) if sourced else coarse
+
+    square_shape = ((VALUES,) + FIELD, F32)
+    end, gains, squared = evolve(begun, right)
+    restart = gains, end, gain
+    (begun,) = call(
+        functools.partial(restart_kernel, lead), "restart", [field], *restart, table
+    )
+    residual, sums, coarse = evolve(begun, restart=restart, squared=squared)
     end, sent = call(
         functools.partial(finish_kernel, count), "finish", [field, field],
         sums, gains, residual, gain, vmem(coarse),

time: 145 us -> 144 us (level)
  waiting for transfers between devices: 46.2 us -> 36.7 us
  Pallas kernels: 14.8 us -> 23.8 us
    ppermute x18, waiting for transfers between devices: 25.7 us -> 16.2 us  [halo(): far = lax.ppermute(x, ('c', 'space'), across)]
    pallas_call x42, Pallas kernels: 14.8 us -> 23.8 us  [call(): pl.pallas_call(kernel, out_shape=shapes, in_specs=[pl.BlockSpec(memory_sp...]
  transfers between devices with their start and end apart: 38 -> 38, of which waited for: 29 -> 29; matrix products, arithmetic and copies ran while one was open for 0% -> 0% of each run, Pallas kernels for 3% -> 10%
where the time goes in v6:
time: 144 us; the launch traced here: 143 us
  starting transfers between devices  53.4 us (37%)
  waiting for transfers between devices  36.7 us (25%)
  blocking collectives  27.7 us (19%)
  Pallas kernels  23.8 us (17%)
    all_to_all x2, blocking collectives, evolve(): gathered = vmem(lax.all_to_all(chunk, 'q', 0, 0))  27.7 us
    ppermute x18, starting transfers between devices, halo(): near = lax.ppermute(x, 'c', [(1 - to, to)])  24.2 us
    pallas_call x42, Pallas kernels, call(): pl.pallas_call(kernel, out_shape=shapes, in_specs=[pl.BlockSpec(memory_sp...  23.8 us
    ppermute x18, starting transfers between devices, halo(): far = lax.ppermute(x, ('c', 'space'), across)  23.2 us
    ppermute x18, waiting for transfers between devices, halo(): near = lax.ppermute(x, 'c', [(1 - to, to)])  19.7 us
    ppermute x18, waiting for transfers between devices, halo(): far = lax.ppermute(x, ('c', 'space'), across)  16.2 us
    ppermute x2, starting transfers between devices, swap_cores(): return lax.ppermute(x, 'c', [(0, 1), (1, 0)])  5.98 us
  transfers between devices with their start and end apart: 38, of which 29 were waited for; matrix products, arithmetic and copies ran while one was open for 0% of the time, Pallas kernels for 10%

profile of v6, /device:TPU:385, one launch (start us, length us, event | category | flops | bytes accessed | tf_op | source)
XLA Modules:
  0.0 142.9 jit_solution(12184239542856054633)
XLA Ops:
  0.6 1.9 %share.1 = (f32[5,64,128]{2,1,0:T(8,128)S(1)}, f32[3,64,128]{2,1,0:T(8,128)S(1)}, f32[64,128]{1,0:T(8,128)S(1)}, s32[8,128]{1,0:T(8,128)S(1)}, s32[8,128]{1,0:T(...) custom-call(s32[6,128]{1,0:T(8,128)} %neighbor_any.1, f32[4,64,128]{2,1,0:T(8,128)} %forcing_any.1, ...), custom_call_target="tpu_custom_call" | custom-call | flops 4194304 | bytes 1048576 | tf_op jit(solution)/shard_map/share/pallas_call | solution.py:42
  2.5 2.6 %collective-permute-start = (f32[3,64,128]{2,1,0:T(8,128)S(1)}, f32[3,64,128]{2,1,0:T(8,128)S(1)}, u32[]{:S(2)}, u32[]{:S(2)}) collective-permute-start(f32[3,64,128]{2,1,0:T(8,128)S(1)} %get-tuple-element.82), channel_id=1, source_target_pairs={{0,16},{16,0},{1,17},{17,1},{2,18},{18,2},{3,19},{19,3},{4,20},{20... | collective-permute-start | bytes 294920 | tf_op jit(solution)/shard_map/ppermute | solution.py:483
  5.1 1.5 %tables.1 = (bf16[128,384]{1,0:T(8,128)(2,1)S(1)}, f32[64,64,128]{2,1,0:T(8,128)S(1)}) custom-call(s32[8,128]{1,0:T(8,128)S(1)} %get-tuple-element.84.mine_ref, f32[6,64,64]{2,1,0:T(8,128)S(1)} %get-tuple-element.85.blocks_ref, f32[64,64,128]{2,1,0:T(8,128)S(1)} %get-tuple-element.86.inverse_ref), custom_call_target="tpu_custom_call" | custom-call | flops 4194304 | bytes 1048576 | tf_op jit(solution)/shard_map/tables/pallas_call | solution.py:42
  9.8 2.2 %collective-permute-done.2.far_ref = f32[64,128]{1,0:T(8,128)S(1)} collective-permute-done((f32[64,128]{1,0:T(8,128)S(1)}, f32[64,128]{1,0:T(8,128)S(1)}, u32[]{:S(2)}, u32[]{:S(2)}) %collective-permute-start.2) | collective-permute-done | bytes 32800 | tf_op jit(solution)/shard_map/ppermute | solution.py:490
  14.6 1.8 %collective-permute-start.3 = (f32[2,64,128]{2,1,0:T(8,128)S(1)}, f32[2,64,128]{2,1,0:T(8,128)S(1)}, u32[]{:S(2)}, u32[]{:S(2)}) collective-permute-start(f32[2,64,128]{2,1,0:T(8,128)S(1)} %open.2.pair_ref), channel_id=1, source_target_pairs={{16,0},{17,1},{18,2},{19,3},{20,4},{21,5},{22,6},{23,7},{24,8},{25... | collective-permute-start | bytes 196616 | tf_op jit(solution)/shard_map/ppermute | solution.py:491
  19.8 2.5 %ahead.15 = (f32[64,128]{1,0:T(8,128)S(1)}, f32[64,64,128]{2,1,0:T(8,128)S(1)}) custom-call(f32[2,64,128]{2,1,0:T(8,128)S(1)} %get-tuple-element.95.pair_ref, bf16[128,384]{1,0:T(8,128)(2,1)S(1)} %get-tuple-element.90.faces_ref.refs_4_, f32[64,64,128]{2,1,0:T(8,128)S(1)} %get-tuple-element.87.table_ref.refs_5_, ...), custom_call_target="tpu_custom_call", output_to_operand_aliasing={{1}: (3, {})} | custom-call | flops 4194304 | bytes 1048576 | tf_op jit(solution)/shard_map/ahead/pallas_call | solution.py:42
  22.8 1.3 collective-permute-done.5.near_ref
  25.0 1.3 collective-permute-start.8
  31.1 2.5 %ahead.17 = (f32[64,128]{1,0:T(8,128)S(1)}, f32[64,64,128]{2,1,0:T(8,128)S(1)}) custom-call(f32[2,64,128]{2,1,0:T(8,128)S(1)} %get-tuple-element.103.pair_ref, bf16[128,384]{1,0:T(8,128)(2,1)S(1)} %get-tuple-element.90.faces_ref.refs_4_, f32[64,64,128]{2,1,0:T(8,128)S(1)} %get-tuple-element.87.table_ref.refs_5_, ...), custom_call_target="tpu_custom_call", output_to_operand_aliasing={{1}: (3, {})} | custom-call | flops 4194304 | bytes 1048576 | tf_op jit(solution)/shard_map/ahead/pallas_call | solution.py:42
  42.3 2.5 %ahead.19 = (f32[64,128]{1,0:T(8,128)S(1)}, f32[64,64,128]{2,1,0:T(8,128)S(1)}) custom-call(f32[2,64,128]{2,1,0:T(8,128)S(1)} %get-tuple-element.111.pair_ref, bf16[128,384]{1,0:T(8,128)(2,1)S(1)} %get-tuple-element.90.faces_ref.refs_4_, f32[64,64,128]{2,1,0:T(8,128)S(1)} %get-tuple-element.87.table_ref.refs_5_, ...), custom_call_target="tpu_custom_call", output_to_operand_aliasing={{1}: (3, {})} | custom-call | flops 4194304 | bytes 1048576 | tf_op jit(solution)/shard_map/ahead/pallas_call | solution.py:42
  53.5 2.5 %tail.2 = (f32[64,128]{1,0:T(8,128)S(1)}, f32[64,64,128]{2,1,0:T(8,128)S(1)}) custom-call(f32[64,128]{1,0:T(8,128)S(1)} %last.2.field_ref, f32[64,128]{1,0:T(8,128)S(1)} %get-tuple-element.115.right_ref.refs_0_, f32[2,64,128]{2,1,0:T(8,128)S(1)} %collective-permute-done.15.near_ref, ...), custom_call_target="tpu_custom_call", output_to_operand_aliasing={{1}: (6, {})} | custom-call | flops 4194304 | bytes 1048576 | tf_op jit(solution)/shard_map/tail/pallas_call | solution.py:42
  56.2 1.5 %collective-permute-done.17.refs_2_ = f32[64,128]{1,0:T(8,128)S(1)} collective-permute-done((f32[64,128]{1,0:T(8,128)S(1)}, f32[64,128]{1,0:T(8,128)S(1)}, u32[]{:S(2)}, u32[]{:S(2)}) %collective-permute-start.17) | collective-permute-done | bytes 32800 | tf_op jit(solution)/shard_map/ppermute | solution.py:491
  58.2 16.8 %all_to_all.10.sums_ref.gains_ref = f32[16,64,128]{2,1,0:T(8,128)S(1)} all-to-all(f32[16,64,128]{2,1,0:T(8,128)S(1)} %get-tuple-element.122), channel_id=1, replica_groups=mesh['q'=16,'c'=2,'space'=16] {'q'}, dimensions={0} | all-to-all | bytes 1048576 | tf_op jit(solution)/shard_map/all_to_all | solution.py:585
  78.2 2.0 %collective-permute-done.20.far_ref = f32[64,128]{1,0:T(8,128)S(1)} collective-permute-done((f32[64,128]{1,0:T(8,128)S(1)}, f32[64,128]{1,0:T(8,128)S(1)}, u32[]{:S(2)}, u32[]{:S(2)}) %collective-permute-start.20) | collective-permute-done | bytes 32800 | tf_op jit(solution)/shard_map/ppermute | solution.py:490
  80.2 1.3 collective-permute-done.19.near_ref
  83.1 1.8 %collective-permute-start.21 = (f32[2,64,128]{2,1,0:T(8,128)S(1)}, f32[2,64,128]{2,1,0:T(8,128)S(1)}, u32[]{:S(2)}, u32[]{:S(2)}) collective-permute-start(f32[2,64,128]{2,1,0:T(8,128)S(1)} %open.3.pair_ref), channel_id=1, source_target_pairs={{16,0},{17,1},{18,2},{19,3},{20,4},{21,5},{22,6},{23,7},{24,8},{25... | collective-permute-start | bytes 196616 | tf_op jit(solution)/shard_map/ppermute | solution.py:491
  88.7 2.7 %collective-permute-done.24.far_ref = f32[2,64,128]{2,1,0:T(8,128)S(1)} collective-permute-done((f32[2,64,128]{2,1,0:T(8,128)S(1)}, f32[2,64,128]{2,1,0:T(8,128)S(1)}, u32[]{:S(2)}, u32[]{:S(2)}) %collective-permute-start.24) | collective-permute-done | bytes 65568 | tf_op jit(solution)/shard_map/ppermute | solution.py:490
  91.4 1.3 collective-permute-done.23.near_ref
  99.9 2.7 %collective-permute-done.28.far_ref = f32[2,64,128]{2,1,0:T(8,128)S(1)} collective-permute-done((f32[2,64,128]{2,1,0:T(8,128)S(1)}, f32[2,64,128]{2,1,0:T(8,128)S(1)}, u32[]{:S(2)}, u32[]{:S(2)}) %collective-permute-start.28) | collective-permute-done | bytes 65568 | tf_op jit(solution)/shard_map/ppermute | solution.py:490
  111.0 2.7 %collective-permute-done.32.far_ref = f32[2,64,128]{2,1,0:T(8,128)S(1)} collective-permute-done((f32[2,64,128]{2,1,0:T(8,128)S(1)}, f32[2,64,128]{2,1,0:T(8,128)S(1)}, u32[]{:S(2)}, u32[]{:S(2)}) %collective-permute-start.32) | collective-permute-done | bytes 65568 | tf_op jit(solution)/shard_map/ppermute | solution.py:490
  122.1 2.4 %collective-permute-done.36.refs_3_ = f32[64,128]{1,0:T(8,128)S(1)} collective-permute-done((f32[64,128]{1,0:T(8,128)S(1)}, f32[64,128]{1,0:T(8,128)S(1)}, u32[]{:S(2)}, u32[]{:S(2)}) %collective-permute-start.36) | collective-permute-done | bytes 32800 | tf_op jit(solution)/shard_map/ppermute | solution.py:490
  124.5 1.5 %collective-permute-done.35.refs_2_ = f32[64,128]{1,0:T(8,128)S(1)} collective-permute-done((f32[64,128]{1,0:T(8,128)S(1)}, f32[64,128]{1,0:T(8,128)S(1)}, u32[]{:S(2)}, u32[]{:S(2)}) %collective-permute-start.35) | collective-permute-done | bytes 32800 | tf_op jit(solution)/shard_map/ppermute | solution.py:491
  126.6 11.0 %all_to_all.11.sums_ref = f32[16,32,128]{2,1,0:T(8,128)S(1)} all-to-all(f32[16,32,128]{2,1,0:T(8,128)S(1)} %get-tuple-element.154), channel_id=1, replica_groups=mesh['q'=16,'c'=2,'space'=16] {'q'}, dimensions={0} | all-to-all | bytes 524288 | tf_op jit(solution)/shard_map/all_to_all | solution.py:585
  137.9 3.4 %collective-permute-start.37 = (f32[64,128]{1,0:T(8,128)S(1)}, f32[64,128]{1,0:T(8,128)S(1)}, u32[]{:S(2)}, u32[]{:S(2)}) collective-permute-start(f32[64,128]{1,0:T(8,128)S(1)} %get-tuple-element.158), channel_id=1, source_target_pairs={{0,16},{16,0},{1,17},{17,1},{2,18},{18,2},{3,19},{19,3},{4,20},{20... | collective-permute-start | bytes 98312 | tf_op jit(solution)/shard_map/ppermute | solution.py:483
  (96 shorter events, 67.7 us)
Async XLA Ops:
  2.5 4.1 %collective-permute-start = (f32[3,64,128]{2,1,0:T(8,128)S(1)}, f32[3,64,128]{2,1,0:T(8,128)S(1)}, u32[]{:S(2)}, u32[]{:S(2)}) collective-permute-start(f32[3,64,128]{2,1,0:T(8,128)S(1)} %get-tuple-element.82), channel_id=1, source_target_pairs={{0,16},{16,0},{1,17},{17,1},{2,18},{18,2},{3,19},{19,3},{4,20},{20... | collective-permute-start | bytes 294920 | tf_op jit(solution)/shard_map/ppermute | solution.py:483
  6.8 5.2 %collective-permute-start.2 = (f32[64,128]{1,0:T(8,128)S(1)}, f32[64,128]{1,0:T(8,128)S(1)}, u32[]{:S(2)}, u32[]{:S(2)}) collective-permute-start(f32[64,128]{1,0:T(8,128)S(1)} %get-tuple-element.88.field_ref), channel_id=1, source_target_pairs={{1,16},{2,17},{3,18},{4,19},{5,20},{6,21},{7,22},{8,23},{9,24},{10... | collective-permute-start | bytes 98312 | tf_op jit(solution)/shard_map/ppermute | solution.py:490
  8.1 4.9 %collective-permute-start.1 = (f32[64,128]{1,0:T(8,128)S(1)}, f32[64,128]{1,0:T(8,128)S(1)}, u32[]{:S(2)}, u32[]{:S(2)}) collective-permute-start(f32[64,128]{1,0:T(8,128)S(1)} %get-tuple-element.88.field_ref), channel_id=1, source_target_pairs={{0,16},{1,17},{2,18},{3,19},{4,20},{5,21},{6,22},{7,23},{8,24},{9,... | collective-permute-start | bytes 98312 | tf_op jit(solution)/shard_map/ppermute | solution.py:491
  13.3 3.1 %collective-permute-start.4 = (f32[2,64,128]{2,1,0:T(8,128)S(1)}, f32[2,64,128]{2,1,0:T(8,128)S(1)}, u32[]{:S(2)}, u32[]{:S(2)}) collective-permute-start(f32[2,64,128]{2,1,0:T(8,128)S(1)} %open.2.pair_ref), channel_id=1, source_target_pairs={{16,1},{17,2},{18,3},{19,4},{20,5},{21,6},{22,7},{23,8},{24,9},{25... | collective-permute-start | bytes 196616 | tf_op jit(solution)/shard_map/ppermute | solution.py:490
  17.2 5.6 %collective-permute-start.6 = (f32[2,64,128]{2,1,0:T(8,128)S(1)}, f32[2,64,128]{2,1,0:T(8,128)S(1)}, u32[]{:S(2)}, u32[]{:S(2)}) collective-permute-start(f32[2,64,128]{2,1,0:T(8,128)S(1)} %get-tuple-element.95.pair_ref), channel_id=1, source_target_pairs={{1,16},{2,17},{3,18},{4,19},{5,20},{6,21},{7,22},{8,23},{9,24},{10... | collective-permute-start | bytes 196616 | tf_op jit(solution)/shard_map/ppermute | solution.py:490
  18.5 5.6 %collective-permute-start.5 = (f32[2,64,128]{2,1,0:T(8,128)S(1)}, f32[2,64,128]{2,1,0:T(8,128)S(1)}, u32[]{:S(2)}, u32[]{:S(2)}) collective-permute-start(f32[2,64,128]{2,1,0:T(8,128)S(1)} %get-tuple-element.95.pair_ref), channel_id=1, source_target_pairs={{0,16},{1,17},{2,18},{3,19},{4,20},{5,21},{6,22},{7,23},{8,24},{9,... | collective-permute-start | bytes 196616 | tf_op jit(solution)/shard_map/ppermute | solution.py:491
  28.5 5.6 %collective-permute-start.10 = (f32[2,64,128]{2,1,0:T(8,128)S(1)}, f32[2,64,128]{2,1,0:T(8,128)S(1)}, u32[]{:S(2)}, u32[]{:S(2)}) collective-permute-start(f32[2,64,128]{2,1,0:T(8,128)S(1)} %get-tuple-element.103.pair_ref), channel_id=1, source_target_pairs={{1,16},{2,17},{3,18},{4,19},{5,20},{6,21},{7,22},{8,23},{9,24},{10... | collective-permute-start | bytes 196616 | tf_op jit(solution)/shard_map/ppermute | solution.py:490
  29.8 5.5 %collective-permute-start.9 = (f32[2,64,128]{2,1,0:T(8,128)S(1)}, f32[2,64,128]{2,1,0:T(8,128)S(1)}, u32[]{:S(2)}, u32[]{:S(2)}) collective-permute-start(f32[2,64,128]{2,1,0:T(8,128)S(1)} %get-tuple-element.103.pair_ref), channel_id=1, source_target_pairs={{0,16},{1,17},{2,18},{3,19},{4,20},{5,21},{6,22},{7,23},{8,24},{9,... | collective-permute-start | bytes 196616 | tf_op jit(solution)/shard_map/ppermute | solution.py:491
  39.7 5.6 %collective-permute-start.14 = (f32[2,64,128]{2,1,0:T(8,128)S(1)}, f32[2,64,128]{2,1,0:T(8,128)S(1)}, u32[]{:S(2)}, u32[]{:S(2)}) collective-permute-start(f32[2,64,128]{2,1,0:T(8,128)S(1)} %get-tuple-element.111.pair_ref), channel_id=1, source_target_pairs={{1,16},{2,17},{3,18},{4,19},{5,20},{6,21},{7,22},{8,23},{9,24},{10... | collective-permute-start | bytes 196616 | tf_op jit(solution)/shard_map/ppermute | solution.py:490
  41.0 5.5 %collective-permute-start.13 = (f32[2,64,128]{2,1,0:T(8,128)S(1)}, f32[2,64,128]{2,1,0:T(8,128)S(1)}, u32[]{:S(2)}, u32[]{:S(2)}) collective-permute-start(f32[2,64,128]{2,1,0:T(8,128)S(1)} %get-tuple-element.111.pair_ref), channel_id=1, source_target_pairs={{0,16},{1,17},{2,18},{3,19},{4,20},{5,21},{6,22},{7,23},{8,24},{9,... | collective-permute-start | bytes 196616 | tf_op jit(solution)/shard_map/ppermute | solution.py:491
  50.9 5.2 %collective-permute-start.18 = (f32[64,128]{1,0:T(8,128)S(1)}, f32[64,128]{1,0:T(8,128)S(1)}, u32[]{:S(2)}, u32[]{:S(2)}) collective-permute-start(f32[64,128]{1,0:T(8,128)S(1)} %last.2.field_ref), channel_id=1, source_target_pairs={{1,16},{2,17},{3,18},{4,19},{5,20},{6,21},{7,22},{8,23},{9,24},{10... | collective-permute-start | bytes 98312 | tf_op jit(solution)/shard_map/ppermute | solution.py:490
  52.2 5.5 %collective-permute-start.17 = (f32[64,128]{1,0:T(8,128)S(1)}, f32[64,128]{1,0:T(8,128)S(1)}, u32[]{:S(2)}, u32[]{:S(2)}) collective-permute-start(f32[64,128]{1,0:T(8,128)S(1)} %last.2.field_ref), channel_id=1, source_target_pairs={{0,16},{1,17},{2,18},{3,19},{4,20},{5,21},{6,22},{7,23},{8,24},{9,... | collective-permute-start | bytes 98312 | tf_op jit(solution)/shard_map/ppermute | solution.py:491
  75.0 5.2 %collective-permute-start.20 = (f32[64,128]{1,0:T(8,128)S(1)}, f32[64,128]{1,0:T(8,128)S(1)}, u32[]{:S(2)}, u32[]{:S(2)}) collective-permute-start(f32[64,128]{1,0:T(8,128)S(1)} %restart.1.field_ref), channel_id=1, source_target_pairs={{1,16},{2,17},{3,18},{4,19},{5,20},{6,21},{7,22},{8,23},{9,24},{10... | collective-permute-start | bytes 98312 | tf_op jit(solution)/shard_map/ppermute | solution.py:490
  76.3 5.3 %collective-permute-start.19 = (f32[64,128]{1,0:T(8,128)S(1)}, f32[64,128]{1,0:T(8,128)S(1)}, u32[]{:S(2)}, u32[]{:S(2)}) collective-permute-start(f32[64,128]{1,0:T(8,128)S(1)} %restart.1.field_ref), channel_id=1, source_target_pairs={{0,16},{1,17},{2,18},{3,19},{4,20},{5,21},{6,22},{7,23},{8,24},{9,... | collective-permute-start | bytes 98312 | tf_op jit(solution)/shard_map/ppermute | solution.py:491
  81.8 3.1 %collective-permute-start.22 = (f32[2,64,128]{2,1,0:T(8,128)S(1)}, f32[2,64,128]{2,1,0:T(8,128)S(1)}, u32[]{:S(2)}, u32[]{:S(2)}) collective-permute-start(f32[2,64,128]{2,1,0:T(8,128)S(1)} %open.3.pair_ref), channel_id=1, source_target_pairs={{16,1},{17,2},{18,3},{19,4},{20,5},{21,6},{22,7},{23,8},{24,9},{25... | collective-permute-start | bytes 196616 | tf_op jit(solution)/shard_map/ppermute | solution.py:490
  85.8 5.6 %collective-permute-start.24 = (f32[2,64,128]{2,1,0:T(8,128)S(1)}, f32[2,64,128]{2,1,0:T(8,128)S(1)}, u32[]{:S(2)}, u32[]{:S(2)}) collective-permute-start(f32[2,64,128]{2,1,0:T(8,128)S(1)} %get-tuple-element.130.pair_ref), channel_id=1, source_target_pairs={{1,16},{2,17},{3,18},{4,19},{5,20},{6,21},{7,22},{8,23},{9,24},{10... | collective-permute-start | bytes 196616 | tf_op jit(solution)/shard_map/ppermute | solution.py:490
  87.1 5.6 %collective-permute-start.23 = (f32[2,64,128]{2,1,0:T(8,128)S(1)}, f32[2,64,128]{2,1,0:T(8,128)S(1)}, u32[]{:S(2)}, u32[]{:S(2)}) collective-permute-start(f32[2,64,128]{2,1,0:T(8,128)S(1)} %get-tuple-element.130.pair_ref), channel_id=1, source_target_pairs={{0,16},{1,17},{2,18},{3,19},{4,20},{5,21},{6,22},{7,23},{8,24},{9,... | collective-permute-start | bytes 196616 | tf_op jit(solution)/shard_map/ppermute | solution.py:491
  97.0 5.6 %collective-permute-start.28 = (f32[2,64,128]{2,1,0:T(8,128)S(1)}, f32[2,64,128]{2,1,0:T(8,128)S(1)}, u32[]{:S(2)}, u32[]{:S(2)}) collective-permute-start(f32[2,64,128]{2,1,0:T(8,128)S(1)} %get-tuple-element.138.pair_ref), channel_id=1, source_target_pairs={{1,16},{2,17},{3,18},{4,19},{5,20},{6,21},{7,22},{8,23},{9,24},{10... | collective-permute-start | bytes 196616 | tf_op jit(solution)/shard_map/ppermute | solution.py:490
  98.3 5.5 %collective-permute-start.27 = (f32[2,64,128]{2,1,0:T(8,128)S(1)}, f32[2,64,128]{2,1,0:T(8,128)S(1)}, u32[]{:S(2)}, u32[]{:S(2)}) collective-permute-start(f32[2,64,128]{2,1,0:T(8,128)S(1)} %get-tuple-element.138.pair_ref), channel_id=1, source_target_pairs={{0,16},{1,17},{2,18},{3,19},{4,20},{5,21},{6,22},{7,23},{8,24},{9,... | collective-permute-start | bytes 196616 | tf_op jit(solution)/shard_map/ppermute | solution.py:491
  108.2 5.6 %collective-permute-start.32 = (f32[2,64,128]{2,1,0:T(8,128)S(1)}, f32[2,64,128]{2,1,0:T(8,128)S(1)}, u32[]{:S(2)}, u32[]{:S(2)}) collective-permute-start(f32[2,64,128]{2,1,0:T(8,128)S(1)} %get-tuple-element.146.pair_ref), channel_id=1, source_target_pairs={{1,16},{2,17},{3,18},{4,19},{5,20},{6,21},{7,22},{8,23},{9,24},{10... | collective-permute-start | bytes 196616 | tf_op jit(solution)/shard_map/ppermute | solution.py:490
  109.5 5.5 %collective-permute-start.31 = (f32[2,64,128]{2,1,0:T(8,128)S(1)}, f32[2,64,128]{2,1,0:T(8,128)S(1)}, u32[]{:S(2)}, u32[]{:S(2)}) collective-permute-start(f32[2,64,128]{2,1,0:T(8,128)S(1)} %get-tuple-element.146.pair_ref), channel_id=1, source_target_pairs={{0,16},{1,17},{2,18},{3,19},{4,20},{5,21},{6,22},{7,23},{8,24},{9,... | collective-permute-start | bytes 196616 | tf_op jit(solution)/shard_map/ppermute | solution.py:491
  119.3 5.2 %collective-permute-start.36 = (f32[64,128]{1,0:T(8,128)S(1)}, f32[64,128]{1,0:T(8,128)S(1)}, u32[]{:S(2)}, u32[]{:S(2)}) collective-permute-start(f32[64,128]{1,0:T(8,128)S(1)} %last.3.field_ref), channel_id=1, source_target_pairs={{1,16},{2,17},{3,18},{4,19},{5,20},{6,21},{7,22},{8,23},{9,24},{10... | collective-permute-start | bytes 98312 | tf_op jit(solution)/shard_map/ppermute | solution.py:490
  120.6 5.5 %collective-permute-start.35 = (f32[64,128]{1,0:T(8,128)S(1)}, f32[64,128]{1,0:T(8,128)S(1)}, u32[]{:S(2)}, u32[]{:S(2)}) collective-permute-start(f32[64,128]{1,0:T(8,128)S(1)} %last.3.field_ref), channel_id=1, source_target_pairs={{0,16},{1,17},{2,18},{3,19},{4,20},{5,21},{6,22},{7,23},{8,24},{9,... | collective-permute-start | bytes 98312 | tf_op jit(solution)/shard_map/ppermute | solution.py:491
  137.9 4.2 %collective-permute-start.37 = (f32[64,128]{1,0:T(8,128)S(1)}, f32[64,128]{1,0:T(8,128)S(1)}, u32[]{:S(2)}, u32[]{:S(2)}) collective-permute-start(f32[64,128]{1,0:T(8,128)S(1)} %get-tuple-element.158), channel_id=1, source_target_pairs={{0,16},{16,0},{1,17},{17,1},{2,18},{18,2},{3,19},{19,3},{4,20},{20... | collective-permute-start | bytes 98312 | tf_op jit(solution)/shard_map/ppermute | solution.py:483
  (14 other events, 34.2 us)

commit v7 on v6

--- a/solution.py
+++ b/solution.py
@@ -16,6 +16,7 @@
 GX = 8
 GY = 8
 SQUARED = 16
+EARLY = 16
 F32 = jnp.float32
 BF16 = jnp.bfloat16
 FIELD = (VALUES, LANES)
@@ -115,8 +116,8 @@
 
 
 def share_kernel(neighbor_any, forcing_any, gain_any, state_any, blocks_any, inverse_any,
-                 own_ref, out_ref, start_ref, mine_ref, place_ref, blocks_ref, inverse_ref,
-                 state_ref, forcing_ref, gain_ref, neighbor_ref, sems):
+                 own_ref, out_ref, start_ref, mine_ref, place_ref, blocks_ref, rest_ref, table_ref,
+                 state_ref, forcing_ref, gain_ref, early_ref, neighbor_ref, sems):
     core = lax.axis_index("c")
     part = VALUES // 8
     first = [
@@ -125,14 +126,20 @@
         pltpu.make_async_copy(gain_any, gain_ref, sems.at[2]),
         pltpu.make_async_copy(state_any, state_ref, sems.at[3]),
     ]
-    later = [pltpu.make_async_copy(blocks_any, blocks_ref, sems.at[4])] + [
-        pltpu.make_async_copy(
-            inverse_any.at[pl.ds(part * k, part)], inverse_ref.at[pl.ds(part * k, part)],
-            sems.at[8 + k],
+    early, later = (
+        [
+            pltpu.make_async_copy(
+                inverse_any.at[pl.ds(begin + part * k, part)], ref.at[pl.ds(part * k, part)],
+                sems.at[8 + begin // part + k],
+            )
+            for k in range(count)
+        ]
+        for begin, ref, count in (
+            (0, early_ref, EARLY // part), (EARLY, rest_ref, (VALUES - EARLY) // part)
         )
-        for k in range(8)
-    ]
-    for copy in first + later:
+    )
+    later.append(pltpu.make_async_copy(blocks_any, blocks_ref, sems.at[4]))
+    for copy in first + early + later:
         copy.start()
     first[0].wait()
     place, order = raster(neighbor_ref[...])
@@ -155,13 +162,18 @@
     for m, field in enumerate(fields):
         own_ref[m] = columns(field, mine)
     start_ref[...] = columns(state_ref[...], mine)
+    for k, copy in enumerate(early):
+        copy.wait()
+        rows = pl.ds(part * k, part)
+        for j in range(VALUES):
+            table_ref[j, rows] = columns(early_ref[rows, j, :], mine)
     for copy in later:
         copy.wait()
 
 
-def tables_kernel(mine_ref, blocks_ref, inverse_ref, faces_ref, table_ref, _):
-    core = lax.axis_index("c")
-    mine = jnp.concatenate([mine_ref[...]] * (VALUES // 8), axis=0)
+def tables_kernel(mine_ref, blocks_ref, rest_ref, _table, faces_ref, table_ref, _):
+    core = lax.axis_index("c")
+    mine = jnp.concatenate([mine_ref[...]] * ((VALUES - EARLY) // 8), axis=0)
     blocks = [blocks_ref[f] for f in range(4)]
     blocks += [
         jnp.where(core == 0, blocks_ref[4], blocks_ref[5]),
@@ -172,7 +184,7 @@
         faces_ref[:VALUES, f * VALUES : (f + 1) * VALUES] = high
         faces_ref[VALUES:, f * VALUES : (f + 1) * VALUES] = low
     for j in range(VALUES):
-        table_ref[j] = columns(inverse_ref[:, j, :], mine)
+        table_ref[j, EARLY:] = columns(rest_ref[:, j, :], mine)
 
 
 def packed(x):
@@ -493,18 +505,19 @@
 
     lead, other = 0, 1
     field, pair_shape = (FIELD, F32), ((2,) + FIELD, F32)
-    index, raw = ((8, LANES), jnp.int32), (face_blocks, block_inverse)
+    index = ((8, LANES), jnp.int32)
+    square_shape = ((VALUES,) + FIELD, F32)
     own, sent, start, mine, place, *raw = call(
         share_kernel, "share",
         [((STEPS + 1,) + FIELD, F32), ((STEPS // 2 + 1,) + FIELD, F32), field, index, index,
-         *((x.shape, x.dtype) for x in raw)],
-        *map(hbm, (neighbor, forcing, coarse_gain, initial_state, *raw)), fetch=True,
-        scratch=(FIELD, forcing.shape, coarse_gain.shape), ints=(neighbor.shape,),
+         (face_blocks.shape, F32), ((VALUES - EARLY,) + FIELD, F32), square_shape],
+        *map(hbm, (neighbor, forcing, coarse_gain, initial_state, face_blocks, block_inverse)),
+        fetch=True, scratch=(FIELD, forcing.shape, coarse_gain.shape, (EARLY,) + FIELD), ints=(neighbor.shape,),
     )
     got = swap_cores(sent)
     faces, table = call(
         tables_kernel, "tables",
-        [((2 * VALUES, 6 * VALUES), BF16), ((VALUES,) + FIELD, F32)], *map(vmem, (mine, *raw)),
+        [((2 * VALUES, 6 * VALUES), BF16), square_shape], *map(vmem, (mine, *raw)), alias={3: 1},
     )
     operator = faces, table = vmem(faces), vmem(table)
     sources, gain, begun, right = call(
@@ -585,7 +598,6 @@
         gathered = vmem(lax.all_to_all(chunk, "q", 0, 0))
         return vmem(residual), gathered, vmem(squared) if sourced else coarse
 
-    square_shape = ((VALUES,) + FIELD, F32)
     end, gains, squared = evolve(begun, right)
     restart = gains, end, gain
     (begun,) = call(

time: 144 us -> 143 us (level)
  no operation moved by 1% of the time
where the time goes in v7:
time: 143 us; the launch traced here: 142 us
  starting transfers between devices  53.4 us (37%)
  waiting for transfers between devices  36.5 us (26%)
  blocking collectives  27.7 us (19%)
  Pallas kernels  23.4 us (16%)
    all_to_all x2, blocking collectives, evolve(): gathered = vmem(lax.all_to_all(chunk, 'q', 0, 0))  27.7 us
    ppermute x18, starting transfers between devices, halo(): near = lax.ppermute(x, 'c', [(1 - to, to)])  24.2 us
    pallas_call x42, Pallas kernels, call(): pl.pallas_call(kernel, out_shape=shapes, in_specs=[pl.BlockSpec(memory_sp...  23.4 us
    ppermute x18, starting transfers between devices, halo(): far = lax.ppermute(x, ('c', 'space'), across)  23.2 us
    ppermute x18, waiting for transfers between devices, halo(): near = lax.ppermute(x, 'c', [(1 - to, to)])  19.7 us
    ppermute x18, waiting for transfers between devices, halo(): far = lax.ppermute(x, ('c', 'space'), across)  16 us
    ppermute x2, starting transfers between devices, swap_cores(): return lax.ppermute(x, 'c', [(0, 1), (1, 0)])  5.98 us
  transfers between devices with their start and end apart: 38, of which 29 were waited for; matrix products, arithmetic and copies ran while one was open for 0% of the time, Pallas kernels for 10%

profile of v7, /device:TPU:385, one launch (start us, length us, event | category | flops | bytes accessed | tf_op | source)
XLA Modules:
  0.0 142.3 jit_solution(10022108038153213529)
XLA Ops:
  0.6 1.8 %share.1 = (f32[5,64,128]{2,1,0:T(8,128)S(1)}, f32[3,64,128]{2,1,0:T(8,128)S(1)}, f32[64,128]{1,0:T(8,128)S(1)}, s32[8,128]{1,0:T(8,128)S(1)}, s32[8,128]{1,0:T(...) custom-call(s32[6,128]{1,0:T(8,128)} %neighbor_any.1, ...), custom_call_target="tpu_custom_call" | custom-call | flops 4194304 | bytes 1048576 | tf_op jit(solution)/shard_map/share/pallas_call | solution.py:43
  2.5 2.6 %collective-permute-start = (f32[3,64,128]{2,1,0:T(8,128)S(1)}, f32[3,64,128]{2,1,0:T(8,128)S(1)}, u32[]{:S(2)}, u32[]{:S(2)}) collective-permute-start(f32[3,64,128]{2,1,0:T(8,128)S(1)} %get-tuple-element.83), channel_id=1, source_target_pairs={{0,16},{16,0},{1,17},{17,1},{2,18},{18,2},{3,19},{19,3},{4,20},{20... | collective-permute-start | bytes 294920 | tf_op jit(solution)/shard_map/ppermute | solution.py:495
  9.3 2.2 %collective-permute-done.2.far_ref = f32[64,128]{1,0:T(8,128)S(1)} collective-permute-done((f32[64,128]{1,0:T(8,128)S(1)}, f32[64,128]{1,0:T(8,128)S(1)}, u32[]{:S(2)}, u32[]{:S(2)}) %collective-permute-start.2) | collective-permute-done | bytes 32800 | tf_op jit(solution)/shard_map/ppermute | solution.py:502
  12.7 1.3 collective-permute-start.4
  14.0 1.8 %collective-permute-start.3 = (f32[2,64,128]{2,1,0:T(8,128)S(1)}, f32[2,64,128]{2,1,0:T(8,128)S(1)}, u32[]{:S(2)}, u32[]{:S(2)}) collective-permute-start(f32[2,64,128]{2,1,0:T(8,128)S(1)} %open.2.pair_ref), channel_id=1, source_target_pairs={{16,0},{17,1},{18,2},{19,3},{20,4},{21,5},{22,6},{23,7},{24,8},{25... | collective-permute-start | bytes 196616 | tf_op jit(solution)/shard_map/ppermute | solution.py:503
  19.3 2.5 %ahead.15 = (f32[64,128]{1,0:T(8,128)S(1)}, f32[64,64,128]{2,1,0:T(8,128)S(1)}) custom-call(f32[2,64,128]{2,1,0:T(8,128)S(1)} %get-tuple-element.97.pair_ref, bf16[128,384]{1,0:T(8,128)(2,1)S(1)} %get-tuple-element.92.faces_ref.refs_4_, f32[64,64,128]{2,1,0:T(8,128)S(1)} %get-tuple-element.89.table_ref.refs_5_, ...), custom_call_target="tpu_custom_call", output_to_operand_aliasing={{1}: (3, {})} | custom-call | flops 4194304 | bytes 1048576 | tf_op jit(solution)/shard_map/ahead/pallas_call | solution.py:43
  22.3 1.3 collective-permute-done.5.near_ref
  25.8 1.3 collective-permute-start.7
  30.6 2.5 %ahead.17 = (f32[64,128]{1,0:T(8,128)S(1)}, f32[64,64,128]{2,1,0:T(8,128)S(1)}) custom-call(f32[2,64,128]{2,1,0:T(8,128)S(1)} %get-tuple-element.105.pair_ref, bf16[128,384]{1,0:T(8,128)(2,1)S(1)} %get-tuple-element.92.faces_ref.refs_4_, f32[64,64,128]{2,1,0:T(8,128)S(1)} %get-tuple-element.89.table_ref.refs_5_, ...), custom_call_target="tpu_custom_call", output_to_operand_aliasing={{1}: (3, {})} | custom-call | flops 4194304 | bytes 1048576 | tf_op jit(solution)/shard_map/ahead/pallas_call | solution.py:43
  41.8 2.5 %ahead.19 = (f32[64,128]{1,0:T(8,128)S(1)}, f32[64,64,128]{2,1,0:T(8,128)S(1)}) custom-call(f32[2,64,128]{2,1,0:T(8,128)S(1)} %get-tuple-element.113.pair_ref, bf16[128,384]{1,0:T(8,128)(2,1)S(1)} %get-tuple-element.92.faces_ref.refs_4_, f32[64,64,128]{2,1,0:T(8,128)S(1)} %get-tuple-element.89.table_ref.refs_5_, ...), custom_call_target="tpu_custom_call", output_to_operand_aliasing={{1}: (3, {})} | custom-call | flops 4194304 | bytes 1048576 | tf_op jit(solution)/shard_map/ahead/pallas_call | solution.py:43
  53.0 2.5 %tail.2 = (f32[64,128]{1,0:T(8,128)S(1)}, f32[64,64,128]{2,1,0:T(8,128)S(1)}) custom-call(f32[64,128]{1,0:T(8,128)S(1)} %last.2.field_ref, f32[64,128]{1,0:T(8,128)S(1)} %get-tuple-element.117.right_ref.refs_0_, f32[2,64,128]{2,1,0:T(8,128)S(1)} %collective-permute-done.15.near_ref, ...), custom_call_target="tpu_custom_call", output_to_operand_aliasing={{1}: (6, {})} | custom-call | flops 4194304 | bytes 1048576 | tf_op jit(solution)/shard_map/tail/pallas_call | solution.py:43
  55.6 1.5 %collective-permute-done.17.refs_2_ = f32[64,128]{1,0:T(8,128)S(1)} collective-permute-done((f32[64,128]{1,0:T(8,128)S(1)}, f32[64,128]{1,0:T(8,128)S(1)}, u32[]{:S(2)}, u32[]{:S(2)}) %collective-permute-start.17) | collective-permute-done | bytes 32800 | tf_op jit(solution)/shard_map/ppermute | solution.py:503
  57.7 16.8 %all_to_all.10.sums_ref.gains_ref = f32[16,64,128]{2,1,0:T(8,128)S(1)} all-to-all(f32[16,64,128]{2,1,0:T(8,128)S(1)} %get-tuple-element.124), channel_id=1, replica_groups=mesh['q'=16,'c'=2,'space'=16] {'q'}, dimensions={0} | all-to-all | bytes 1048576 | tf_op jit(solution)/shard_map/all_to_all | solution.py:598
  77.7 2.0 %collective-permute-done.20.far_ref = f32[64,128]{1,0:T(8,128)S(1)} collective-permute-done((f32[64,128]{1,0:T(8,128)S(1)}, f32[64,128]{1,0:T(8,128)S(1)}, u32[]{:S(2)}, u32[]{:S(2)}) %collective-permute-start.20) | collective-permute-done | bytes 32800 | tf_op jit(solution)/shard_map/ppermute | solution.py:502
  79.7 1.3 collective-permute-done.19.near_ref
  82.6 1.8 %collective-permute-start.21 = (f32[2,64,128]{2,1,0:T(8,128)S(1)}, f32[2,64,128]{2,1,0:T(8,128)S(1)}, u32[]{:S(2)}, u32[]{:S(2)}) collective-permute-start(f32[2,64,128]{2,1,0:T(8,128)S(1)} %open.3.pair_ref), channel_id=1, source_target_pairs={{16,0},{17,1},{18,2},{19,3},{20,4},{21,5},{22,6},{23,7},{24,8},{25... | collective-permute-start | bytes 196616 | tf_op jit(solution)/shard_map/ppermute | solution.py:503
  88.3 2.5 %collective-permute-done.24.far_ref = f32[2,64,128]{2,1,0:T(8,128)S(1)} collective-permute-done((f32[2,64,128]{2,1,0:T(8,128)S(1)}, f32[2,64,128]{2,1,0:T(8,128)S(1)}, u32[]{:S(2)}, u32[]{:S(2)}) %collective-permute-start.24) | collective-permute-done | bytes 65568 | tf_op jit(solution)/shard_map/ppermute | solution.py:502
  90.8 1.3 collective-permute-done.23.near_ref
  99.3 2.7 %collective-permute-done.28.far_ref = f32[2,64,128]{2,1,0:T(8,128)S(1)} collective-permute-done((f32[2,64,128]{2,1,0:T(8,128)S(1)}, f32[2,64,128]{2,1,0:T(8,128)S(1)}, u32[]{:S(2)}, u32[]{:S(2)}) %collective-permute-start.28) | collective-permute-done | bytes 65568 | tf_op jit(solution)/shard_map/ppermute | solution.py:502
  110.5 2.7 %collective-permute-done.32.far_ref = f32[2,64,128]{2,1,0:T(8,128)S(1)} collective-permute-done((f32[2,64,128]{2,1,0:T(8,128)S(1)}, f32[2,64,128]{2,1,0:T(8,128)S(1)}, u32[]{:S(2)}, u32[]{:S(2)}) %collective-permute-start.32) | collective-permute-done | bytes 65568 | tf_op jit(solution)/shard_map/ppermute | solution.py:502
  121.6 2.4 %collective-permute-done.36.refs_3_ = f32[64,128]{1,0:T(8,128)S(1)} collective-permute-done((f32[64,128]{1,0:T(8,128)S(1)}, f32[64,128]{1,0:T(8,128)S(1)}, u32[]{:S(2)}, u32[]{:S(2)}) %collective-permute-start.36) | collective-permute-done | bytes 32800 | tf_op jit(solution)/shard_map/ppermute | solution.py:502
  124.0 1.5 %collective-permute-done.35.refs_2_ = f32[64,128]{1,0:T(8,128)S(1)} collective-permute-done((f32[64,128]{1,0:T(8,128)S(1)}, f32[64,128]{1,0:T(8,128)S(1)}, u32[]{:S(2)}, u32[]{:S(2)}) %collective-permute-start.35) | collective-permute-done | bytes 32800 | tf_op jit(solution)/shard_map/ppermute | solution.py:503
  126.0 11.0 %all_to_all.11.sums_ref = f32[16,32,128]{2,1,0:T(8,128)S(1)} all-to-all(f32[16,32,128]{2,1,0:T(8,128)S(1)} %get-tuple-element.156), channel_id=1, replica_groups=mesh['q'=16,'c'=2,'space'=16] {'q'}, dimensions={0} | all-to-all | bytes 524288 | tf_op jit(solution)/shard_map/all_to_all | solution.py:598
  137.3 3.4 %collective-permute-start.37 = (f32[64,128]{1,0:T(8,128)S(1)}, f32[64,128]{1,0:T(8,128)S(1)}, u32[]{:S(2)}, u32[]{:S(2)}) collective-permute-start(f32[64,128]{1,0:T(8,128)S(1)} %get-tuple-element.160), channel_id=1, source_target_pairs={{0,16},{16,0},{1,17},{17,1},{2,18},{18,2},{3,19},{19,3},{4,20},{20... | collective-permute-start | bytes 98312 | tf_op jit(solution)/shard_map/ppermute | solution.py:495
  (96 shorter events, 67.6 us)
Async XLA Ops:
  2.5 3.6 %collective-permute-start = (f32[3,64,128]{2,1,0:T(8,128)S(1)}, f32[3,64,128]{2,1,0:T(8,128)S(1)}, u32[]{:S(2)}, u32[]{:S(2)}) collective-permute-start(f32[3,64,128]{2,1,0:T(8,128)S(1)} %get-tuple-element.83), channel_id=1, source_target_pairs={{0,16},{16,0},{1,17},{17,1},{2,18},{18,2},{3,19},{19,3},{4,20},{20... | collective-permute-start | bytes 294920 | tf_op jit(solution)/shard_map/ppermute | solution.py:495
  6.2 5.2 %collective-permute-start.2 = (f32[64,128]{1,0:T(8,128)S(1)}, f32[64,128]{1,0:T(8,128)S(1)}, u32[]{:S(2)}, u32[]{:S(2)}) collective-permute-start(f32[64,128]{1,0:T(8,128)S(1)} %get-tuple-element.90.field_ref), channel_id=1, source_target_pairs={{1,16},{2,17},{3,18},{4,19},{5,20},{6,21},{7,22},{8,23},{9,24},{10... | collective-permute-start | bytes 98312 | tf_op jit(solution)/shard_map/ppermute | solution.py:502
  7.5 4.9 %collective-permute-start.1 = (f32[64,128]{1,0:T(8,128)S(1)}, f32[64,128]{1,0:T(8,128)S(1)}, u32[]{:S(2)}, u32[]{:S(2)}) collective-permute-start(f32[64,128]{1,0:T(8,128)S(1)} %get-tuple-element.90.field_ref), channel_id=1, source_target_pairs={{0,16},{1,17},{2,18},{3,19},{4,20},{5,21},{6,22},{7,23},{8,24},{9,... | collective-permute-start | bytes 98312 | tf_op jit(solution)/shard_map/ppermute | solution.py:503
  12.7 3.1 %collective-permute-start.4 = (f32[2,64,128]{2,1,0:T(8,128)S(1)}, f32[2,64,128]{2,1,0:T(8,128)S(1)}, u32[]{:S(2)}, u32[]{:S(2)}) collective-permute-start(f32[2,64,128]{2,1,0:T(8,128)S(1)} %open.2.pair_ref), channel_id=1, source_target_pairs={{16,1},{17,2},{18,3},{19,4},{20,5},{21,6},{22,7},{23,8},{24,9},{25... | collective-permute-start | bytes 196616 | tf_op jit(solution)/shard_map/ppermute | solution.py:502
  16.7 5.6 %collective-permute-start.6 = (f32[2,64,128]{2,1,0:T(8,128)S(1)}, f32[2,64,128]{2,1,0:T(8,128)S(1)}, u32[]{:S(2)}, u32[]{:S(2)}) collective-permute-start(f32[2,64,128]{2,1,0:T(8,128)S(1)} %get-tuple-element.97.pair_ref), channel_id=1, source_target_pairs={{1,16},{2,17},{3,18},{4,19},{5,20},{6,21},{7,22},{8,23},{9,24},{10... | collective-permute-start | bytes 196616 | tf_op jit(solution)/shard_map/ppermute | solution.py:502
  18.0 5.6 %collective-permute-start.5 = (f32[2,64,128]{2,1,0:T(8,128)S(1)}, f32[2,64,128]{2,1,0:T(8,128)S(1)}, u32[]{:S(2)}, u32[]{:S(2)}) collective-permute-start(f32[2,64,128]{2,1,0:T(8,128)S(1)} %get-tuple-element.97.pair_ref), channel_id=1, source_target_pairs={{0,16},{1,17},{2,18},{3,19},{4,20},{5,21},{6,22},{7,23},{8,24},{9,... | collective-permute-start | bytes 196616 | tf_op jit(solution)/shard_map/ppermute | solution.py:503
  28.0 5.6 %collective-permute-start.10 = (f32[2,64,128]{2,1,0:T(8,128)S(1)}, f32[2,64,128]{2,1,0:T(8,128)S(1)}, u32[]{:S(2)}, u32[]{:S(2)}) collective-permute-start(f32[2,64,128]{2,1,0:T(8,128)S(1)} %get-tuple-element.105.pair_ref), channel_id=1, source_target_pairs={{1,16},{2,17},{3,18},{4,19},{5,20},{6,21},{7,22},{8,23},{9,24},{10... | collective-permute-start | bytes 196616 | tf_op jit(solution)/shard_map/ppermute | solution.py:502
  29.3 5.5 %collective-permute-start.9 = (f32[2,64,128]{2,1,0:T(8,128)S(1)}, f32[2,64,128]{2,1,0:T(8,128)S(1)}, u32[]{:S(2)}, u32[]{:S(2)}) collective-permute-start(f32[2,64,128]{2,1,0:T(8,128)S(1)} %get-tuple-element.105.pair_ref), channel_id=1, source_target_pairs={{0,16},{1,17},{2,18},{3,19},{4,20},{5,21},{6,22},{7,23},{8,24},{9,... | collective-permute-start | bytes 196616 | tf_op jit(solution)/shard_map/ppermute | solution.py:503
  39.2 5.6 %collective-permute-start.14 = (f32[2,64,128]{2,1,0:T(8,128)S(1)}, f32[2,64,128]{2,1,0:T(8,128)S(1)}, u32[]{:S(2)}, u32[]{:S(2)}) collective-permute-start(f32[2,64,128]{2,1,0:T(8,128)S(1)} %get-tuple-element.113.pair_ref), channel_id=1, source_target_pairs={{1,16},{2,17},{3,18},{4,19},{5,20},{6,21},{7,22},{8,23},{9,24},{10... | collective-permute-start | bytes 196616 | tf_op jit(solution)/shard_map/ppermute | solution.py:502
  40.5 5.5 %collective-permute-start.13 = (f32[2,64,128]{2,1,0:T(8,128)S(1)}, f32[2,64,128]{2,1,0:T(8,128)S(1)}, u32[]{:S(2)}, u32[]{:S(2)}) collective-permute-start(f32[2,64,128]{2,1,0:T(8,128)S(1)} %get-tuple-element.113.pair_ref), channel_id=1, source_target_pairs={{0,16},{1,17},{2,18},{3,19},{4,20},{5,21},{6,22},{7,23},{8,24},{9,... | collective-permute-start | bytes 196616 | tf_op jit(solution)/shard_map/ppermute | solution.py:503
  50.4 5.2 %collective-permute-start.18 = (f32[64,128]{1,0:T(8,128)S(1)}, f32[64,128]{1,0:T(8,128)S(1)}, u32[]{:S(2)}, u32[]{:S(2)}) collective-permute-start(f32[64,128]{1,0:T(8,128)S(1)} %last.2.field_ref), channel_id=1, source_target_pairs={{1,16},{2,17},{3,18},{4,19},{5,20},{6,21},{7,22},{8,23},{9,24},{10... | collective-permute-start | bytes 98312 | tf_op jit(solution)/shard_map/ppermute | solution.py:502
  51.7 5.5 %collective-permute-start.17 = (f32[64,128]{1,0:T(8,128)S(1)}, f32[64,128]{1,0:T(8,128)S(1)}, u32[]{:S(2)}, u32[]{:S(2)}) collective-permute-start(f32[64,128]{1,0:T(8,128)S(1)} %last.2.field_ref), channel_id=1, source_target_pairs={{0,16},{1,17},{2,18},{3,19},{4,20},{5,21},{6,22},{7,23},{8,24},{9,... | collective-permute-start | bytes 98312 | tf_op jit(solution)/shard_map/ppermute | solution.py:503
  74.4 5.2 %collective-permute-start.20 = (f32[64,128]{1,0:T(8,128)S(1)}, f32[64,128]{1,0:T(8,128)S(1)}, u32[]{:S(2)}, u32[]{:S(2)}) collective-permute-start(f32[64,128]{1,0:T(8,128)S(1)} %restart.1.field_ref), channel_id=1, source_target_pairs={{1,16},{2,17},{3,18},{4,19},{5,20},{6,21},{7,22},{8,23},{9,24},{10... | collective-permute-start | bytes 98312 | tf_op jit(solution)/shard_map/ppermute | solution.py:502
  75.7 5.3 %collective-permute-start.19 = (f32[64,128]{1,0:T(8,128)S(1)}, f32[64,128]{1,0:T(8,128)S(1)}, u32[]{:S(2)}, u32[]{:S(2)}) collective-permute-start(f32[64,128]{1,0:T(8,128)S(1)} %restart.1.field_ref), channel_id=1, source_target_pairs={{0,16},{1,17},{2,18},{3,19},{4,20},{5,21},{6,22},{7,23},{8,24},{9,... | collective-permute-start | bytes 98312 | tf_op jit(solution)/shard_map/ppermute | solution.py:503
  81.3 3.1 %collective-permute-start.22 = (f32[2,64,128]{2,1,0:T(8,128)S(1)}, f32[2,64,128]{2,1,0:T(8,128)S(1)}, u32[]{:S(2)}, u32[]{:S(2)}) collective-permute-start(f32[2,64,128]{2,1,0:T(8,128)S(1)} %open.3.pair_ref), channel_id=1, source_target_pairs={{16,1},{17,2},{18,3},{19,4},{20,5},{21,6},{22,7},{23,8},{24,9},{25... | collective-permute-start | bytes 196616 | tf_op jit(solution)/shard_map/ppermute | solution.py:502
  85.3 5.6 %collective-permute-start.24 = (f32[2,64,128]{2,1,0:T(8,128)S(1)}, f32[2,64,128]{2,1,0:T(8,128)S(1)}, u32[]{:S(2)}, u32[]{:S(2)}) collective-permute-start(f32[2,64,128]{2,1,0:T(8,128)S(1)} %get-tuple-element.132.pair_ref), channel_id=1, source_target_pairs={{1,16},{2,17},{3,18},{4,19},{5,20},{6,21},{7,22},{8,23},{9,24},{10... | collective-permute-start | bytes 196616 | tf_op jit(solution)/shard_map/ppermute | solution.py:502
  86.5 5.6 %collective-permute-start.23 = (f32[2,64,128]{2,1,0:T(8,128)S(1)}, f32[2,64,128]{2,1,0:T(8,128)S(1)}, u32[]{:S(2)}, u32[]{:S(2)}) collective-permute-start(f32[2,64,128]{2,1,0:T(8,128)S(1)} %get-tuple-element.132.pair_ref), channel_id=1, source_target_pairs={{0,16},{1,17},{2,18},{3,19},{4,20},{5,21},{6,22},{7,23},{8,24},{9,... | collective-permute-start | bytes 196616 | tf_op jit(solution)/shard_map/ppermute | solution.py:503
  96.5 5.6 %collective-permute-start.28 = (f32[2,64,128]{2,1,0:T(8,128)S(1)}, f32[2,64,128]{2,1,0:T(8,128)S(1)}, u32[]{:S(2)}, u32[]{:S(2)}) collective-permute-start(f32[2,64,128]{2,1,0:T(8,128)S(1)} %get-tuple-element.140.pair_ref), channel_id=1, source_target_pairs={{1,16},{2,17},{3,18},{4,19},{5,20},{6,21},{7,22},{8,23},{9,24},{10... | collective-permute-start | bytes 196616 | tf_op jit(solution)/shard_map/ppermute | solution.py:502
  97.8 5.5 %collective-permute-start.27 = (f32[2,64,128]{2,1,0:T(8,128)S(1)}, f32[2,64,128]{2,1,0:T(8,128)S(1)}, u32[]{:S(2)}, u32[]{:S(2)}) collective-permute-start(f32[2,64,128]{2,1,0:T(8,128)S(1)} %get-tuple-element.140.pair_ref), channel_id=1, source_target_pairs={{0,16},{1,17},{2,18},{3,19},{4,20},{5,21},{6,22},{7,23},{8,24},{9,... | collective-permute-start | bytes 196616 | tf_op jit(solution)/shard_map/ppermute | solution.py:503
  107.6 5.6 %collective-permute-start.32 = (f32[2,64,128]{2,1,0:T(8,128)S(1)}, f32[2,64,128]{2,1,0:T(8,128)S(1)}, u32[]{:S(2)}, u32[]{:S(2)}) collective-permute-start(f32[2,64,128]{2,1,0:T(8,128)S(1)} %get-tuple-element.148.pair_ref), channel_id=1, source_target_pairs={{1,16},{2,17},{3,18},{4,19},{5,20},{6,21},{7,22},{8,23},{9,24},{10... | collective-permute-start | bytes 196616 | tf_op jit(solution)/shard_map/ppermute | solution.py:502
  108.9 5.5 %collective-permute-start.31 = (f32[2,64,128]{2,1,0:T(8,128)S(1)}, f32[2,64,128]{2,1,0:T(8,128)S(1)}, u32[]{:S(2)}, u32[]{:S(2)}) collective-permute-start(f32[2,64,128]{2,1,0:T(8,128)S(1)} %get-tuple-element.148.pair_ref), channel_id=1, source_target_pairs={{0,16},{1,17},{2,18},{3,19},{4,20},{5,21},{6,22},{7,23},{8,24},{9,... | collective-permute-start | bytes 196616 | tf_op jit(solution)/shard_map/ppermute | solution.py:503
  118.7 5.2 %collective-permute-start.36 = (f32[64,128]{1,0:T(8,128)S(1)}, f32[64,128]{1,0:T(8,128)S(1)}, u32[]{:S(2)}, u32[]{:S(2)}) collective-permute-start(f32[64,128]{1,0:T(8,128)S(1)} %last.3.field_ref), channel_id=1, source_target_pairs={{1,16},{2,17},{3,18},{4,19},{5,20},{6,21},{7,22},{8,23},{9,24},{10... | collective-permute-start | bytes 98312 | tf_op jit(solution)/shard_map/ppermute | solution.py:502
  120.0 5.5 %collective-permute-start.35 = (f32[64,128]{1,0:T(8,128)S(1)}, f32[64,128]{1,0:T(8,128)S(1)}, u32[]{:S(2)}, u32[]{:S(2)}) collective-permute-start(f32[64,128]{1,0:T(8,128)S(1)} %last.3.field_ref), channel_id=1, source_target_pairs={{0,16},{1,17},{2,18},{3,19},{4,20},{5,21},{6,22},{7,23},{8,24},{9,... | collective-permute-start | bytes 98312 | tf_op jit(solution)/shard_map/ppermute | solution.py:503
  137.3 4.2 %collective-permute-start.37 = (f32[64,128]{1,0:T(8,128)S(1)}, f32[64,128]{1,0:T(8,128)S(1)}, u32[]{:S(2)}, u32[]{:S(2)}) collective-permute-start(f32[64,128]{1,0:T(8,128)S(1)} %get-tuple-element.160), channel_id=1, source_target_pairs={{0,16},{16,0},{1,17},{17,1},{2,18},{18,2},{3,19},{19,3},{4,20},{20... | collective-permute-start | bytes 98312 | tf_op jit(solution)/shard_map/ppermute | solution.py:495
  (14 other events, 34.2 us)

commit v8 on v7

--- a/solution.py
+++ b/solution.py
@@ -16,7 +16,7 @@
 GX = 8
 GY = 8
 SQUARED = 16
-EARLY = 16
+EARLY = 8
 F32 = jnp.float32
 BF16 = jnp.bfloat16
 FIELD = (VALUES, LANES)

time: 143 us -> 144 us (level)
  no operation moved by 1% of the time
where the time goes in v8:
time: 144 us; the launch traced here: 143 us
  starting transfers between devices  53.5 us (37%)
  waiting for transfers between devices  36.7 us (25%)
  blocking collectives  27.7 us (19%)
  Pallas kernels  23.5 us (16%)
    all_to_all x2, blocking collectives, evolve(): gathered = vmem(lax.all_to_all(chunk, 'q', 0, 0))  27.7 us
    ppermute x18, starting transfers between devices, halo(): near = lax.ppermute(x, 'c', [(1 - to, to)])  24.4 us
    pallas_call x42, Pallas kernels, call(): pl.pallas_call(kernel, out_shape=shapes, in_specs=[pl.BlockSpec(memory_sp...  23.5 us
    ppermute x18, starting transfers between devices, halo(): far = lax.ppermute(x, ('c', 'space'), across)  23.2 us
    ppermute x18, waiting for transfers between devices, halo(): near = lax.ppermute(x, 'c', [(1 - to, to)])  19.9 us
    ppermute x18, waiting for transfers between devices, halo(): far = lax.ppermute(x, ('c', 'space'), across)  16 us
    ppermute x2, starting transfers between devices, swap_cores(): return lax.ppermute(x, 'c', [(0, 1), (1, 0)])  5.98 us
  transfers between devices with their start and end apart: 38, of which 29 were waited for; matrix products, arithmetic and copies ran while one was open for 0% of the time, Pallas kernels for 10%

profile of v8, /device:TPU:385, one launch (start us, length us, event | category | flops | bytes accessed | tf_op | source)
XLA Modules:
  0.0 142.7 jit_solution(30739244489161651)
XLA Ops:
  0.6 1.8 %share.1 = (f32[5,64,128]{2,1,0:T(8,128)S(1)}, f32[3,64,128]{2,1,0:T(8,128)S(1)}, f32[64,128]{1,0:T(8,128)S(1)}, s32[8,128]{1,0:T(8,128)S(1)}, s32[8,128]{1,0:T(...) custom-call(s32[6,128]{1,0:T(8,128)} %neighbor_any.1, ...), custom_call_target="tpu_custom_call" | custom-call | flops 4194304 | bytes 1048576 | tf_op jit(solution)/shard_map/share/pallas_call | solution.py:43
  2.5 2.6 %collective-permute-start = (f32[3,64,128]{2,1,0:T(8,128)S(1)}, f32[3,64,128]{2,1,0:T(8,128)S(1)}, u32[]{:S(2)}, u32[]{:S(2)}) collective-permute-start(f32[3,64,128]{2,1,0:T(8,128)S(1)} %get-tuple-element.83), channel_id=1, source_target_pairs={{0,16},{16,0},{1,17},{17,1},{2,18},{18,2},{3,19},{19,3},{4,20},{20... | collective-permute-start | bytes 294920 | tf_op jit(solution)/shard_map/ppermute | solution.py:495
  9.5 2.2 %collective-permute-done.2.far_ref = f32[64,128]{1,0:T(8,128)S(1)} collective-permute-done((f32[64,128]{1,0:T(8,128)S(1)}, f32[64,128]{1,0:T(8,128)S(1)}, u32[]{:S(2)}, u32[]{:S(2)}) %collective-permute-start.2) | collective-permute-done | bytes 32800 | tf_op jit(solution)/shard_map/ppermute | solution.py:502
  13.0 1.3 collective-permute-start.4
  14.3 1.8 %collective-permute-start.3 = (f32[2,64,128]{2,1,0:T(8,128)S(1)}, f32[2,64,128]{2,1,0:T(8,128)S(1)}, u32[]{:S(2)}, u32[]{:S(2)}) collective-permute-start(f32[2,64,128]{2,1,0:T(8,128)S(1)} %open.2.pair_ref), channel_id=1, source_target_pairs={{16,0},{17,1},{18,2},{19,3},{20,4},{21,5},{22,6},{23,7},{24,8},{25... | collective-permute-start | bytes 196616 | tf_op jit(solution)/shard_map/ppermute | solution.py:503
  19.5 2.5 %ahead.15 = (f32[64,128]{1,0:T(8,128)S(1)}, f32[64,64,128]{2,1,0:T(8,128)S(1)}) custom-call(f32[2,64,128]{2,1,0:T(8,128)S(1)} %get-tuple-element.97.pair_ref, bf16[128,384]{1,0:T(8,128)(2,1)S(1)} %get-tuple-element.92.faces_ref.refs_4_, f32[64,64,128]{2,1,0:T(8,128)S(1)} %get-tuple-element.89.table_ref.refs_5_, ...), custom_call_target="tpu_custom_call", output_to_operand_aliasing={{1}: (3, {})} | custom-call | flops 4194304 | bytes 1048576 | tf_op jit(solution)/shard_map/ahead/pallas_call | solution.py:43
  22.5 1.3 collective-permute-done.5.near_ref
  30.8 2.5 %ahead.17 = (f32[64,128]{1,0:T(8,128)S(1)}, f32[64,64,128]{2,1,0:T(8,128)S(1)}) custom-call(f32[2,64,128]{2,1,0:T(8,128)S(1)} %get-tuple-element.105.pair_ref, bf16[128,384]{1,0:T(8,128)(2,1)S(1)} %get-tuple-element.92.faces_ref.refs_4_, f32[64,64,128]{2,1,0:T(8,128)S(1)} %get-tuple-element.89.table_ref.refs_5_, ...), custom_call_target="tpu_custom_call", output_to_operand_aliasing={{1}: (3, {})} | custom-call | flops 4194304 | bytes 1048576 | tf_op jit(solution)/shard_map/ahead/pallas_call | solution.py:43
  42.0 2.5 %ahead.19 = (f32[64,128]{1,0:T(8,128)S(1)}, f32[64,64,128]{2,1,0:T(8,128)S(1)}) custom-call(f32[2,64,128]{2,1,0:T(8,128)S(1)} %get-tuple-element.113.pair_ref, bf16[128,384]{1,0:T(8,128)(2,1)S(1)} %get-tuple-element.92.faces_ref.refs_4_, f32[64,64,128]{2,1,0:T(8,128)S(1)} %get-tuple-element.89.table_ref.refs_5_, ...), custom_call_target="tpu_custom_call", output_to_operand_aliasing={{1}: (3, {})} | custom-call | flops 4194304 | bytes 1048576 | tf_op jit(solution)/shard_map/ahead/pallas_call | solution.py:43
  53.2 2.5 %tail.2 = (f32[64,128]{1,0:T(8,128)S(1)}, f32[64,64,128]{2,1,0:T(8,128)S(1)}) custom-call(f32[64,128]{1,0:T(8,128)S(1)} %last.2.field_ref, f32[64,128]{1,0:T(8,128)S(1)} %get-tuple-element.117.right_ref.refs_0_, f32[2,64,128]{2,1,0:T(8,128)S(1)} %collective-permute-done.15.near_ref, ...), custom_call_target="tpu_custom_call", output_to_operand_aliasing={{1}: (6, {})} | custom-call | flops 4194304 | bytes 1048576 | tf_op jit(solution)/shard_map/tail/pallas_call | solution.py:43
  55.9 1.5 %collective-permute-done.17.refs_2_ = f32[64,128]{1,0:T(8,128)S(1)} collective-permute-done((f32[64,128]{1,0:T(8,128)S(1)}, f32[64,128]{1,0:T(8,128)S(1)}, u32[]{:S(2)}, u32[]{:S(2)}) %collective-permute-start.17) | collective-permute-done | bytes 32800 | tf_op jit(solution)/shard_map/ppermute | solution.py:503
  57.9 16.8 %all_to_all.10.sums_ref.gains_ref = f32[16,64,128]{2,1,0:T(8,128)S(1)} all-to-all(f32[16,64,128]{2,1,0:T(8,128)S(1)} %get-tuple-element.124), channel_id=1, replica_groups=mesh['q'=16,'c'=2,'space'=16] {'q'}, dimensions={0} | all-to-all | bytes 1048576 | tf_op jit(solution)/shard_map/all_to_all | solution.py:598
  77.9 2.0 %collective-permute-done.20.far_ref = f32[64,128]{1,0:T(8,128)S(1)} collective-permute-done((f32[64,128]{1,0:T(8,128)S(1)}, f32[64,128]{1,0:T(8,128)S(1)}, u32[]{:S(2)}, u32[]{:S(2)}) %collective-permute-start.20) | collective-permute-done | bytes 32800 | tf_op jit(solution)/shard_map/ppermute | solution.py:502
  79.9 1.3 collective-permute-done.19.near_ref
  82.8 1.8 %collective-permute-start.21 = (f32[2,64,128]{2,1,0:T(8,128)S(1)}, f32[2,64,128]{2,1,0:T(8,128)S(1)}, u32[]{:S(2)}, u32[]{:S(2)}) collective-permute-start(f32[2,64,128]{2,1,0:T(8,128)S(1)} %open.3.pair_ref), channel_id=1, source_target_pairs={{16,0},{17,1},{18,2},{19,3},{20,4},{21,5},{22,6},{23,7},{24,8},{25... | collective-permute-start | bytes 196616 | tf_op jit(solution)/shard_map/ppermute | solution.py:503
  86.8 1.5 %collective-permute-start.23 = (f32[2,64,128]{2,1,0:T(8,128)S(1)}, f32[2,64,128]{2,1,0:T(8,128)S(1)}, u32[]{:S(2)}, u32[]{:S(2)}) collective-permute-start(f32[2,64,128]{2,1,0:T(8,128)S(1)} %get-tuple-element.132.pair_ref), channel_id=1, source_target_pairs={{0,16},{1,17},{2,18},{3,19},{4,20},{5,21},{6,22},{7,23},{8,24},{9,... | collective-permute-start | bytes 196616 | tf_op jit(solution)/shard_map/ppermute | solution.py:503
  88.5 2.5 %collective-permute-done.24.far_ref = f32[2,64,128]{2,1,0:T(8,128)S(1)} collective-permute-done((f32[2,64,128]{2,1,0:T(8,128)S(1)}, f32[2,64,128]{2,1,0:T(8,128)S(1)}, u32[]{:S(2)}, u32[]{:S(2)}) %collective-permute-start.24) | collective-permute-done | bytes 65568 | tf_op jit(solution)/shard_map/ppermute | solution.py:502
  91.1 1.5 %collective-permute-done.23.near_ref = f32[2,64,128]{2,1,0:T(8,128)S(1)} collective-permute-done((f32[2,64,128]{2,1,0:T(8,128)S(1)}, f32[2,64,128]{2,1,0:T(8,128)S(1)}, u32[]{:S(2)}, u32[]{:S(2)}) %collective-permute-start.23) | collective-permute-done | bytes 65568 | tf_op jit(solution)/shard_map/ppermute | solution.py:503
  99.7 2.7 %collective-permute-done.28.far_ref = f32[2,64,128]{2,1,0:T(8,128)S(1)} collective-permute-done((f32[2,64,128]{2,1,0:T(8,128)S(1)}, f32[2,64,128]{2,1,0:T(8,128)S(1)}, u32[]{:S(2)}, u32[]{:S(2)}) %collective-permute-start.28) | collective-permute-done | bytes 65568 | tf_op jit(solution)/shard_map/ppermute | solution.py:502
  110.9 2.7 %collective-permute-done.32.far_ref = f32[2,64,128]{2,1,0:T(8,128)S(1)} collective-permute-done((f32[2,64,128]{2,1,0:T(8,128)S(1)}, f32[2,64,128]{2,1,0:T(8,128)S(1)}, u32[]{:S(2)}, u32[]{:S(2)}) %collective-permute-start.32) | collective-permute-done | bytes 65568 | tf_op jit(solution)/shard_map/ppermute | solution.py:502
  122.0 2.4 %collective-permute-done.36.refs_3_ = f32[64,128]{1,0:T(8,128)S(1)} collective-permute-done((f32[64,128]{1,0:T(8,128)S(1)}, f32[64,128]{1,0:T(8,128)S(1)}, u32[]{:S(2)}, u32[]{:S(2)}) %collective-permute-start.36) | collective-permute-done | bytes 32800 | tf_op jit(solution)/shard_map/ppermute | solution.py:502
  124.4 1.5 %collective-permute-done.35.refs_2_ = f32[64,128]{1,0:T(8,128)S(1)} collective-permute-done((f32[64,128]{1,0:T(8,128)S(1)}, f32[64,128]{1,0:T(8,128)S(1)}, u32[]{:S(2)}, u32[]{:S(2)}) %collective-permute-start.35) | collective-permute-done | bytes 32800 | tf_op jit(solution)/shard_map/ppermute | solution.py:503
  126.5 11.0 %all_to_all.11.sums_ref = f32[16,32,128]{2,1,0:T(8,128)S(1)} all-to-all(f32[16,32,128]{2,1,0:T(8,128)S(1)} %get-tuple-element.156), channel_id=1, replica_groups=mesh['q'=16,'c'=2,'space'=16] {'q'}, dimensions={0} | all-to-all | bytes 524288 | tf_op jit(solution)/shard_map/all_to_all | solution.py:598
  137.7 3.4 %collective-permute-start.37 = (f32[64,128]{1,0:T(8,128)S(1)}, f32[64,128]{1,0:T(8,128)S(1)}, u32[]{:S(2)}, u32[]{:S(2)}) collective-permute-start(f32[64,128]{1,0:T(8,128)S(1)} %get-tuple-element.160), channel_id=1, source_target_pairs={{0,16},{16,0},{1,17},{17,1},{2,18},{18,2},{3,19},{19,3},{4,20},{20... | collective-permute-start | bytes 98312 | tf_op jit(solution)/shard_map/ppermute | solution.py:495
  (96 shorter events, 67.7 us)
Async XLA Ops:
  2.5 3.9 %collective-permute-start = (f32[3,64,128]{2,1,0:T(8,128)S(1)}, f32[3,64,128]{2,1,0:T(8,128)S(1)}, u32[]{:S(2)}, u32[]{:S(2)}) collective-permute-start(f32[3,64,128]{2,1,0:T(8,128)S(1)} %get-tuple-element.83), channel_id=1, source_target_pairs={{0,16},{16,0},{1,17},{17,1},{2,18},{18,2},{3,19},{19,3},{4,20},{20... | collective-permute-start | bytes 294920 | tf_op jit(solution)/shard_map/ppermute | solution.py:495
  6.4 5.2 %collective-permute-start.2 = (f32[64,128]{1,0:T(8,128)S(1)}, f32[64,128]{1,0:T(8,128)S(1)}, u32[]{:S(2)}, u32[]{:S(2)}) collective-permute-start(f32[64,128]{1,0:T(8,128)S(1)} %get-tuple-element.90.field_ref), channel_id=1, source_target_pairs={{1,16},{2,17},{3,18},{4,19},{5,20},{6,21},{7,22},{8,23},{9,24},{10... | collective-permute-start | bytes 98312 | tf_op jit(solution)/shard_map/ppermute | solution.py:502
  7.7 4.9 %collective-permute-start.1 = (f32[64,128]{1,0:T(8,128)S(1)}, f32[64,128]{1,0:T(8,128)S(1)}, u32[]{:S(2)}, u32[]{:S(2)}) collective-permute-start(f32[64,128]{1,0:T(8,128)S(1)} %get-tuple-element.90.field_ref), channel_id=1, source_target_pairs={{0,16},{1,17},{2,18},{3,19},{4,20},{5,21},{6,22},{7,23},{8,24},{9,... | collective-permute-start | bytes 98312 | tf_op jit(solution)/shard_map/ppermute | solution.py:503
  13.0 3.1 %collective-permute-start.4 = (f32[2,64,128]{2,1,0:T(8,128)S(1)}, f32[2,64,128]{2,1,0:T(8,128)S(1)}, u32[]{:S(2)}, u32[]{:S(2)}) collective-permute-start(f32[2,64,128]{2,1,0:T(8,128)S(1)} %open.2.pair_ref), channel_id=1, source_target_pairs={{16,1},{17,2},{18,3},{19,4},{20,5},{21,6},{22,7},{23,8},{24,9},{25... | collective-permute-start | bytes 196616 | tf_op jit(solution)/shard_map/ppermute | solution.py:502
  16.9 5.6 %collective-permute-start.6 = (f32[2,64,128]{2,1,0:T(8,128)S(1)}, f32[2,64,128]{2,1,0:T(8,128)S(1)}, u32[]{:S(2)}, u32[]{:S(2)}) collective-permute-start(f32[2,64,128]{2,1,0:T(8,128)S(1)} %get-tuple-element.97.pair_ref), channel_id=1, source_target_pairs={{1,16},{2,17},{3,18},{4,19},{5,20},{6,21},{7,22},{8,23},{9,24},{10... | collective-permute-start | bytes 196616 | tf_op jit(solution)/shard_map/ppermute | solution.py:502
  18.2 5.6 %collective-permute-start.5 = (f32[2,64,128]{2,1,0:T(8,128)S(1)}, f32[2,64,128]{2,1,0:T(8,128)S(1)}, u32[]{:S(2)}, u32[]{:S(2)}) collective-permute-start(f32[2,64,128]{2,1,0:T(8,128)S(1)} %get-tuple-element.97.pair_ref), channel_id=1, source_target_pairs={{0,16},{1,17},{2,18},{3,19},{4,20},{5,21},{6,22},{7,23},{8,24},{9,... | collective-permute-start | bytes 196616 | tf_op jit(solution)/shard_map/ppermute | solution.py:503
  28.2 5.6 %collective-permute-start.10 = (f32[2,64,128]{2,1,0:T(8,128)S(1)}, f32[2,64,128]{2,1,0:T(8,128)S(1)}, u32[]{:S(2)}, u32[]{:S(2)}) collective-permute-start(f32[2,64,128]{2,1,0:T(8,128)S(1)} %get-tuple-element.105.pair_ref), channel_id=1, source_target_pairs={{1,16},{2,17},{3,18},{4,19},{5,20},{6,21},{7,22},{8,23},{9,24},{10... | collective-permute-start | bytes 196616 | tf_op jit(solution)/shard_map/ppermute | solution.py:502
  29.5 5.5 %collective-permute-start.9 = (f32[2,64,128]{2,1,0:T(8,128)S(1)}, f32[2,64,128]{2,1,0:T(8,128)S(1)}, u32[]{:S(2)}, u32[]{:S(2)}) collective-permute-start(f32[2,64,128]{2,1,0:T(8,128)S(1)} %get-tuple-element.105.pair_ref), channel_id=1, source_target_pairs={{0,16},{1,17},{2,18},{3,19},{4,20},{5,21},{6,22},{7,23},{8,24},{9,... | collective-permute-start | bytes 196616 | tf_op jit(solution)/shard_map/ppermute | solution.py:503
  39.4 5.6 %collective-permute-start.14 = (f32[2,64,128]{2,1,0:T(8,128)S(1)}, f32[2,64,128]{2,1,0:T(8,128)S(1)}, u32[]{:S(2)}, u32[]{:S(2)}) collective-permute-start(f32[2,64,128]{2,1,0:T(8,128)S(1)} %get-tuple-element.113.pair_ref), channel_id=1, source_target_pairs={{1,16},{2,17},{3,18},{4,19},{5,20},{6,21},{7,22},{8,23},{9,24},{10... | collective-permute-start | bytes 196616 | tf_op jit(solution)/shard_map/ppermute | solution.py:502
  40.7 5.5 %collective-permute-start.13 = (f32[2,64,128]{2,1,0:T(8,128)S(1)}, f32[2,64,128]{2,1,0:T(8,128)S(1)}, u32[]{:S(2)}, u32[]{:S(2)}) collective-permute-start(f32[2,64,128]{2,1,0:T(8,128)S(1)} %get-tuple-element.113.pair_ref), channel_id=1, source_target_pairs={{0,16},{1,17},{2,18},{3,19},{4,20},{5,21},{6,22},{7,23},{8,24},{9,... | collective-permute-start | bytes 196616 | tf_op jit(solution)/shard_map/ppermute | solution.py:503
  50.6 5.2 %collective-permute-start.18 = (f32[64,128]{1,0:T(8,128)S(1)}, f32[64,128]{1,0:T(8,128)S(1)}, u32[]{:S(2)}, u32[]{:S(2)}) collective-permute-start(f32[64,128]{1,0:T(8,128)S(1)} %last.2.field_ref), channel_id=1, source_target_pairs={{1,16},{2,17},{3,18},{4,19},{5,20},{6,21},{7,22},{8,23},{9,24},{10... | collective-permute-start | bytes 98312 | tf_op jit(solution)/shard_map/ppermute | solution.py:502
  51.9 5.5 %collective-permute-start.17 = (f32[64,128]{1,0:T(8,128)S(1)}, f32[64,128]{1,0:T(8,128)S(1)}, u32[]{:S(2)}, u32[]{:S(2)}) collective-permute-start(f32[64,128]{1,0:T(8,128)S(1)} %last.2.field_ref), channel_id=1, source_target_pairs={{0,16},{1,17},{2,18},{3,19},{4,20},{5,21},{6,22},{7,23},{8,24},{9,... | collective-permute-start | bytes 98312 | tf_op jit(solution)/shard_map/ppermute | solution.py:503
  74.7 5.2 %collective-permute-start.20 = (f32[64,128]{1,0:T(8,128)S(1)}, f32[64,128]{1,0:T(8,128)S(1)}, u32[]{:S(2)}, u32[]{:S(2)}) collective-permute-start(f32[64,128]{1,0:T(8,128)S(1)} %restart.1.field_ref), channel_id=1, source_target_pairs={{1,16},{2,17},{3,18},{4,19},{5,20},{6,21},{7,22},{8,23},{9,24},{10... | collective-permute-start | bytes 98312 | tf_op jit(solution)/shard_map/ppermute | solution.py:502
  76.0 5.3 %collective-permute-start.19 = (f32[64,128]{1,0:T(8,128)S(1)}, f32[64,128]{1,0:T(8,128)S(1)}, u32[]{:S(2)}, u32[]{:S(2)}) collective-permute-start(f32[64,128]{1,0:T(8,128)S(1)} %restart.1.field_ref), channel_id=1, source_target_pairs={{0,16},{1,17},{2,18},{3,19},{4,20},{5,21},{6,22},{7,23},{8,24},{9,... | collective-permute-start | bytes 98312 | tf_op jit(solution)/shard_map/ppermute | solution.py:503
  81.5 3.1 %collective-permute-start.22 = (f32[2,64,128]{2,1,0:T(8,128)S(1)}, f32[2,64,128]{2,1,0:T(8,128)S(1)}, u32[]{:S(2)}, u32[]{:S(2)}) collective-permute-start(f32[2,64,128]{2,1,0:T(8,128)S(1)} %open.3.pair_ref), channel_id=1, source_target_pairs={{16,1},{17,2},{18,3},{19,4},{20,5},{21,6},{22,7},{23,8},{24,9},{25... | collective-permute-start | bytes 196616 | tf_op jit(solution)/shard_map/ppermute | solution.py:502
  85.5 5.6 %collective-permute-start.24 = (f32[2,64,128]{2,1,0:T(8,128)S(1)}, f32[2,64,128]{2,1,0:T(8,128)S(1)}, u32[]{:S(2)}, u32[]{:S(2)}) collective-permute-start(f32[2,64,128]{2,1,0:T(8,128)S(1)} %get-tuple-element.132.pair_ref), channel_id=1, source_target_pairs={{1,16},{2,17},{3,18},{4,19},{5,20},{6,21},{7,22},{8,23},{9,24},{10... | collective-permute-start | bytes 196616 | tf_op jit(solution)/shard_map/ppermute | solution.py:502
  86.8 5.8 %collective-permute-start.23 = (f32[2,64,128]{2,1,0:T(8,128)S(1)}, f32[2,64,128]{2,1,0:T(8,128)S(1)}, u32[]{:S(2)}, u32[]{:S(2)}) collective-permute-start(f32[2,64,128]{2,1,0:T(8,128)S(1)} %get-tuple-element.132.pair_ref), channel_id=1, source_target_pairs={{0,16},{1,17},{2,18},{3,19},{4,20},{5,21},{6,22},{7,23},{8,24},{9,... | collective-permute-start | bytes 196616 | tf_op jit(solution)/shard_map/ppermute | solution.py:503
  96.9 5.6 %collective-permute-start.28 = (f32[2,64,128]{2,1,0:T(8,128)S(1)}, f32[2,64,128]{2,1,0:T(8,128)S(1)}, u32[]{:S(2)}, u32[]{:S(2)}) collective-permute-start(f32[2,64,128]{2,1,0:T(8,128)S(1)} %get-tuple-element.140.pair_ref), channel_id=1, source_target_pairs={{1,16},{2,17},{3,18},{4,19},{5,20},{6,21},{7,22},{8,23},{9,24},{10... | collective-permute-start | bytes 196616 | tf_op jit(solution)/shard_map/ppermute | solution.py:502
  98.2 5.5 %collective-permute-start.27 = (f32[2,64,128]{2,1,0:T(8,128)S(1)}, f32[2,64,128]{2,1,0:T(8,128)S(1)}, u32[]{:S(2)}, u32[]{:S(2)}) collective-permute-start(f32[2,64,128]{2,1,0:T(8,128)S(1)} %get-tuple-element.140.pair_ref), channel_id=1, source_target_pairs={{0,16},{1,17},{2,18},{3,19},{4,20},{5,21},{6,22},{7,23},{8,24},{9,... | collective-permute-start | bytes 196616 | tf_op jit(solution)/shard_map/ppermute | solution.py:503
  108.0 5.6 %collective-permute-start.32 = (f32[2,64,128]{2,1,0:T(8,128)S(1)}, f32[2,64,128]{2,1,0:T(8,128)S(1)}, u32[]{:S(2)}, u32[]{:S(2)}) collective-permute-start(f32[2,64,128]{2,1,0:T(8,128)S(1)} %get-tuple-element.148.pair_ref), channel_id=1, source_target_pairs={{1,16},{2,17},{3,18},{4,19},{5,20},{6,21},{7,22},{8,23},{9,24},{10... | collective-permute-start | bytes 196616 | tf_op jit(solution)/shard_map/ppermute | solution.py:502
  109.3 5.5 %collective-permute-start.31 = (f32[2,64,128]{2,1,0:T(8,128)S(1)}, f32[2,64,128]{2,1,0:T(8,128)S(1)}, u32[]{:S(2)}, u32[]{:S(2)}) collective-permute-start(f32[2,64,128]{2,1,0:T(8,128)S(1)} %get-tuple-element.148.pair_ref), channel_id=1, source_target_pairs={{0,16},{1,17},{2,18},{3,19},{4,20},{5,21},{6,22},{7,23},{8,24},{9,... | collective-permute-start | bytes 196616 | tf_op jit(solution)/shard_map/ppermute | solution.py:503
  119.2 5.2 %collective-permute-start.36 = (f32[64,128]{1,0:T(8,128)S(1)}, f32[64,128]{1,0:T(8,128)S(1)}, u32[]{:S(2)}, u32[]{:S(2)}) collective-permute-start(f32[64,128]{1,0:T(8,128)S(1)} %last.3.field_ref), channel_id=1, source_target_pairs={{1,16},{2,17},{3,18},{4,19},{5,20},{6,21},{7,22},{8,23},{9,24},{10... | collective-permute-start | bytes 98312 | tf_op jit(solution)/shard_map/ppermute | solution.py:502
  120.5 5.5 %collective-permute-start.35 = (f32[64,128]{1,0:T(8,128)S(1)}, f32[64,128]{1,0:T(8,128)S(1)}, u32[]{:S(2)}, u32[]{:S(2)}) collective-permute-start(f32[64,128]{1,0:T(8,128)S(1)} %last.3.field_ref), channel_id=1, source_target_pairs={{0,16},{1,17},{2,18},{3,19},{4,20},{5,21},{6,22},{7,23},{8,24},{9,... | collective-permute-start | bytes 98312 | tf_op jit(solution)/shard_map/ppermute | solution.py:503
  137.7 4.2 %collective-permute-start.37 = (f32[64,128]{1,0:T(8,128)S(1)}, f32[64,128]{1,0:T(8,128)S(1)}, u32[]{:S(2)}, u32[]{:S(2)}) collective-permute-start(f32[64,128]{1,0:T(8,128)S(1)} %get-tuple-element.160), channel_id=1, source_target_pairs={{0,16},{16,0},{1,17},{17,1},{2,18},{18,2},{3,19},{19,3},{4,20},{20... | collective-permute-start | bytes 98312 | tf_op jit(solution)/shard_map/ppermute | solution.py:495
  (14 other events, 34.2 us)
